TPU v7x, 512 devices: a whole 4x8x8 slice. The times are simulated.
512 devices in a mesh: ctx: 256 (over z_lo, y, x, core), head: 2 (over z_hi).
Axes of the slice: x: 4, y: 8, z: 8 (z_hi: 2, z_lo: 4; z = z_hi * 4 + z_lo), core: 2. Of those that a mesh axis runs over, the one named last changes fastest.
Arguments:
- queries: bfloat16 [131072, 8, 128], P('ctx', 'head'), may hold values from -6 to 6
- keys: bfloat16 [131072, 128], P('ctx'), may hold values from -6 to 6
- values: bfloat16 [131072, 128], P('ctx'), may hold values from -6 to 6
- outputs: bfloat16 [131072, 8, 128], P('ctx', 'head'), may hold values from -4 to 4
- grad_out: bfloat16 [131072, 8, 128], P('ctx', 'head'), may hold values from -6 to 6
- lse: float32 [8, 131072], P('head', 'ctx'), may hold values from 4 to 6
- span_order: int32 [512], replicated, may hold values from 0 to 511, each once
Outputs:
- grad_queries: bfloat16 [131072, 8, 128], P('ctx', 'head')
- grad_keys: bfloat16 [131072, 128], P(('ctx', 'head'))
- grad_values: bfloat16 [131072, 128], P(('ctx', 'head'))
Inputs may be any that keep to these rules, and one draw needn't show every extreme that they name: `span_order`: each number once; slots 2 d and 2 d + 1 are the two spans of 256 rows of index d of ctx.
All inputs are finite; a program needn't handle non-finite values.
Results may differ from a plain program's by a relative error of at most 0.0059.
Values may be sent and summed in bfloat16 or wider, within the bound.
No kernel may reach another device: no remote copies, remote signals or barrier semaphores. Data moves between devices by JAX's collectives and lax.ppermute only.
A program may use at most 64 MiB of HBM per device.

v0:
```python
import jax
import jax.numpy as jnp
from jax import lax
from jax.sharding import PartitionSpec as P


def shifted(value, axis, steps):
    count = lax.axis_size(axis)
    pairs = [(source, (source + steps) % count) for source in range(count)]
    return lax.ppermute(value, axis, pairs)


def slot_positions(span_order, device, tok_rows):
    half_rows = tok_rows // 2
    span_ids = lax.dynamic_slice_in_dim(span_order, device * 2, 2)
    within = jnp.arange(tok_rows, dtype=jnp.int32)
    first = within < half_rows
    placed = jnp.where(first, span_ids[0], span_ids[1]) * half_rows + jnp.where(
        first, within, within - half_rows
    )
    return (placed, span_ids)


def tile_terms(query, grad_rows, lse_rows, delta_rows, query_pos, key, value, key_pos):
    scale = query.shape[-1] ** (-0.5)
    scores = jnp.einsum("rgh,kh->grk", query, key, preferred_element_type=jnp.float32) * scale
    allowed = key_pos[None, None, :] <= query_pos[None, :, None]
    probs = jnp.where(allowed, jnp.exp(scores - lse_rows[:, :, None]), jnp.float32(0.0))
    dprobs = jnp.einsum("rgh,kh->grk", grad_rows, value, preferred_element_type=jnp.float32)
    dscores = (probs * (dprobs - delta_rows[:, :, None])).astype(jnp.bfloat16)
    probs_low = probs.astype(jnp.bfloat16)
    grad_value = jnp.einsum("grk,rgh->kh", probs_low, grad_rows, preferred_element_type=jnp.float32)
    grad_key = jnp.einsum("grk,rgh->kh", dscores, query, preferred_element_type=jnp.float32) * scale
    grad_query = jnp.einsum("grk,kh->rgh", dscores, key, preferred_element_type=jnp.float32) * scale
    return (grad_query, grad_key, grad_value)


def block_terms(query, grad_rows, lse_rows, delta_rows, query_pos, key, value, key_pos):
    return tile_terms(query, grad_rows, lse_rows, delta_rows, query_pos, key, value, key_pos)


def local(queries, keys, values, outputs, grad_out, lse, span_order):
    tok_rows = queries.shape[0]
    cycle_size = lax.axis_size("ctx")
    own_index = lax.axis_index("ctx")
    delta = jnp.einsum("rgh,rgh->gr", grad_out, outputs, preferred_element_type=jnp.float32)
    own_pos, own_ids = slot_positions(span_order, own_index, tok_rows)

    def terms_for(key, value, distance):
        source = (own_index + distance) % cycle_size
        key_pos, key_ids = slot_positions(span_order, source, tok_rows)
        return block_terms(queries, grad_out, lse, delta, own_pos, key, value, key_pos)

    grad_query, grad_key, grad_value = terms_for(keys, values, 0)
    for distance in (1, -1, 2, -2):
        far_key, far_value = shifted((keys, values), "ctx", -distance)
        part_q, part_k, part_v = terms_for(far_key, far_value, distance)
        grad_query = grad_query + part_q
        back_k, back_v = shifted((part_k, part_v), "ctx", distance)
        grad_key = grad_key + back_k
        grad_value = grad_value + back_v
    summed_k, summed_v = (
        lax.psum_scatter(grad_key, "head", scatter_dimension=0, tiled=True),
        lax.psum_scatter(grad_value, "head", scatter_dimension=0, tiled=True),
    )
    return (
        grad_query.astype(jnp.bfloat16),
        summed_k.astype(jnp.bfloat16),
        summed_v.astype(jnp.bfloat16),
    )


def solution(mesh):
    return jax.shard_map(
        local,
        mesh=mesh,
        in_specs=(
            P("ctx", "head", None),
            P("ctx", None),
            P("ctx", None),
            P("ctx", "head", None),
            P("ctx", "head", None),
            P("head", "ctx"),
            P(),
        ),
        out_specs=(P("ctx", "head", None), P(("ctx", "head"), None), P(("ctx", "head"), None)),
        check_vma=False,
    )
```

profile of v0, /device:TPU:1, one launch (start us, length us, event | category | flops | bytes accessed | tf_op | source)
XLA Modules:
  0.0 193.8 jit_solution(8924741335548331653)
XLA Ops:
  7.2 0.0 reduce-scatter.3.cloned.1.call-start
  7.3 4.6 %collective-permute-start.3 = (bf16[512,128]{1,0:T(8,128)(2,1)}, bf16[512,128]{1,0:T(8,128)(2,1)S(1)}, u32[]{:S(2)}, u32[]{:S(2)}) collective-permute-start(bf16[512,128]{1,0:T(8,128)(2,1)} %param.9), channel_id=1, source_target_pairs={{0,2},{2,4},{4,6},{6,8},{8,10},{10,12},{12,14},{14,16},{16,18},{18... | collective-permute-start | bytes 393224 | tf_op jit(solution)/shard_map/ppermute | solution.py:10
  11.9 6.2 %collective-permute-start.1 = (bf16[512,128]{1,0:T(8,128)(2,1)}, bf16[512,128]{1,0:T(8,128)(2,1)S(1)}, u32[]{:S(2)}, u32[]{:S(2)}) collective-permute-start(bf16[512,128]{1,0:T(8,128)(2,1)} %param.9), channel_id=1, source_target_pairs={{0,510},{2,0},{4,2},{6,4},{8,6},{10,8},{12,10},{14,12},{16,14},{18... | collective-permute-start | bytes 393224 | tf_op jit(solution)/shard_map/ppermute | solution.py:10
  18.1 1.9 collective-permute-start.7
  20.0 9.4 %collective-permute-start.5 = (bf16[512,128]{1,0:T(8,128)(2,1)}, bf16[512,128]{1,0:T(8,128)(2,1)S(1)}, u32[]{:S(2)}, u32[]{:S(2)}) collective-permute-start(bf16[512,128]{1,0:T(8,128)(2,1)} %param.9), channel_id=1, source_target_pairs={{0,508},{2,510},{4,0},{6,2},{8,4},{10,6},{12,8},{14,10},{16,12},{1... | collective-permute-start | bytes 393224 | tf_op jit(solution)/shard_map/ppermute | solution.py:10
  29.4 3.3 %collective-permute-start.4 = (bf16[512,128]{1,0:T(8,128)(2,1)}, bf16[512,128]{1,0:T(8,128)(2,1)S(1)}, u32[]{:S(2)}, u32[]{:S(2)}) collective-permute-start(bf16[512,128]{1,0:T(8,128)(2,1)} %param.8), channel_id=1, source_target_pairs={{0,508},{2,510},{4,0},{6,2},{8,4},{10,6},{12,8},{14,10},{16,12},{1... | collective-permute-start | bytes 393224 | tf_op jit(solution)/shard_map/ppermute | solution.py:10
  32.8 1.8 fusion.81
  34.6 0.1 copy.42
  34.8 3.6 %fusion.103 = f32[512,512,4]{1,0,2:T(8,128)} fusion(bf16[512,128]{1,0:T(8,128)(2,1)} %param.8, bf16[512,4,128]{2,1,0:T(4,128)(2,1)S(1)} %copy-done), kind=kOutput, calls=%fused_computation.103 | convolution fusion | flops 268435456 | bytes 4849664 | tf_op jit(solution)/shard_map/rgh,kh->grk/dot_general | solution.py:26
  38.3 0.1 fusion.136
  38.4 0.6 fusion.137
  39.0 1.3 multiply_add_fusion.2
  40.3 1.3 multiply_add_fusion.3
  41.7 0.6 fusion.141
  42.2 1.3 multiply_add_fusion
  43.6 1.3 multiply_add_fusion.4
  44.9 0.6 fusion.139
  45.5 1.3 fusion.105
  46.8 1.3 multiply_add_fusion.1
  48.1 0.9 broadcast_compare_fusion.2
  49.0 0.7 copy-done.7
  49.7 3.7 %fusion.17 = bf16[4,512,512]{1,2,0:T(8,128)(2,1)S(1)} fusion(f32[512,512,4]{1,0,2:T(8,128)} %fusion.103, f32[4,512]{1,0:T(4,128)S(1)} %copy.42, f32[4,512]{1,0:T(4,128)S(1)} %copy-done.10, pred[512,512]{0,1:T(8,128)(4,1)S(1)} %get-tuple-element.10, bf16[512,128]{1,0:T(8,128)(2,1)S(1)} %copy-done.9, bf16[512,4,128]{2,1,0:T(4,128)(2,1)S(1)} %copy-done.6), kind=kOutput, calls=%fused_computation.26 | convolution fusion | flops 274726912 | bytes 7225344 | tf_op jit(solution)/shard_map/rgh,kh->grk/dot_general | solution.py:29
  53.4 0.7 fusion.101
  54.2 2.0 %collective-permute-start.6 = (bf16[512,128]{1,0:T(8,128)(2,1)S(1)}, bf16[512,128]{1,0:T(8,128)(2,1)S(1)}, u32[]{:S(2)}, u32[]{:S(2)}) collective-permute-start(bf16[512,128]{1,0:T(8,128)(2,1)S(1)} %copy-done.5), channel_id=1, source_target_pairs={{0,4},{2,6},{4,8},{6,10},{8,12},{10,14},{12,16},{14,18},{16,20},{1... | collective-permute-start | bytes 393224 | tf_op jit(solution)/shard_map/ppermute | solution.py:10
  56.2 0.7 fusion.90
  57.0 1.7 fusion.54
  58.6 7.3 %collective-permute-done.6 = bf16[512,128]{1,0:T(8,128)(2,1)S(1)} collective-permute-done((bf16[512,128]{1,0:T(8,128)(2,1)S(1)}, bf16[512,128]{1,0:T(8,128)(2,1)S(1)}, u32[]{:S(2)}, u32[]{:S(2)}) %collective-permute-start.6) | collective-permute-done | bytes 131104 | tf_op jit(solution)/shard_map/ppermute | solution.py:10
  65.9 10.0 %collective-permute-start = (bf16[512,128]{1,0:T(8,128)(2,1)S(1)}, bf16[512,128]{1,0:T(8,128)(2,1)S(1)}, u32[]{:S(2)}, u32[]{:S(2)}) collective-permute-start(bf16[512,128]{1,0:T(8,128)(2,1)S(1)} %copy-done.5), channel_id=1, source_target_pairs={{0,510},{2,0},{4,2},{6,4},{8,6},{10,8},{12,10},{14,12},{16,14},{18... | collective-permute-start | bytes 393224 | tf_op jit(solution)/shard_map/ppermute | solution.py:10
  76.0 0.7 fusion.85
  76.7 1.7 fusion.57
  78.3 1.9 collective-permute-start.2
  80.3 1.6 fusion.5
  81.9 0.7 fusion.61
  82.6 1.9 collective-permute-start.10
  84.5 0.7 fusion.94
  85.2 1.7 fusion.51
  86.9 2.1 %collective-permute-start.14 = (f32[512,128]{1,0:T(8,128)}, f32[512,128]{1,0:T(8,128)}, u32[]{:S(2)}, u32[]{:S(2)}) collective-permute-start(f32[512,128]{1,0:T(8,128)} %fusion.54), channel_id=1, source_target_pairs={{0,4},{2,6},{4,8},{6,10},{8,12},{10,14},{12,16},{14,18},{16,20},{1... | collective-permute-start | bytes 786440 | tf_op jit(solution)/shard_map/ppermute | solution.py:10
  89.0 1.6 fusion.1
  90.6 0.7 fusion.60
  91.3 9.4 %collective-permute-start.11 = (f32[512,128]{1,0:T(8,128)S(1)}, f32[512,128]{1,0:T(8,128)S(1)}, u32[]{:S(2)}, u32[]{:S(2)}) collective-permute-start(f32[512,128]{1,0:T(8,128)S(1)} %fusion.60), channel_id=1, source_target_pairs={{0,508},{2,510},{4,0},{6,2},{8,4},{10,6},{12,8},{14,10},{16,12},{1... | collective-permute-start | bytes 786440 | tf_op jit(solution)/shard_map/ppermute | solution.py:10
  100.7 1.6 fusion.9
  102.3 0.7 fusion.62
  103.1 0.7 copy-done.1
  103.7 10.5 %collective-permute-start.9 = (f32[512,128]{1,0:T(8,128)S(1)}, f32[512,128]{1,0:T(8,128)S(1)}, u32[]{:S(2)}, u32[]{:S(2)}) collective-permute-start(f32[512,128]{1,0:T(8,128)S(1)} %fusion.62), channel_id=1, source_target_pairs={{0,510},{2,0},{4,2},{6,4},{8,6},{10,8},{12,10},{14,12},{16,14},{18... | collective-permute-start | bytes 786440 | tf_op jit(solution)/shard_map/ppermute | solution.py:10
  114.2 0.7 fusion.98
  115.0 1.7 fusion.48
  116.6 1.6 fusion.13
  118.2 0.7 fusion.63
  118.9 1.9 collective-permute-start.8
  120.9 0.7 convolution_add_fusion.1
  121.6 9.3 %collective-permute-start.15 = (f32[512,128]{1,0:T(8,128)}, f32[512,128]{1,0:T(8,128)}, u32[]{:S(2)}, u32[]{:S(2)}) collective-permute-start(f32[512,128]{1,0:T(8,128)} %fusion.57), channel_id=1, source_target_pairs={{0,508},{2,510},{4,0},{6,2},{8,4},{10,6},{12,8},{14,10},{16,12},{1... | collective-permute-start | bytes 786440 | tf_op jit(solution)/shard_map/ppermute | solution.py:10
  130.9 1.9 collective-permute-start.13
  132.9 3.6 %collective-permute-start.12 = (f32[512,128]{1,0:T(8,128)}, f32[512,128]{1,0:T(8,128)}, u32[]{:S(2)}, u32[]{:S(2)}) collective-permute-start(f32[512,128]{1,0:T(8,128)} %fusion.48), channel_id=1, source_target_pairs={{0,2},{2,4},{4,6},{6,8},{8,10},{10,12},{12,14},{14,16},{16,18},{18... | collective-permute-start | bytes 786440 | tf_op jit(solution)/shard_map/ppermute | solution.py:10
  136.5 1.4 fusion.68
  138.0 0.3 reduce-scatter.5.cloned.1.call-start
  138.3 2.3 %fusion.88 = f32[4,512,128]{2,1,0:T(8,128)S(1)} fusion(bf16[4,512,512]{1,2,0:T(8,128)(2,1)} %copy-done.4, bf16[512,128]{1,0:T(8,128)(2,1)S(1)} %collective-permute-done.4), kind=kOutput, calls=%fused_computation.88 | convolution fusion | flops 268435456 | bytes 3276800 | tf_op jit(solution)/shard_map/grk,kh->rgh/dot_general | solution.py:34
  140.6 4.2 %fusion.78 = f32[512,128]{1,0:T(8,128)} fusion(f32[512,128]{1,0:T(8,128)} %collective-permute-done.15, f32[512,128]{1,0:T(8,128)} %collective-permute-done.14, f32[512,128]{1,0:T(8,128)} %collective-permute-done.13, f32[512,128]{1,0:T(8,128)} %collective-permute-done.12, f32[512,512,4]{1,0,2:T(8,128)} %fusion.103, f32[4,512]{1,0:T(4,128)S(1)} %copy-done.10, ...), kind=kOutput, calls=%fused_computation.74 | convolution fusion | flops 272891904 | bytes 6299648 | tf_op jit(solution)/shard_map/grk,rgh->kh/dot_general | solution.py:32
  144.9 2.5 %fusion.83 = f32[4,512,128]{2,1,0:T(8,128)S(1)} fusion(bf16[4,512,512]{1,2,0:T(8,128)(2,1)} %copy-done.3, bf16[512,128]{1,0:T(8,128)(2,1)S(1)} %collective-permute-done.6), kind=kOutput, calls=%fused_computation.83 | convolution fusion | flops 268435456 | bytes 3276800 | tf_op jit(solution)/shard_map/grk,kh->rgh/dot_general | solution.py:34
  147.4 0.8 fusion.44
  148.2 1.2 copy.35
  149.4 9.8 %reduce-scatter.3.cloned.1.call-done = f32[256,128]{1,0:T(8,128)} async-done(((f32[512,128]{1,0:T(8,128)}), f32[256,128]{1,0:T(8,128)}) %reduce-scatter.3.cloned.1.call-update) | async-done | bytes 131088 | tf_op jit(solution)/shard_map/reduce_scatter | solution.py:63
  159.2 1.5 convert_element_type.45
  160.8 24.6 %reduce-scatter.5.cloned.1.call-done = f32[256,128]{1,0:T(8,128)} async-done(((f32[512,128]{1,0:T(8,128)}), f32[256,128]{1,0:T(8,128)}) %reduce-scatter.5.cloned.1.call-update) | async-done | bytes 131088 | tf_op jit(solution)/shard_map/reduce_scatter | solution.py:64
  185.4 1.5 convert_element_type.51
  (37 shorter events, 0.1 us)
Async XLA Ops:
  7.2 27.6 %copy-start = (bf16[512,4,128]{2,1,0:T(4,128)(2,1)S(1)}, bf16[512,4,128]{2,1,0:T(4,128)(2,1)}, u32[]{:S(2)}) copy-start(bf16[512,4,128]{2,1,0:T(4,128)(2,1)} %param.7) | copy-start | bytes 1572868
  7.2 42.5 %copy-start.9 = (bf16[512,128]{1,0:T(8,128)(2,1)S(1)}, bf16[512,128]{1,0:T(8,128)(2,1)}, u32[]{:S(2)}) copy-start(bf16[512,128]{1,0:T(8,128)(2,1)} %param.9) | copy-start | bytes 393220
  7.2 42.5 %copy-start.6 = (bf16[512,4,128]{2,1,0:T(4,128)(2,1)S(1)}, bf16[512,4,128]{2,1,0:T(4,128)(2,1)}, u32[]{:S(2)}) copy-start(bf16[512,4,128]{2,1,0:T(4,128)(2,1)} %param.11) | copy-start | bytes 1572868
  7.2 31.1 %copy-start.8 = (s32[512]{0:T(512)S(1)}, s32[512]{0:T(512)}, u32[]{:S(2)}) copy-start(s32[512]{0:T(512)} %param.13) | copy-start | bytes 6148
  7.2 42.5 %copy-start.10 = (f32[4,512]{1,0:T(4,128)S(1)}, f32[4,512]{1,0:T(4,128)}, u32[]{:S(2)}) copy-start(f32[4,512]{1,0:T(4,128)} %param.12) | copy-start | bytes 24580
  7.2 152.0 %reduce-scatter.3.cloned.1.call-start = ((), (), s32[]{:S(2)}) async-start(), calls=%async_computation.2 | async-start | bytes 393216 | tf_op jit(solution)/shard_map/reduce_scatter | solution.py:63
  7.3 84.1 %collective-permute-start.3 = (bf16[512,128]{1,0:T(8,128)(2,1)}, bf16[512,128]{1,0:T(8,128)(2,1)S(1)}, u32[]{:S(2)}, u32[]{:S(2)}) collective-permute-start(bf16[512,128]{1,0:T(8,128)(2,1)} %param.9), channel_id=1, source_target_pairs={{0,2},{2,4},{4,6},{6,8},{8,10},{10,12},{12,14},{14,16},{16,18},{18... | collective-permute-start | bytes 393224 | tf_op jit(solution)/shard_map/ppermute | solution.py:10
  11.9 104.7 %collective-permute-start.1 = (bf16[512,128]{1,0:T(8,128)(2,1)}, bf16[512,128]{1,0:T(8,128)(2,1)S(1)}, u32[]{:S(2)}, u32[]{:S(2)}) collective-permute-start(bf16[512,128]{1,0:T(8,128)(2,1)} %param.9), channel_id=1, source_target_pairs={{0,510},{2,0},{4,2},{6,4},{8,6},{10,8},{12,10},{14,12},{16,14},{18... | collective-permute-start | bytes 393224 | tf_op jit(solution)/shard_map/ppermute | solution.py:10
  18.1 68.8 %collective-permute-start.7 = (bf16[512,128]{1,0:T(8,128)(2,1)}, bf16[512,128]{1,0:T(8,128)(2,1)S(1)}, u32[]{:S(2)}, u32[]{:S(2)}) collective-permute-start(bf16[512,128]{1,0:T(8,128)(2,1)} %param.9), channel_id=1, source_target_pairs={{0,4},{2,6},{4,8},{6,10},{8,12},{10,14},{12,16},{14,18},{16,20},{1... | collective-permute-start | bytes 393224 | tf_op jit(solution)/shard_map/ppermute | solution.py:10
  20.0 58.3 %collective-permute-start.5 = (bf16[512,128]{1,0:T(8,128)(2,1)}, bf16[512,128]{1,0:T(8,128)(2,1)S(1)}, u32[]{:S(2)}, u32[]{:S(2)}) collective-permute-start(bf16[512,128]{1,0:T(8,128)(2,1)} %param.9), channel_id=1, source_target_pairs={{0,508},{2,510},{4,0},{6,2},{8,4},{10,6},{12,8},{14,10},{16,12},{1... | collective-permute-start | bytes 393224 | tf_op jit(solution)/shard_map/ppermute | solution.py:10
  29.4 24.8 %collective-permute-start.4 = (bf16[512,128]{1,0:T(8,128)(2,1)}, bf16[512,128]{1,0:T(8,128)(2,1)S(1)}, u32[]{:S(2)}, u32[]{:S(2)}) collective-permute-start(bf16[512,128]{1,0:T(8,128)(2,1)} %param.8), channel_id=1, source_target_pairs={{0,508},{2,510},{4,0},{6,2},{8,4},{10,6},{12,8},{14,10},{16,12},{1... | collective-permute-start | bytes 393224 | tf_op jit(solution)/shard_map/ppermute | solution.py:10
  49.0 0.7 copy-start.7
  49.7 3.7 %copy-start.5 = (bf16[512,128]{1,0:T(8,128)(2,1)S(1)}, bf16[512,128]{1,0:T(8,128)(2,1)}, u32[]{:S(2)}) copy-start(bf16[512,128]{1,0:T(8,128)(2,1)} %param.8) | copy-start | bytes 393220
  54.2 11.7 %collective-permute-start.6 = (bf16[512,128]{1,0:T(8,128)(2,1)S(1)}, bf16[512,128]{1,0:T(8,128)(2,1)S(1)}, u32[]{:S(2)}, u32[]{:S(2)}) collective-permute-start(bf16[512,128]{1,0:T(8,128)(2,1)S(1)} %copy-done.5), channel_id=1, source_target_pairs={{0,4},{2,6},{4,8},{6,10},{8,12},{10,14},{12,16},{14,18},{16,20},{1... | collective-permute-start | bytes 393224 | tf_op jit(solution)/shard_map/ppermute | solution.py:10
  65.9 37.1 %collective-permute-start = (bf16[512,128]{1,0:T(8,128)(2,1)S(1)}, bf16[512,128]{1,0:T(8,128)(2,1)S(1)}, u32[]{:S(2)}, u32[]{:S(2)}) collective-permute-start(bf16[512,128]{1,0:T(8,128)(2,1)S(1)} %copy-done.5), channel_id=1, source_target_pairs={{0,510},{2,0},{4,2},{6,4},{8,6},{10,8},{12,10},{14,12},{16,14},{18... | collective-permute-start | bytes 393224 | tf_op jit(solution)/shard_map/ppermute | solution.py:10
  78.3 4.2 %collective-permute-start.2 = (bf16[512,128]{1,0:T(8,128)(2,1)S(1)}, bf16[512,128]{1,0:T(8,128)(2,1)S(1)}, u32[]{:S(2)}, u32[]{:S(2)}) collective-permute-start(bf16[512,128]{1,0:T(8,128)(2,1)S(1)} %copy-done.5), channel_id=1, source_target_pairs={{0,2},{2,4},{4,6},{6,8},{8,10},{10,12},{12,14},{14,16},{16,18},{18... | collective-permute-start | bytes 393224 | tf_op jit(solution)/shard_map/ppermute | solution.py:10
  81.9 5.0 %copy-start.4 = (bf16[4,512,512]{1,2,0:T(8,128)(2,1)}, bf16[4,512,512]{1,2,0:T(8,128)(2,1)S(1)}, u32[]{:S(2)}) copy-start(bf16[4,512,512]{1,2,0:T(8,128)(2,1)S(1)} %fusion.5) | copy-start | bytes 6291460
  82.6 39.0 %collective-permute-start.10 = (f32[512,128]{1,0:T(8,128)S(1)}, f32[512,128]{1,0:T(8,128)S(1)}, u32[]{:S(2)}, u32[]{:S(2)}) collective-permute-start(f32[512,128]{1,0:T(8,128)S(1)} %fusion.61), channel_id=1, source_target_pairs={{0,4},{2,6},{4,8},{6,10},{8,12},{10,14},{12,16},{14,18},{16,20},{1... | collective-permute-start | bytes 786440 | tf_op jit(solution)/shard_map/ppermute | solution.py:10
  86.9 53.7 %collective-permute-start.14 = (f32[512,128]{1,0:T(8,128)}, f32[512,128]{1,0:T(8,128)}, u32[]{:S(2)}, u32[]{:S(2)}) collective-permute-start(f32[512,128]{1,0:T(8,128)} %fusion.54), channel_id=1, source_target_pairs={{0,4},{2,6},{4,8},{6,10},{8,12},{10,14},{12,16},{14,18},{16,20},{1... | collective-permute-start | bytes 786440 | tf_op jit(solution)/shard_map/ppermute | solution.py:10
  90.6 11.7 %copy-start.3 = (bf16[4,512,512]{1,2,0:T(8,128)(2,1)}, bf16[4,512,512]{1,2,0:T(8,128)(2,1)S(1)}, u32[]{:S(2)}) copy-start(bf16[4,512,512]{1,2,0:T(8,128)(2,1)S(1)} %fusion.1) | copy-start | bytes 6291460
  91.3 39.6 %collective-permute-start.11 = (f32[512,128]{1,0:T(8,128)S(1)}, f32[512,128]{1,0:T(8,128)S(1)}, u32[]{:S(2)}, u32[]{:S(2)}) collective-permute-start(f32[512,128]{1,0:T(8,128)S(1)} %fusion.60), channel_id=1, source_target_pairs={{0,508},{2,510},{4,0},{6,2},{8,4},{10,6},{12,8},{14,10},{16,12},{1... | collective-permute-start | bytes 786440 | tf_op jit(solution)/shard_map/ppermute | solution.py:10
  102.3 1.4 copy-start.1
  103.7 29.1 %collective-permute-start.9 = (f32[512,128]{1,0:T(8,128)S(1)}, f32[512,128]{1,0:T(8,128)S(1)}, u32[]{:S(2)}, u32[]{:S(2)}) collective-permute-start(f32[512,128]{1,0:T(8,128)S(1)} %fusion.62), channel_id=1, source_target_pairs={{0,510},{2,0},{4,2},{6,4},{8,6},{10,8},{12,10},{14,12},{16,14},{18... | collective-permute-start | bytes 786440 | tf_op jit(solution)/shard_map/ppermute | solution.py:10
  118.9 17.6 %collective-permute-start.8 = (f32[512,128]{1,0:T(8,128)S(1)}, f32[512,128]{1,0:T(8,128)S(1)}, u32[]{:S(2)}, u32[]{:S(2)}) collective-permute-start(f32[512,128]{1,0:T(8,128)S(1)} %fusion.63), channel_id=1, source_target_pairs={{0,2},{2,4},{4,6},{6,8},{8,10},{10,12},{12,14},{14,16},{16,18},{18... | collective-permute-start | bytes 786440 | tf_op jit(solution)/shard_map/ppermute | solution.py:10
  121.6 19.0 %collective-permute-start.15 = (f32[512,128]{1,0:T(8,128)}, f32[512,128]{1,0:T(8,128)}, u32[]{:S(2)}, u32[]{:S(2)}) collective-permute-start(f32[512,128]{1,0:T(8,128)} %fusion.57), channel_id=1, source_target_pairs={{0,508},{2,510},{4,0},{6,2},{8,4},{10,6},{12,8},{14,10},{16,12},{1... | collective-permute-start | bytes 786440 | tf_op jit(solution)/shard_map/ppermute | solution.py:10
  130.9 9.7 %collective-permute-start.13 = (f32[512,128]{1,0:T(8,128)}, f32[512,128]{1,0:T(8,128)}, u32[]{:S(2)}, u32[]{:S(2)}) collective-permute-start(f32[512,128]{1,0:T(8,128)} %fusion.51), channel_id=1, source_target_pairs={{0,510},{2,0},{4,2},{6,4},{8,6},{10,8},{12,10},{14,12},{16,14},{18... | collective-permute-start | bytes 786440 | tf_op jit(solution)/shard_map/ppermute | solution.py:10
  132.9 7.8 %collective-permute-start.12 = (f32[512,128]{1,0:T(8,128)}, f32[512,128]{1,0:T(8,128)}, u32[]{:S(2)}, u32[]{:S(2)}) collective-permute-start(f32[512,128]{1,0:T(8,128)} %fusion.48), channel_id=1, source_target_pairs={{0,2},{2,4},{4,6},{6,8},{8,10},{10,12},{12,14},{14,16},{16,18},{18... | collective-permute-start | bytes 786440 | tf_op jit(solution)/shard_map/ppermute | solution.py:10
  138.0 47.4 %reduce-scatter.5.cloned.1.call-start = ((), (), s32[]{:S(2)}) async-start(), calls=%async_computation.3 | async-start | bytes 393216 | tf_op jit(solution)/shard_map/reduce_scatter | solution.py:64
  144.9 2.5 %copy-start.2 = (bf16[4,512,512]{1,2,0:T(8,128)(2,1)S(1)}, bf16[4,512,512]{1,2,0:T(8,128)(2,1)}, u32[]{:S(2)}) copy-start(bf16[4,512,512]{1,2,0:T(8,128)(2,1)} %copy-done.1) | copy-start | bytes 6291460
Sparse Core Ops, SparseCore 0:
  138.1 21.0 reduce-scatter.2
  162.2 23.1 reduce-scatter.4
where the time goes:
time: 195 us; the launch traced here: 194 us
  starting transfers between devices  80.3 us (41%)
  waiting for transfers between devices  41.8 us (21%)
  matrix products  38.8 us (20%)
  between operations  14.6 us (7%)
  other arithmetic  13.7 us (7%)
  local copies, waits for them, and re-layouts  4.57 us (2%)
    ppermute x16, starting transfers between devices, shifted(): return lax.ppermute(value, axis, pairs)  80 us
    reduce_scatter x1, waiting for transfers between devices, local(): lax.psum_scatter(grad_value, 'head', scatter_dimension=0, tiled=True)  24.6 us
    dot_general x5, matrix products, tile_terms(): jnp.einsum('grk,rgh->kh', probs_low, grad_rows, preferred_element_type=jn...  10.9 us
    dot_general x5, matrix products, tile_terms(): jnp.einsum('rgh,kh->grk', grad_rows, value, preferred_element_type=jnp.fl...  10.1 us
    reduce_scatter x1, waiting for transfers between devices, local(): lax.psum_scatter(grad_key, 'head', scatter_dimension=0, tiled=True)  9.79 us
    add x6, other arithmetic, slot_positions(): jnp.where(first, span_ids[0], span_ids[1]) * half_rows  7.88 us
    ppermute x16, waiting for transfers between devices, shifted(): return lax.ppermute(value, axis, pairs)  7.37 us
    dot_general x5, matrix products, tile_terms(): jnp.einsum('grk,kh->rgh', dscores, key, preferred_element_type=jnp.float32)  7.15 us
  transfers between devices with their start and end apart: 18, of which 3 were waited for; matrix products, arithmetic and copies ran while one was open for 28% of the time, Pallas kernels for 0%

commit v1 on v0

v1 whole, which is shorter than its diff:
```python
import functools

import jax
import jax.numpy as jnp
from jax import lax
from jax.experimental import pallas as pl
from jax.experimental.pallas import tpu as pltpu
from jax.sharding import PartitionSpec as P

F32 = jnp.float32
BF16 = jnp.bfloat16
LOG2E = 1.4426950408889634
SUB = 512
VMEM = pl.BlockSpec(memory_space=pltpu.VMEM)
SMEM = pl.BlockSpec(memory_space=pltpu.SMEM)


def dot(a, b, ca, cb):
    return lax.dot_general(a, b, (((ca,), (cb,)), ((), ())), preferred_element_type=F32)


def lane_ones(rows, low, high):
    lane = lax.broadcasted_iota(jnp.int32, (rows, 128), 1)
    return jnp.where((lane >= low) & (lane < high), 1.0, 0.0).astype(BF16)


def prep_kernel(grad_ref, out_ref, lse_ref, extra_ref, wide):
    heads, tokens = lse_ref.shape
    depth = grad_ref.shape[1]
    lse = lse_ref[...] * float(depth**0.5)
    turned = jnp.concatenate([lse, jnp.zeros((128 - heads, tokens), F32)], axis=0).T
    for g in range(heads):
        wide[pl.ds(g, tokens, stride=heads), :] = jnp.broadcast_to(
            turned[:, g : g + 1], (tokens, 128)
        )
    delta = jnp.sum(
        grad_ref[...].astype(F32) * out_ref[...].astype(F32), axis=1, keepdims=True
    )
    lane = lax.broadcasted_iota(jnp.int32, wide.shape, 1)
    rest = jnp.where(lane < 3, wide[...], delta)
    high = rest.astype(BF16).astype(F32)
    rest = rest - high
    mid = rest.astype(BF16).astype(F32)
    low = rest - mid
    place = jnp.where(lane < 3, lane, lane - 3)
    term = jnp.where(place == 0, high, jnp.where(place == 1, mid, low))
    extra_ref[...] = jnp.where(lane < 6, -term, 0.0).astype(BF16)


def prep(grad_rows, out_rows, lse):
    rows, depth = grad_rows.shape
    return pl.pallas_call(
        prep_kernel,
        out_shape=jax.ShapeDtypeStruct((rows, 128), BF16),
        in_specs=[VMEM] * 3,
        out_specs=VMEM,
        scratch_shapes=[pltpu.VMEM((rows, 128), F32)],
        compiler_params=pltpu.CompilerParams(vmem_limit_bytes=16 * 2**20),
        cost_estimate=pl.CostEstimate(flops=rows * 1024, bytes_accessed=rows * 768, transcendentals=0),
        name="prep",
    )(grad_rows, out_rows, lse)


def tile(q_ref, do_ref, x_ref, key, value, q_base, rows, mask=None):
    span, depth = key.shape
    exponent = float(depth**-0.5 * LOG2E)
    key_x = jnp.concatenate([key, lane_ones(span, 0, 3)], axis=1)
    value_x = jnp.concatenate([value, lane_ones(span, 3, 6)], axis=1)

    def front(i):
        at = pl.ds(pl.multiple_of(q_base + i * SUB, SUB), SUB)
        q, do, x = q_ref[at, :], do_ref[at, :], x_ref[at, :]
        p = jnp.exp2(dot(jnp.concatenate([q, x], axis=1), key_x, 1, 1) * exponent)
        if mask is not None:
            p = jnp.where(mask(i * SUB, SUB, span), p, 0.0)
        dp = dot(jnp.concatenate([do, x], axis=1), value_x, 1, 1)
        return at, q, do, p.astype(BF16), (p * dp).astype(BF16)

    dk, dv = None, None
    pieces = rows // SUB
    later = front(0)
    terms = []
    for i in range(pieces):
        at, q, do, p, ds = later
        if i + 1 < pieces:
            later = front(i + 1)
        yield_dq = dot(ds, key, 1, 0)
        terms.append((at, yield_dq))
        part_v, part_k = dot(do, p, 0, 0), dot(q, ds, 0, 0)
        dv = part_v if dv is None else dv + part_v
        dk = part_k if dk is None else dk + part_k
    return terms, dk, dv


def far_kernel(distances, first, span_ref, q_ref, do_ref, x_ref, kv_ref, *refs):
    if first:
        dq_ref, g_ref = refs
        dq_ref[...] = jnp.zeros_like(dq_ref)
    else:
        _, dq_ref, g_ref = refs
    count = lax.axis_size("ctx")
    me = lax.axis_index("ctx")
    sign = 1 - 2 * (me % 2)
    depth = q_ref.shape[1]
    tokens = kv_ref.shape[0] // (2 * len(distances))
    span = tokens // 2
    half = q_ref.shape[0] // 2
    q0, q1 = span_ref[2 * me], span_ref[2 * me + 1]

    def step(t, carry):
        chunk, j = t // 2, t % 2
        distance = distances[0] if len(distances) == 1 else jnp.where(chunk == 0, *distances)
        source = (me + sign * distance + count) % count
        k_id = span_ref[2 * source + j]
        at = pl.multiple_of(chunk * 2 * tokens + j * span, span)
        key = lambda: kv_ref[pl.ds(at, span), :]
        value = lambda: kv_ref[pl.ds(at + tokens, span), :]
        k_rows = pl.ds(pl.multiple_of(chunk * 2 * depth, depth), depth)
        v_rows = pl.ds(pl.multiple_of(chunk * 2 * depth + depth, depth), depth)
        lanes = pl.ds(pl.multiple_of(j * span, span), span)
        a0, a1 = k_id < q0, k_id < q1

        def run(base, rows):
            terms, dk, dv = tile(q_ref, do_ref, x_ref, key(), value(), base, rows)
            for rows_at, term in terms:
                dq_ref[rows_at, :] += term
            g_ref[k_rows, lanes] = dk.astype(g_ref.dtype)
            g_ref[v_rows, lanes] = dv.astype(g_ref.dtype)

        @pl.when(a0 & a1)
        def _():
            run(0, 2 * half)

        @pl.when(a0 != a1)
        def _():
            run(jnp.where(a1, half, 0), half)

        @pl.when(~(a0 | a1))
        def _():
            g_ref[k_rows, lanes] = jnp.zeros((depth, span), g_ref.dtype)
            g_ref[v_rows, lanes] = jnp.zeros((depth, span), g_ref.dtype)

        return carry

    lax.fori_loop(0, 2 * len(distances), step, 0)


def far(distances, spans, q, do, x, kv, dq, dtype, name):
    rows, depth = q.shape
    chunks = len(distances)
    tokens = kv.shape[0] // (2 * chunks)
    args = [spans, q, do, x, kv] + ([] if dq is None else [dq])
    return pl.pallas_call(
        functools.partial(far_kernel, distances, dq is None),
        out_shape=[
            jax.ShapeDtypeStruct((rows, depth), F32),
            jax.ShapeDtypeStruct((chunks * 2 * depth, tokens), dtype),
        ],
        in_specs=[SMEM] + [VMEM] * (len(args) - 1),
        out_specs=[VMEM, VMEM],
        input_output_aliases={} if dq is None else {5: 0},
        compiler_params=pltpu.CompilerParams(vmem_limit_bytes=24 * 2**20),
        cost_estimate=pl.CostEstimate(
            flops=chunks * 10 * rows * tokens * depth,
            bytes_accessed=chunks * 2**20,
            transcendentals=chunks * rows * tokens,
        ),
        name=name,
    )(*args)


def own_kernel(span_ref, q_ref, do_ref, x_ref, kv_ref, dqin_ref, dq_ref, g_ref, acc):
    me = lax.axis_index("ctx")
    depth = q_ref.shape[1]
    tokens = kv_ref.shape[0] // 2
    span = tokens // 2
    half = q_ref.shape[0] // 2
    heads = half // span
    later_first = span_ref[2 * me] > span_ref[2 * me + 1]

    def causal(base, rows, span):
        token = (base + lax.broadcasted_iota(jnp.int32, (rows, span), 0)) // heads
        return lax.broadcasted_iota(jnp.int32, (rows, span), 1) <= token

    def load(j):
        at = pl.multiple_of(j * span, span)
        return kv_ref[pl.ds(at, span), :], kv_ref[pl.ds(at + tokens, span), :]

    def step(j, carry):
        key, value = load(j)
        terms, dk, dv = tile(q_ref, do_ref, x_ref, key, value, j * half, half, causal)
        for rows_at, term in terms:
            acc[rows_at, :] = dqin_ref[rows_at, :] + term
        lanes = pl.ds(pl.multiple_of(j * span, span), span)
        g_ref[0:depth, lanes] = dk
        g_ref[depth : 2 * depth, lanes] = dv
        return carry

    lax.fori_loop(0, 2, step, 0)
    j = jnp.where(later_first, 1, 0)
    key, value = load(j)
    terms, dk, dv = tile(q_ref, do_ref, x_ref, key, value, (1 - j) * half, half)
    for rows_at, term in terms:
        acc[rows_at, :] += term
    lanes = pl.ds(pl.multiple_of(j * span, span), span)
    g_ref[0:depth, lanes] += dk
    g_ref[depth : 2 * depth, lanes] += dv
    dq_ref[...] = (acc[...] * float(depth**-0.5)).astype(dq_ref.dtype)


def own(spans, q, do, x, kv, dq):
    rows, depth = q.shape
    tokens = kv.shape[0] // 2
    return pl.pallas_call(
        own_kernel,
        out_shape=[
            jax.ShapeDtypeStruct((rows, depth), BF16),
            jax.ShapeDtypeStruct((2 * depth, tokens), F32),
        ],
        in_specs=[SMEM] + [VMEM] * 5,
        out_specs=[VMEM, VMEM],
        scratch_shapes=[pltpu.VMEM((rows, depth), F32)],
        compiler_params=pltpu.CompilerParams(vmem_limit_bytes=24 * 2**20),
        cost_estimate=pl.CostEstimate(
            flops=10 * rows * tokens * depth,
            bytes_accessed=2**20,
            transcendentals=rows * tokens,
        ),
        name="own",
    )(spans, q, do, x, kv, dq)


def add_kernel(a_ref, b_ref, o_ref):
    rows = o_ref.shape[0]
    o_ref[...] = (a_ref[...] + b_ref[pl.ds(rows, rows), :].astype(F32)).astype(BF16)


def add(a, b):
    return pl.pallas_call(
        add_kernel,
        out_shape=jax.ShapeDtypeStruct(a.shape, BF16),
        in_specs=[VMEM, VMEM],
        out_specs=VMEM,
        compiler_params=pltpu.CompilerParams(vmem_limit_bytes=8 * 2**20),
        name="add",
    )(a, b)


def merge_kernel(own_ref, a_ref, b_ref, c_ref, keep_ref, send_ref):
    rows, tokens = own_ref.shape
    half = tokens // 2
    head = lax.axis_index("head")

    def part(index):
        lanes = pl.ds(pl.multiple_of(index * half, half), half)
        return (
            own_ref[:, lanes]
            + a_ref[:, lanes].astype(F32)
            + b_ref[:, lanes].astype(F32)
            + c_ref[0:rows, lanes].astype(F32)
        )

    send_ref[...] = part(1 - head).astype(BF16)
    keep_ref[...] = part(head)


def merge(g, a, b, c):
    rows, tokens = g.shape
    return pl.pallas_call(
        merge_kernel,
        out_shape=[
            jax.ShapeDtypeStruct((rows, tokens // 2), F32),
            jax.ShapeDtypeStruct((rows, tokens // 2), BF16),
        ],
        in_specs=[VMEM] * 4,
        out_specs=[VMEM, VMEM],
        compiler_params=pltpu.CompilerParams(vmem_limit_bytes=8 * 2**20),
        name="merge",
    )(g, a, b, c)


def last_kernel(keep_ref, got_ref, dk_ref, dv_ref):
    total = keep_ref[...] + got_ref[...].astype(F32)
    depth = total.shape[0] // 2
    dk_ref[...] = (total[:depth].T * float(depth**-0.5)).astype(BF16)
    dv_ref[...] = total[depth:].T.astype(BF16)


def last(keep, got):
    rows, tokens = keep.shape
    shape = jax.ShapeDtypeStruct((tokens, rows // 2), BF16)
    return pl.pallas_call(
        last_kernel,
        out_shape=[shape, shape],
        in_specs=[VMEM, VMEM],
        out_specs=[VMEM, VMEM],
        compiler_params=pltpu.CompilerParams(vmem_limit_bytes=8 * 2**20),
        name="last",
    )(keep, got)


def local(queries, keys, values, outputs, grad_out, lse, span_order):
    tokens, heads, depth = queries.shape
    count = lax.axis_size("ctx")
    q = queries.reshape(tokens * heads, depth)
    do = grad_out.reshape(tokens * heads, depth)
    out = outputs.reshape(tokens * heads, depth)
    even, odd = range(0, count, 2), range(1, count, 2)
    over_two = [(d, (d + 2) % count) for d in even] + [(d, (d - 2) % count) for d in odd]
    back_two = [(b, a) for a, b in over_two]
    over_one = [(d, (d - 1) % count) for d in even] + [(d, (d + 1) % count) for d in odd]
    mates = [(d, d ^ 1) for d in range(count)]

    kv = jnp.concatenate([keys, values], axis=0)
    kv_b = lax.ppermute(kv, "ctx", over_one)
    kv_a = lax.ppermute(kv, "ctx", over_two)
    x = prep(do, out, lse)
    kv_cd = lax.ppermute(jnp.concatenate([kv, kv_b], axis=0), "ctx", mates)

    dq, g_a = far((-2,), span_order, q, do, x, kv_a, None, BF16, "far_a")
    got_a = lax.ppermute(g_a, "ctx", back_two)
    dq, g_cd = far((1, 2), span_order, q, do, x, kv_cd, dq, BF16, "far_cd")
    got_cd = lax.ppermute(g_cd, "ctx", mates)
    dq, g_b = far((-1,), span_order, q, do, x, kv_b, dq, F32, "far_b")
    got_b = lax.ppermute(add(g_b, got_cd), "ctx", over_one)
    dq, g_own = own(span_order, q, do, x, kv, dq)
    keep, send = merge(g_own, got_a, got_b, got_cd)
    got = lax.ppermute(send, "head", [(0, 1), (1, 0)])
    grad_k, grad_v = last(keep, got)
    return dq.reshape(tokens, heads, depth), grad_k, grad_v


def solution(mesh):
    return jax.shard_map(
        local,
        mesh=mesh,
        in_specs=(
            P("ctx", "head", None),
            P("ctx", None),
            P("ctx", None),
            P("ctx", "head", None),
            P("ctx", "head", None),
            P("head", "ctx"),
            P(),
        ),
        out_specs=(P("ctx", "head", None), P(("ctx", "head"), None), P(("ctx", "head"), None)),
        check_vma=False,
    )
```

time: 195 us -> 76.4 us (0.39)
  the two profiles are of different devices: /device:TPU:1 before, /device:TPU:256 now
where the time goes in v1:
time: 76.4 us; the launch traced here: 76 us
  waiting for transfers between devices  31 us (41%)
  starting transfers between devices  27.9 us (37%)
  Pallas kernels  15.2 us (20%)
  local copies, waits for them, and re-layouts  1.01 us (1%)
  between operations  0.84 us (1%)
    ppermute x1, waiting for transfers between devices, local(): kv_a = lax.ppermute(kv, 'ctx', over_two)  11.5 us
    ppermute x1, starting transfers between devices, local(): kv_b = lax.ppermute(kv, 'ctx', over_one)  9.87 us
    pallas_call x3, Pallas kernels, far(): pl.pallas_call(functools.partial(far_kernel, distances, dq is None), out_...  9.25 us
    ppermute x1, waiting for transfers between devices, local(): got = lax.ppermute(send, 'head', [(0, 1), (1, 0)])  8.73 us
    ppermute x1, starting transfers between devices, local(): got_a = lax.ppermute(g_a, 'ctx', back_two)  7.4 us
    ppermute x1, waiting for transfers between devices, local(): got_b = lax.ppermute(add(g_b, got_cd), 'ctx', over_one)  6.72 us
    pallas_call x1, Pallas kernels, own(): pl.pallas_call(own_kernel, out_shape=[jax.ShapeDtypeStruct((rows, depth),...  4.1 us
    ppermute x1, waiting for transfers between devices, local(): kv_b = lax.ppermute(kv, 'ctx', over_one)  4.04 us
  transfers between devices with their start and end apart: 7, of which 4 were waited for; matrix products, arithmetic and copies ran while one was open for 0% of the time, Pallas kernels for 13%

profile of v1, /device:TPU:256, one launch (start us, length us, event | category | flops | bytes accessed | tf_op | source)
XLA Modules:
  0.0 76.0 jit_solution(3556576552107186363)
XLA Ops:
  0.6 0.0 copy-start.6
  0.6 1.0 %constant_dynamic-update-slice_fusion.1 = bf16[1024,128]{1,0:T(8,128)(2,1)S(1)} fusion(bf16[512,128]{1,0:T(8,128)(2,1)} %param.8), kind=kLoop, calls=%fused_computation.2 | loop fusion | bytes 262144
  1.6 0.0 copy-done.6
  1.6 0.0 copy-start.5
  1.6 0.0 copy-start.2
  1.7 0.0 copy-start
  1.7 0.0 copy-start.1
  1.7 9.9 %collective-permute-start = (bf16[1024,128]{1,0:T(8,128)(2,1)S(1)}, bf16[1024,128]{1,0:T(8,128)(2,1)S(1)}, u32[]{:S(2)}, u32[]{:S(2)}) collective-permute-start(bf16[1024,128]{1,0:T(8,128)(2,1)S(1)} %constant_dynamic-update-slice_fusion.kv_ref), channel_id=1, source_target_pairs={{0,510},{4,2},{8,6},{12,10},{16,14},{20,18},{24,22},{28,26},{32,30... | collective-permute-start | bytes 786440 | tf_op jit(solution)/shard_map/ppermute | solution.py:315
  11.6 4.0 %collective-permute-done.kv_ref = bf16[1024,128]{1,0:T(8,128)(2,1)S(1)} collective-permute-done((bf16[1024,128]{1,0:T(8,128)(2,1)S(1)}, bf16[1024,128]{1,0:T(8,128)(2,1)S(1)}, u32[]{:S(2)}, u32[]{:S(2)}) %collective-permute-start) | collective-permute-done | bytes 262176 | tf_op jit(solution)/shard_map/ppermute | solution.py:315
  15.6 0.0 copy-done.5
  15.6 1.9 %collective-permute-start.1 = (bf16[2048,128]{1,0:T(8,128)(2,1)S(1)}, bf16[2048,128]{1,0:T(8,128)(2,1)S(1)}, u32[]{:S(2)}, u32[]{:S(2)}) collective-permute-start(bf16[2048,128]{1,0:T(8,128)(2,1)S(1)} %pad_maximum_fusion), channel_id=1, source_target_pairs={{0,2},{2,0},{4,6},{6,4},{8,10},{10,8},{12,14},{14,12},{16,18},{18,... | collective-permute-start | bytes 1572872 | tf_op jit(solution)/shard_map/ppermute | solution.py:318
  17.6 1.9 %collective-permute-start.2 = (bf16[1024,128]{1,0:T(8,128)(2,1)S(1)}, bf16[1024,128]{1,0:T(8,128)(2,1)S(1)}, u32[]{:S(2)}, u32[]{:S(2)}) collective-permute-start(bf16[1024,128]{1,0:T(8,128)(2,1)S(1)} %constant_dynamic-update-slice_fusion.kv_ref), channel_id=1, source_target_pairs={{0,4},{4,8},{8,12},{12,16},{16,20},{20,24},{24,28},{28,32},{32,36}... | collective-permute-start | bytes 786440 | tf_op jit(solution)/shard_map/ppermute | solution.py:316
  19.5 0.0 copy-done.2
  19.5 0.0 copy-done
  19.5 0.0 copy-done.1
  19.5 0.0 copy-start.3
  19.5 0.0 copy-start.4
  19.6 0.9 %prep.1.x_ref = bf16[2048,128]{1,0:T(8,128)(2,1)S(1)} custom-call(bf16[2048,128]{1,0:T(8,128)(2,1)S(1)} %bitcast.5, bf16[2048,128]{1,0:T(8,128)(2,1)S(1)} %bitcast.4, f32[4,512]{1,0:T(4,128)S(1)} %copy-done.2), custom_call_target="tpu_custom_call" | custom-call | flops 2097152 | bytes 1572864 | tf_op jit(solution)/shard_map/prep/pallas_call | solution.py:52
  20.5 11.5 %collective-permute-done.2.kv_ref = bf16[1024,128]{1,0:T(8,128)(2,1)S(1)} collective-permute-done((bf16[1024,128]{1,0:T(8,128)(2,1)S(1)}, bf16[1024,128]{1,0:T(8,128)(2,1)S(1)}, u32[]{:S(2)}, u32[]{:S(2)}) %collective-permute-start.2) | collective-permute-done | bytes 262176 | tf_op jit(solution)/shard_map/ppermute | solution.py:316
  32.0 0.0 copy-done.3
  32.0 0.0 copy-done.4
  32.0 2.1 %far_a.1 = (f32[2048,128]{1,0:T(8,128)S(1)}, bf16[256,512]{1,0:T(8,128)(2,1)S(1)}) custom-call(s32[512]{0:T(512)S(1)} %copy-done.4, bf16[2048,128]{1,0:T(8,128)(2,1)S(1)} %bitcast.10, bf16[2048,128]{1,0:T(8,128)(2,1)S(1)} %bitcast.6, bf16[2048,128]{1,0:T(8,128)(2,1)S(1)} %prep.1.x_ref, bf16[1024,128]{1,0:T(8,128)(2,1)S(1)} %collective-permute-done.2.kv_ref), custom_call_target="tpu_custom_call" | custom-call | flops 1342177280 | bytes 1048576 | tf_op jit(solution)/shard_map/far_a/pallas_call | solution.py:153
  34.1 0.0 collective-permute-done.1.kv_ref
  34.1 4.3 %far_cd.1 = (f32[2048,128]{1,0:T(8,128)S(1)}, bf16[512,512]{1,0:T(8,128)(2,1)S(1)}) custom-call(s32[512]{0:T(512)S(1)} %copy-done.4, bf16[2048,128]{1,0:T(8,128)(2,1)S(1)} %bitcast.11, bf16[2048,128]{1,0:T(8,128)(2,1)S(1)} %bitcast.7, bf16[2048,128]{1,0:T(8,128)(2,1)S(1)} %prep.1.x_ref, ...), custom_call_target="tpu_custom_call", output_to_operand_aliasing={{0}: (5, {})} | custom-call | flops 2684354560 | bytes 2097152 | tf_op jit(solution)/shard_map/far_cd/pallas_call | solution.py:153
  38.4 1.9 %collective-permute-start.4 = (bf16[512,512]{1,0:T(8,128)(2,1)S(1)}, bf16[512,512]{1,0:T(8,128)(2,1)S(1)}, u32[]{:S(2)}, u32[]{:S(2)}) collective-permute-start(bf16[512,512]{1,0:T(8,128)(2,1)S(1)} %get-tuple-element.22), channel_id=1, source_target_pairs={{0,2},{2,0},{4,6},{6,4},{8,10},{10,8},{12,14},{14,12},{16,18},{18,... | collective-permute-start | bytes 1572872 | tf_op jit(solution)/shard_map/ppermute | solution.py:323
  40.3 7.4 %collective-permute-start.3 = (bf16[256,512]{1,0:T(8,128)(2,1)S(1)}, bf16[256,512]{1,0:T(8,128)(2,1)S(1)}, u32[]{:S(2)}, u32[]{:S(2)}) collective-permute-start(bf16[256,512]{1,0:T(8,128)(2,1)S(1)} %get-tuple-element.20), channel_id=1, source_target_pairs={{4,0},{8,4},{12,8},{16,12},{20,16},{24,20},{28,24},{32,28},{36,32}... | collective-permute-start | bytes 786440 | tf_op jit(solution)/shard_map/ppermute | solution.py:321
  47.8 2.8 %far_b.1 = (f32[2048,128]{1,0:T(8,128)S(1)}, f32[256,512]{1,0:T(8,128)S(1)}) custom-call(s32[512]{0:T(512)S(1)} %copy-done.4, bf16[2048,128]{1,0:T(8,128)(2,1)S(1)} %bitcast.12, bf16[2048,128]{1,0:T(8,128)(2,1)S(1)} %bitcast.8, bf16[2048,128]{1,0:T(8,128)(2,1)S(1)} %prep.1.x_ref, ...), custom_call_target="tpu_custom_call", output_to_operand_aliasing={{0}: (5, {})} | custom-call | flops 1342177280 | bytes 1048576 | tf_op jit(solution)/shard_map/far_b/pallas_call | solution.py:153
  50.6 0.0 collective-permute-done.4.b_ref.c_ref
  50.6 0.1 add.1
  50.7 2.9 %collective-permute-start.5 = (bf16[256,512]{1,0:T(8,128)(2,1)S(1)}, bf16[256,512]{1,0:T(8,128)(2,1)S(1)}, u32[]{:S(2)}, u32[]{:S(2)}) collective-permute-start(bf16[256,512]{1,0:T(8,128)(2,1)S(1)} %add.1), channel_id=1, source_target_pairs={{0,510},{4,2},{8,6},{12,10},{16,14},{20,18},{24,22},{28,26},{32,30... | collective-permute-start | bytes 786440 | tf_op jit(solution)/shard_map/ppermute | solution.py:325
  53.6 4.1 %own.1 = (bf16[2048,128]{1,0:T(8,128)(2,1)}, f32[256,512]{1,0:T(8,128)S(1)}) custom-call(s32[512]{0:T(512)S(1)} %copy-done.4, bf16[2048,128]{1,0:T(8,128)(2,1)S(1)} %bitcast.13, bf16[2048,128]{1,0:T(8,128)(2,1)S(1)} %bitcast.9, bf16[2048,128]{1,0:T(8,128)(2,1)S(1)} %prep.1.x_ref, bf16[1024,128]{1,0:T(8,128)(2,1)S(1)} %constant_dynamic-update-slice_fusion.kv_ref, ...), custom_call_target="tpu_custom_call" | custom-call | flops 1342177280 | bytes 1048576 | tf_op jit(solution)/shard_map/own/pallas_call | solution.py:214
  57.7 0.0 collective-permute-done.3.a_ref
  57.7 6.7 %collective-permute-done.5.b_ref = bf16[256,512]{1,0:T(8,128)(2,1)S(1)} collective-permute-done((bf16[256,512]{1,0:T(8,128)(2,1)S(1)}, bf16[256,512]{1,0:T(8,128)(2,1)S(1)}, u32[]{:S(2)}, u32[]{:S(2)}) %collective-permute-start.5) | collective-permute-done | bytes 262176 | tf_op jit(solution)/shard_map/ppermute | solution.py:325
  64.4 0.1 merge.1
  64.5 2.0 %collective-permute-start.6 = (bf16[256,256]{1,0:T(8,128)(2,1)S(1)}, bf16[256,256]{1,0:T(8,128)(2,1)S(1)}, u32[]{:S(2)}, u32[]{:S(2)}) collective-permute-start(bf16[256,256]{1,0:T(8,128)(2,1)S(1)} %get-tuple-element.24), channel_id=1, source_target_pairs={{0,1},{1,0},{2,3},{3,2},{4,5},{5,4},{6,7},{7,6},{8,9},{9,8},{10,11... | collective-permute-start | bytes 393224 | tf_op jit(solution)/shard_map/ppermute | solution.py:328
  66.5 8.7 %collective-permute-done.6.got_ref = bf16[256,256]{1,0:T(8,128)(2,1)S(1)} collective-permute-done((bf16[256,256]{1,0:T(8,128)(2,1)S(1)}, bf16[256,256]{1,0:T(8,128)(2,1)S(1)}, u32[]{:S(2)}, u32[]{:S(2)}) %collective-permute-start.6) | collective-permute-done | bytes 131104 | tf_op jit(solution)/shard_map/ppermute | solution.py:328
  75.3 0.8 %last.1 = (bf16[256,128]{1,0:T(8,128)(2,1)}, bf16[256,128]{1,0:T(8,128)(2,1)}) custom-call(f32[256,256]{1,0:T(8,128)S(1)} %get-tuple-element.23.keep_ref, bf16[256,256]{1,0:T(8,128)(2,1)S(1)} %collective-permute-done.6.got_ref), custom_call_target="tpu_custom_call" | custom-call | tf_op jit(solution)/shard_map/last/pallas_call | solution.py:292
  (2 shorter events, 0.1 us)
Async XLA Ops:
  0.6 1.0 %copy-start.6 = (bf16[512,128]{1,0:T(8,128)(2,1)S(1)}, bf16[512,128]{1,0:T(8,128)(2,1)}, u32[]{:S(2)}) copy-start(bf16[512,128]{1,0:T(8,128)(2,1)} %param.9) | copy-start | bytes 393220
  1.6 14.0 %copy-start.5 = (bf16[512,128]{1,0:T(8,128)(2,1)S(1)}, bf16[512,128]{1,0:T(8,128)(2,1)}, u32[]{:S(2)}) copy-start(bf16[512,128]{1,0:T(8,128)(2,1)} %param.8) | copy-start | bytes 393220
  1.6 17.9 %copy-start.2 = (f32[4,512]{1,0:T(4,128)S(1)}, f32[4,512]{1,0:T(4,128)}, u32[]{:S(2)}) copy-start(f32[4,512]{1,0:T(4,128)} %lse_ref.1) | copy-start | bytes 24580
  1.7 17.9 %copy-start = (bf16[512,4,128]{2,1,0:T(4,128)(2,1)S(1)}, bf16[512,4,128]{2,1,0:T(4,128)(2,1)}, u32[]{:S(2)}) copy-start(bf16[512,4,128]{2,1,0:T(4,128)(2,1)} %param.10) | copy-start | bytes 1572868
  1.7 17.9 %copy-start.1 = (bf16[512,4,128]{2,1,0:T(4,128)(2,1)S(1)}, bf16[512,4,128]{2,1,0:T(4,128)(2,1)}, u32[]{:S(2)}) copy-start(bf16[512,4,128]{2,1,0:T(4,128)(2,1)} %param.11) | copy-start | bytes 1572868
  1.7 13.9 %collective-permute-start = (bf16[1024,128]{1,0:T(8,128)(2,1)S(1)}, bf16[1024,128]{1,0:T(8,128)(2,1)S(1)}, u32[]{:S(2)}, u32[]{:S(2)}) collective-permute-start(bf16[1024,128]{1,0:T(8,128)(2,1)S(1)} %constant_dynamic-update-slice_fusion.kv_ref), channel_id=1, source_target_pairs={{0,510},{4,2},{8,6},{12,10},{16,14},{20,18},{24,22},{28,26},{32,30... | collective-permute-start | bytes 786440 | tf_op jit(solution)/shard_map/ppermute | solution.py:315
  15.6 18.4 %collective-permute-start.1 = (bf16[2048,128]{1,0:T(8,128)(2,1)S(1)}, bf16[2048,128]{1,0:T(8,128)(2,1)S(1)}, u32[]{:S(2)}, u32[]{:S(2)}) collective-permute-start(bf16[2048,128]{1,0:T(8,128)(2,1)S(1)} %pad_maximum_fusion), channel_id=1, source_target_pairs={{0,2},{2,0},{4,6},{6,4},{8,10},{10,8},{12,14},{14,12},{16,18},{18,... | collective-permute-start | bytes 1572872 | tf_op jit(solution)/shard_map/ppermute | solution.py:318
  17.6 14.4 %collective-permute-start.2 = (bf16[1024,128]{1,0:T(8,128)(2,1)S(1)}, bf16[1024,128]{1,0:T(8,128)(2,1)S(1)}, u32[]{:S(2)}, u32[]{:S(2)}) collective-permute-start(bf16[1024,128]{1,0:T(8,128)(2,1)S(1)} %constant_dynamic-update-slice_fusion.kv_ref), channel_id=1, source_target_pairs={{0,4},{4,8},{8,12},{12,16},{16,20},{20,24},{24,28},{28,32},{32,36}... | collective-permute-start | bytes 786440 | tf_op jit(solution)/shard_map/ppermute | solution.py:316
  19.5 12.4 %copy-start.3 = (bf16[512,4,128]{2,1,0:T(4,128)(2,1)S(1)}, bf16[512,4,128]{2,1,0:T(4,128)(2,1)}, u32[]{:S(2)}) copy-start(bf16[512,4,128]{2,1,0:T(4,128)(2,1)} %param.7) | copy-start | bytes 1572868
  19.5 12.4 %copy-start.4 = (s32[512]{0:T(512)S(1)}, s32[512]{0:T(512)}, u32[]{:S(2)}) copy-start(s32[512]{0:T(512)} %span_ref.7) | copy-start | bytes 6148
  38.4 12.2 %collective-permute-start.4 = (bf16[512,512]{1,0:T(8,128)(2,1)S(1)}, bf16[512,512]{1,0:T(8,128)(2,1)S(1)}, u32[]{:S(2)}, u32[]{:S(2)}) collective-permute-start(bf16[512,512]{1,0:T(8,128)(2,1)S(1)} %get-tuple-element.22), channel_id=1, source_target_pairs={{0,2},{2,0},{4,6},{6,4},{8,10},{10,8},{12,14},{14,12},{16,18},{18,... | collective-permute-start | bytes 1572872 | tf_op jit(solution)/shard_map/ppermute | solution.py:323
  40.3 17.3 %collective-permute-start.3 = (bf16[256,512]{1,0:T(8,128)(2,1)S(1)}, bf16[256,512]{1,0:T(8,128)(2,1)S(1)}, u32[]{:S(2)}, u32[]{:S(2)}) collective-permute-start(bf16[256,512]{1,0:T(8,128)(2,1)S(1)} %get-tuple-element.20), channel_id=1, source_target_pairs={{4,0},{8,4},{12,8},{16,12},{20,16},{24,20},{28,24},{32,28},{36,32}... | collective-permute-start | bytes 786440 | tf_op jit(solution)/shard_map/ppermute | solution.py:321
  50.7 13.7 %collective-permute-start.5 = (bf16[256,512]{1,0:T(8,128)(2,1)S(1)}, bf16[256,512]{1,0:T(8,128)(2,1)S(1)}, u32[]{:S(2)}, u32[]{:S(2)}) collective-permute-start(bf16[256,512]{1,0:T(8,128)(2,1)S(1)} %add.1), channel_id=1, source_target_pairs={{0,510},{4,2},{8,6},{12,10},{16,14},{20,18},{24,22},{28,26},{32,30... | collective-permute-start | bytes 786440 | tf_op jit(solution)/shard_map/ppermute | solution.py:325
  64.5 10.8 %collective-permute-start.6 = (bf16[256,256]{1,0:T(8,128)(2,1)S(1)}, bf16[256,256]{1,0:T(8,128)(2,1)S(1)}, u32[]{:S(2)}, u32[]{:S(2)}) collective-permute-start(bf16[256,256]{1,0:T(8,128)(2,1)S(1)} %get-tuple-element.24), channel_id=1, source_target_pairs={{0,1},{1,0},{2,3},{3,2},{4,5},{5,4},{6,7},{7,6},{8,9},{9,8},{10,11... | collective-permute-start | bytes 393224 | tf_op jit(solution)/shard_map/ppermute | solution.py:328

commit v2 on v1

--- a/solution.py
+++ b/solution.py
@@ -299,30 +299,58 @@
     )(keep, got)
 
 
+def pack_kernel(a_ref, b_ref, _, o_ref):
+    rows = a_ref.shape[0]
+    o_ref[0:rows, :] = a_ref[...]
+    o_ref[rows : 2 * rows, :] = b_ref[...]
+
+
+def pack(a, b, after):
+    rows, depth = a.shape
+    return pl.pallas_call(
+        pack_kernel,
+        out_shape=jax.ShapeDtypeStruct((2 * rows, depth), a.dtype),
+        in_specs=[VMEM, VMEM, pl.BlockSpec(memory_space=pl.ANY)],
+        out_specs=VMEM,
+        compiler_params=pltpu.CompilerParams(vmem_limit_bytes=8 * 2**20),
+        name="pack",
+    )(a, b, after)
+
+
+def ring(count, move):
+    pairs = []
+    for d in range(count):
+        target = move(d)
+        flip = 0 if 0 <= target < count else 1
+        for h in range(2):
+            pairs.append((2 * d + h, 2 * (target % count) + (h ^ flip)))
+    return pairs
+
+
 def local(queries, keys, values, outputs, grad_out, lse, span_order):
     tokens, heads, depth = queries.shape
     count = lax.axis_size("ctx")
+    both = ("ctx", "head")
     q = queries.reshape(tokens * heads, depth)
     do = grad_out.reshape(tokens * heads, depth)
     out = outputs.reshape(tokens * heads, depth)
-    even, odd = range(0, count, 2), range(1, count, 2)
-    over_two = [(d, (d + 2) % count) for d in even] + [(d, (d - 2) % count) for d in odd]
+    over_two = ring(count, lambda d: d - 2 if d % 2 else d + 2)
     back_two = [(b, a) for a, b in over_two]
-    over_one = [(d, (d - 1) % count) for d in even] + [(d, (d + 1) % count) for d in odd]
+    over_one = ring(count, lambda d: d + 1 if d % 2 else d - 1)
     mates = [(d, d ^ 1) for d in range(count)]
 
     kv = jnp.concatenate([keys, values], axis=0)
-    kv_b = lax.ppermute(kv, "ctx", over_one)
-    kv_a = lax.ppermute(kv, "ctx", over_two)
+    kv_a = lax.ppermute(kv, both, over_two)
+    kv_b = lax.ppermute(kv, both, over_one)
     x = prep(do, out, lse)
-    kv_cd = lax.ppermute(jnp.concatenate([kv, kv_b], axis=0), "ctx", mates)
 
     dq, g_a = far((-2,), span_order, q, do, x, kv_a, None, BF16, "far_a")
-    got_a = lax.ppermute(g_a, "ctx", back_two)
+    kv_cd = lax.ppermute(pack(kv, kv_b, g_a), "ctx", mates)
+    got_a = lax.ppermute(g_a, both, back_two)
+    dq, g_b = far((-1,), span_order, q, do, x, kv_b, dq, F32, "far_b")
     dq, g_cd = far((1, 2), span_order, q, do, x, kv_cd, dq, BF16, "far_cd")
     got_cd = lax.ppermute(g_cd, "ctx", mates)
-    dq, g_b = far((-1,), span_order, q, do, x, kv_b, dq, F32, "far_b")
-    got_b = lax.ppermute(add(g_b, got_cd), "ctx", over_one)
+    got_b = lax.ppermute(add(g_b, got_cd), both, over_one)
     dq, g_own = own(span_order, q, do, x, kv, dq)
     keep, send = merge(g_own, got_a, got_b, got_cd)
     got = lax.ppermute(send, "head", [(0, 1), (1, 0)])

time: 76.4 us -> 68.7 us (0.90)
  the two profiles are of different devices: /device:TPU:256 before, /device:TPU:1 now
where the time goes in v2:
time: 68.7 us; the launch traced here: 68.3 us
  starting transfers between devices  31.8 us (46%)
  Pallas kernels  19.3 us (28%)
  waiting for transfers between devices  12.5 us (18%)
  local copies, waits for them, and re-layouts  3.92 us (6%)
  between operations  0.8 us (1%)
    ppermute x1, starting transfers between devices, local(): kv_a = lax.ppermute(kv, both, over_two)  16.6 us
    pallas_call x3, Pallas kernels, far(): pl.pallas_call(functools.partial(far_kernel, distances, dq is None), out_...  13.3 us
    ppermute x1, waiting for transfers between devices, local(): got = lax.ppermute(send, 'head', [(0, 1), (1, 0)])  8.75 us
    pallas_call x1, Pallas kernels, own(): pl.pallas_call(own_kernel, out_shape=[jax.ShapeDtypeStruct((rows, depth),...  4.1 us
    ppermute x1, starting transfers between devices, local(): got_b = lax.ppermute(add(g_b, got_cd), both, over_one)  4.03 us
    ppermute x1, waiting for transfers between devices, local(): got_a = lax.ppermute(g_a, both, back_two)  3.7 us
    ppermute x1, starting transfers between devices, local(): kv_cd = lax.ppermute(pack(kv, kv_b, g_a), 'ctx', mates)  3.46 us
    unnamed x13, local copies, waits for them, and re-layouts  3 us
  transfers between devices with their start and end apart: 7, of which 2 were waited for; matrix products, arithmetic and copies ran while one was open for 0% of the time, Pallas kernels for 18%

profile of v2, /device:TPU:1, one launch (start us, length us, event | category | flops | bytes accessed | tf_op | source)
XLA Modules:
  0.0 68.3 jit_solution(18069296734470642161)
XLA Ops:
  0.6 0.0 copy-start
  0.6 1.0 %constant_dynamic-update-slice_fusion.1 = bf16[1024,128]{1,0:T(8,128)(2,1)S(1)} fusion(bf16[512,128]{1,0:T(8,128)(2,1)} %param.8), kind=kLoop, calls=%fused_computation.1 | loop fusion | bytes 262144
  1.6 0.9 %constant_dynamic-update-slice_fusion.a_ref.kv_ref = bf16[1024,128]{1,0:T(8,128)(2,1)S(1)} fusion(bf16[1024,128]{1,0:T(8,128)(2,1)S(1)} %constant_dynamic-update-slice_fusion.1, bf16[512,128]{1,0:T(8,128)(2,1)} %param.9), kind=kLoop, calls=%fused_computation | loop fusion | bytes 262144 | tf_op jit(solution)/shard_map/concatenate | solution.py:342
  2.5 16.6 %collective-permute-start.1 = (bf16[1024,128]{1,0:T(8,128)(2,1)S(1)}, bf16[1024,128]{1,0:T(8,128)(2,1)S(1)}, u32[]{:S(2)}, u32[]{:S(2)}) collective-permute-start(bf16[1024,128]{1,0:T(8,128)(2,1)S(1)} %constant_dynamic-update-slice_fusion.a_ref.kv_ref), channel_id=1, source_target_pairs={{0,4},{1,5},{2,511},{3,510},{4,8},{5,9},{6,2},{7,3},{8,12},{9,13},... | collective-permute-start | bytes 786440 | tf_op jit(solution)/shard_map/ppermute | solution.py:343
  19.1 1.9 %collective-permute-start = (bf16[1024,128]{1,0:T(8,128)(2,1)S(1)}, bf16[1024,128]{1,0:T(8,128)(2,1)S(1)}, u32[]{:S(2)}, u32[]{:S(2)}) collective-permute-start(bf16[1024,128]{1,0:T(8,128)(2,1)S(1)} %constant_dynamic-update-slice_fusion.a_ref.kv_ref), channel_id=1, source_target_pairs={{0,511},{1,510},{2,4},{3,5},{4,2},{5,3},{6,8},{7,9},{8,6},{9,7},{1... | collective-permute-start | bytes 786440 | tf_op jit(solution)/shard_map/ppermute | solution.py:344
  21.1 0.0 copy-done
  21.1 0.0 copy-start.1
  21.1 1.0 %copy-done.1 = bf16[512,4,128]{2,1,0:T(4,128)(2,1)S(1)} copy-done((bf16[512,4,128]{2,1,0:T(4,128)(2,1)S(1)}, bf16[512,4,128]{2,1,0:T(4,128)(2,1)}, u32[]{:S(2)}) %copy-start.1) | copy-done | bytes 524312
  22.1 0.0 copy-start.3
  22.1 0.7 %copy-done.3 = f32[4,512]{1,0:T(4,128)S(1)} copy-done((f32[4,512]{1,0:T(4,128)S(1)}, f32[4,512]{1,0:T(4,128)}, u32[]{:S(2)}) %copy-start.3) | copy-done | bytes 8216
  22.8 0.0 copy-start.2
  22.8 0.0 copy-start.4
  22.8 0.0 copy-start.5
  22.8 0.9 %prep.1.x_ref = bf16[2048,128]{1,0:T(8,128)(2,1)S(1)} custom-call(bf16[2048,128]{1,0:T(8,128)(2,1)S(1)} %bitcast.5, bf16[2048,128]{1,0:T(8,128)(2,1)S(1)} %bitcast.4, f32[4,512]{1,0:T(4,128)S(1)} %copy-done.3), custom_call_target="tpu_custom_call" | custom-call | flops 2097152 | bytes 1572864 | tf_op jit(solution)/shard_map/prep/pallas_call | solution.py:52
  23.7 0.0 collective-permute-done.1.kv_ref
  23.7 0.1 copy-done.2
  23.9 0.2 copy-done.4
  24.0 0.0 copy-done.5
  24.0 3.5 %far_a.1 = (f32[2048,128]{1,0:T(8,128)S(1)}, bf16[256,512]{1,0:T(8,128)(2,1)S(1)}) custom-call(s32[512]{0:T(512)S(1)} %copy-done.5, bf16[2048,128]{1,0:T(8,128)(2,1)S(1)} %bitcast.10, bf16[2048,128]{1,0:T(8,128)(2,1)S(1)} %bitcast.6, bf16[2048,128]{1,0:T(8,128)(2,1)S(1)} %prep.1.x_ref, bf16[1024,128]{1,0:T(8,128)(2,1)S(1)} %collective-permute-done.1.kv_ref), custom_call_target="tpu_custom_call" | custom-call | flops 1342177280 | bytes 1048576 | tf_op jit(solution)/shard_map/far_a/pallas_call | solution.py:153
  27.5 0.0 collective-permute-done.b_ref.kv_ref
  27.6 3.5 %collective-permute-start.2 = (bf16[2048,128]{1,0:T(8,128)(2,1)S(1)}, bf16[2048,128]{1,0:T(8,128)(2,1)S(1)}, u32[]{:S(2)}, u32[]{:S(2)}) collective-permute-start(bf16[2048,128]{1,0:T(8,128)(2,1)S(1)} %pack.1), channel_id=1, source_target_pairs={{0,2},{2,0},{4,6},{6,4},{8,10},{10,8},{12,14},{14,12},{16,18},{18,... | collective-permute-start | bytes 1572872 | tf_op jit(solution)/shard_map/ppermute | solution.py:348
  31.1 3.5 %far_b.1 = (f32[2048,128]{1,0:T(8,128)S(1)}, f32[256,512]{1,0:T(8,128)S(1)}) custom-call(s32[512]{0:T(512)S(1)} %copy-done.5, bf16[2048,128]{1,0:T(8,128)(2,1)S(1)} %bitcast.11, bf16[2048,128]{1,0:T(8,128)(2,1)S(1)} %bitcast.7, bf16[2048,128]{1,0:T(8,128)(2,1)S(1)} %prep.1.x_ref, ...), custom_call_target="tpu_custom_call", output_to_operand_aliasing={{0}: (5, {})} | custom-call | flops 1342177280 | bytes 1048576 | tf_op jit(solution)/shard_map/far_b/pallas_call | solution.py:153
  34.5 0.0 collective-permute-done.2.kv_ref
  34.5 6.4 %far_cd.1 = (f32[2048,128]{1,0:T(8,128)S(1)}, bf16[512,512]{1,0:T(8,128)(2,1)S(1)}) custom-call(s32[512]{0:T(512)S(1)} %copy-done.5, bf16[2048,128]{1,0:T(8,128)(2,1)S(1)} %bitcast.12, bf16[2048,128]{1,0:T(8,128)(2,1)S(1)} %bitcast.8, bf16[2048,128]{1,0:T(8,128)(2,1)S(1)} %prep.1.x_ref, ...), custom_call_target="tpu_custom_call", output_to_operand_aliasing={{0}: (5, {})} | custom-call | flops 2684354560 | bytes 2097152 | tf_op jit(solution)/shard_map/far_cd/pallas_call | solution.py:153
  40.9 1.9 %collective-permute-start.4 = (bf16[512,512]{1,0:T(8,128)(2,1)S(1)}, bf16[512,512]{1,0:T(8,128)(2,1)S(1)}, u32[]{:S(2)}, u32[]{:S(2)}) collective-permute-start(bf16[512,512]{1,0:T(8,128)(2,1)S(1)} %get-tuple-element.22), channel_id=1, source_target_pairs={{0,2},{2,0},{4,6},{6,4},{8,10},{10,8},{12,14},{14,12},{16,18},{18,... | collective-permute-start | bytes 1572872 | tf_op jit(solution)/shard_map/ppermute | solution.py:352
  42.8 1.9 %collective-permute-start.3 = (bf16[256,512]{1,0:T(8,128)(2,1)S(1)}, bf16[256,512]{1,0:T(8,128)(2,1)S(1)}, u32[]{:S(2)}, u32[]{:S(2)}) collective-permute-start(bf16[256,512]{1,0:T(8,128)(2,1)S(1)} %get-tuple-element.15._), channel_id=1, source_target_pairs={{4,0},{5,1},{511,2},{510,3},{8,4},{9,5},{2,6},{3,7},{12,8},{13,9},... | collective-permute-start | bytes 786440 | tf_op jit(solution)/shard_map/ppermute | solution.py:349
  44.8 0.0 collective-permute-done.4.b_ref.c_ref
  44.8 0.1 add.1
  44.9 4.0 %collective-permute-start.5 = (bf16[256,512]{1,0:T(8,128)(2,1)S(1)}, bf16[256,512]{1,0:T(8,128)(2,1)S(1)}, u32[]{:S(2)}, u32[]{:S(2)}) collective-permute-start(bf16[256,512]{1,0:T(8,128)(2,1)S(1)} %add.1), channel_id=1, source_target_pairs={{0,511},{1,510},{2,4},{3,5},{4,2},{5,3},{6,8},{7,9},{8,6},{9,7},{1... | collective-permute-start | bytes 786440 | tf_op jit(solution)/shard_map/ppermute | solution.py:353
  48.9 4.1 %own.1 = (bf16[2048,128]{1,0:T(8,128)(2,1)}, f32[256,512]{1,0:T(8,128)S(1)}) custom-call(s32[512]{0:T(512)S(1)} %copy-done.5, bf16[2048,128]{1,0:T(8,128)(2,1)S(1)} %bitcast.13, bf16[2048,128]{1,0:T(8,128)(2,1)S(1)} %bitcast.9, bf16[2048,128]{1,0:T(8,128)(2,1)S(1)} %prep.1.x_ref, bf16[1024,128]{1,0:T(8,128)(2,1)S(1)} %constant_dynamic-update-slice_fusion.a_ref.kv_ref, ...), custom_call_target="tpu_custom_call" | custom-call | flops 1342177280 | bytes 1048576 | tf_op jit(solution)/shard_map/own/pallas_call | solution.py:214
  53.0 3.7 %collective-permute-done.3.a_ref = bf16[256,512]{1,0:T(8,128)(2,1)S(1)} collective-permute-done((bf16[256,512]{1,0:T(8,128)(2,1)S(1)}, bf16[256,512]{1,0:T(8,128)(2,1)S(1)}, u32[]{:S(2)}, u32[]{:S(2)}) %collective-permute-start.3) | collective-permute-done | bytes 262176 | tf_op jit(solution)/shard_map/ppermute | solution.py:349
  56.7 0.0 collective-permute-done.5.b_ref
  56.7 0.1 merge.1
  56.8 1.9 %collective-permute-start.6 = (bf16[256,256]{1,0:T(8,128)(2,1)S(1)}, bf16[256,256]{1,0:T(8,128)(2,1)S(1)}, u32[]{:S(2)}, u32[]{:S(2)}) collective-permute-start(bf16[256,256]{1,0:T(8,128)(2,1)S(1)} %get-tuple-element.24), channel_id=1, source_target_pairs={{0,1},{1,0},{2,3},{3,2},{4,5},{5,4},{6,7},{7,6},{8,9},{9,8},{10,11... | collective-permute-start | bytes 393224 | tf_op jit(solution)/shard_map/ppermute | solution.py:356
  58.7 8.8 %collective-permute-done.6.got_ref = bf16[256,256]{1,0:T(8,128)(2,1)S(1)} collective-permute-done((bf16[256,256]{1,0:T(8,128)(2,1)S(1)}, bf16[256,256]{1,0:T(8,128)(2,1)S(1)}, u32[]{:S(2)}, u32[]{:S(2)}) %collective-permute-start.6) | collective-permute-done | bytes 131104 | tf_op jit(solution)/shard_map/ppermute | solution.py:356
  67.5 0.8 %last.1 = (bf16[256,128]{1,0:T(8,128)(2,1)}, bf16[256,128]{1,0:T(8,128)(2,1)}) custom-call(f32[256,256]{1,0:T(8,128)S(1)} %get-tuple-element.23.keep_ref, bf16[256,256]{1,0:T(8,128)(2,1)S(1)} %collective-permute-done.6.got_ref), custom_call_target="tpu_custom_call" | custom-call | tf_op jit(solution)/shard_map/last/pallas_call | solution.py:292
  (1 shorter events, 0.0 us)
Async XLA Ops:
  0.6 20.4 %copy-start = (bf16[512,4,128]{2,1,0:T(4,128)(2,1)S(1)}, bf16[512,4,128]{2,1,0:T(4,128)(2,1)}, u32[]{:S(2)}) copy-start(bf16[512,4,128]{2,1,0:T(4,128)(2,1)} %param.10) | copy-start | bytes 1572868
  2.5 21.2 %collective-permute-start.1 = (bf16[1024,128]{1,0:T(8,128)(2,1)S(1)}, bf16[1024,128]{1,0:T(8,128)(2,1)S(1)}, u32[]{:S(2)}, u32[]{:S(2)}) collective-permute-start(bf16[1024,128]{1,0:T(8,128)(2,1)S(1)} %constant_dynamic-update-slice_fusion.a_ref.kv_ref), channel_id=1, source_target_pairs={{0,4},{1,5},{2,511},{3,510},{4,8},{5,9},{6,2},{7,3},{8,12},{9,13},... | collective-permute-start | bytes 786440 | tf_op jit(solution)/shard_map/ppermute | solution.py:343
  19.1 8.4 %collective-permute-start = (bf16[1024,128]{1,0:T(8,128)(2,1)S(1)}, bf16[1024,128]{1,0:T(8,128)(2,1)S(1)}, u32[]{:S(2)}, u32[]{:S(2)}) collective-permute-start(bf16[1024,128]{1,0:T(8,128)(2,1)S(1)} %constant_dynamic-update-slice_fusion.a_ref.kv_ref), channel_id=1, source_target_pairs={{0,511},{1,510},{2,4},{3,5},{4,2},{5,3},{6,8},{7,9},{8,6},{9,7},{1... | collective-permute-start | bytes 786440 | tf_op jit(solution)/shard_map/ppermute | solution.py:344
  21.1 1.0 %copy-start.1 = (bf16[512,4,128]{2,1,0:T(4,128)(2,1)S(1)}, bf16[512,4,128]{2,1,0:T(4,128)(2,1)}, u32[]{:S(2)}) copy-start(bf16[512,4,128]{2,1,0:T(4,128)(2,1)} %param.11) | copy-start | bytes 1572868
  22.1 0.7 %copy-start.3 = (f32[4,512]{1,0:T(4,128)S(1)}, f32[4,512]{1,0:T(4,128)}, u32[]{:S(2)}) copy-start(f32[4,512]{1,0:T(4,128)} %lse_ref.1) | copy-start | bytes 24580
  22.8 1.0 %copy-start.2 = (bf16[512,4,128]{2,1,0:T(4,128)(2,1)S(1)}, bf16[512,4,128]{2,1,0:T(4,128)(2,1)}, u32[]{:S(2)}) copy-start(bf16[512,4,128]{2,1,0:T(4,128)(2,1)} %param.11) | copy-start | bytes 1572868
  22.8 1.2 %copy-start.4 = (bf16[512,4,128]{2,1,0:T(4,128)(2,1)S(1)}, bf16[512,4,128]{2,1,0:T(4,128)(2,1)}, u32[]{:S(2)}) copy-start(bf16[512,4,128]{2,1,0:T(4,128)(2,1)} %param.7) | copy-start | bytes 1572868
  22.8 1.2 %copy-start.5 = (s32[512]{0:T(512)S(1)}, s32[512]{0:T(512)}, u32[]{:S(2)}) copy-start(s32[512]{0:T(512)} %span_ref.7) | copy-start | bytes 6148
  27.6 6.9 %collective-permute-start.2 = (bf16[2048,128]{1,0:T(8,128)(2,1)S(1)}, bf16[2048,128]{1,0:T(8,128)(2,1)S(1)}, u32[]{:S(2)}, u32[]{:S(2)}) collective-permute-start(bf16[2048,128]{1,0:T(8,128)(2,1)S(1)} %pack.1), channel_id=1, source_target_pairs={{0,2},{2,0},{4,6},{6,4},{8,10},{10,8},{12,14},{14,12},{16,18},{18,... | collective-permute-start | bytes 1572872 | tf_op jit(solution)/shard_map/ppermute | solution.py:348
  40.9 3.9 %collective-permute-start.4 = (bf16[512,512]{1,0:T(8,128)(2,1)S(1)}, bf16[512,512]{1,0:T(8,128)(2,1)S(1)}, u32[]{:S(2)}, u32[]{:S(2)}) collective-permute-start(bf16[512,512]{1,0:T(8,128)(2,1)S(1)} %get-tuple-element.22), channel_id=1, source_target_pairs={{0,2},{2,0},{4,6},{6,4},{8,10},{10,8},{12,14},{14,12},{16,18},{18,... | collective-permute-start | bytes 1572872 | tf_op jit(solution)/shard_map/ppermute | solution.py:352
  42.8 13.8 %collective-permute-start.3 = (bf16[256,512]{1,0:T(8,128)(2,1)S(1)}, bf16[256,512]{1,0:T(8,128)(2,1)S(1)}, u32[]{:S(2)}, u32[]{:S(2)}) collective-permute-start(bf16[256,512]{1,0:T(8,128)(2,1)S(1)} %get-tuple-element.15._), channel_id=1, source_target_pairs={{4,0},{5,1},{511,2},{510,3},{8,4},{9,5},{2,6},{3,7},{12,8},{13,9},... | collective-permute-start | bytes 786440 | tf_op jit(solution)/shard_map/ppermute | solution.py:349
  44.9 11.8 %collective-permute-start.5 = (bf16[256,512]{1,0:T(8,128)(2,1)S(1)}, bf16[256,512]{1,0:T(8,128)(2,1)S(1)}, u32[]{:S(2)}, u32[]{:S(2)}) collective-permute-start(bf16[256,512]{1,0:T(8,128)(2,1)S(1)} %add.1), channel_id=1, source_target_pairs={{0,511},{1,510},{2,4},{3,5},{4,2},{5,3},{6,8},{7,9},{8,6},{9,7},{1... | collective-permute-start | bytes 786440 | tf_op jit(solution)/shard_map/ppermute | solution.py:353
  56.8 10.7 %collective-permute-start.6 = (bf16[256,256]{1,0:T(8,128)(2,1)S(1)}, bf16[256,256]{1,0:T(8,128)(2,1)S(1)}, u32[]{:S(2)}, u32[]{:S(2)}) collective-permute-start(bf16[256,256]{1,0:T(8,128)(2,1)S(1)} %get-tuple-element.24), channel_id=1, source_target_pairs={{0,1},{1,0},{2,3},{3,2},{4,5},{5,4},{6,7},{7,6},{8,9},{9,8},{10,11... | collective-permute-start | bytes 393224 | tf_op jit(solution)/shard_map/ppermute | solution.py:356

commit v3 on v2

--- a/solution.py
+++ b/solution.py
@@ -22,6 +22,40 @@
 def lane_ones(rows, low, high):
     lane = lax.broadcasted_iota(jnp.int32, (rows, 128), 1)
     return jnp.where((lane >= low) & (lane < high), 1.0, 0.0).astype(BF16)
+
+
+def load_kernel(k_ref, v_ref, q_ref, do_ref, out_ref, kv_to, q_to, do_to, out_to, sems):
+    rows = k_ref.shape[0]
+    copies = [
+        pltpu.make_async_copy(source, target, sems.at[i])
+        for i, (source, target) in enumerate(
+            [
+                (k_ref, kv_to.at[pl.ds(0, rows)]),
+                (v_ref, kv_to.at[pl.ds(rows, rows)]),
+                (do_ref, do_to),
+                (out_ref, out_to),
+                (q_ref, q_to),
+            ]
+        )
+    ]
+    for copy in copies:
+        copy.start()
+    for copy in copies:
+        copy.wait()
+
+
+def load(keys, values, q, do, out):
+    rows, depth = keys.shape
+    wide = jax.ShapeDtypeStruct(q.shape, q.dtype)
+    return pl.pallas_call(
+        load_kernel,
+        out_shape=[jax.ShapeDtypeStruct((2 * rows, depth), keys.dtype)] + [wide] * 3,
+        in_specs=[pl.BlockSpec(memory_space=pltpu.HBM)] * 5,
+        out_specs=[VMEM] * 4,
+        scratch_shapes=[pltpu.SemaphoreType.DMA((5,))],
+        compiler_params=pltpu.CompilerParams(vmem_limit_bytes=8 * 2**20),
+        name="load",
+    )(keys, values, q, do, out)
 
 
 def prep_kernel(grad_ref, out_ref, lse_ref, extra_ref, wide):
@@ -107,42 +141,58 @@
     half = q_ref.shape[0] // 2
     q0, q1 = span_ref[2 * me], span_ref[2 * me + 1]
 
-    def step(t, carry):
-        chunk, j = t // 2, t % 2
+    def run(base, rows, at, keys, k_rows, v_rows, lanes):
+        key, value = kv_ref[pl.ds(at, keys), :], kv_ref[pl.ds(at + tokens, keys), :]
+        terms, dk, dv = tile(q_ref, do_ref, x_ref, key, value, base, rows)
+        for rows_at, term in terms:
+            dq_ref[rows_at, :] += term
+        g_ref[k_rows, lanes] = dk.astype(g_ref.dtype)
+        g_ref[v_rows, lanes] = dv.astype(g_ref.dtype)
+
+    def block(chunk, carry):
         distance = distances[0] if len(distances) == 1 else jnp.where(chunk == 0, *distances)
         source = (me + sign * distance + count) % count
-        k_id = span_ref[2 * source + j]
-        at = pl.multiple_of(chunk * 2 * tokens + j * span, span)
-        key = lambda: kv_ref[pl.ds(at, span), :]
-        value = lambda: kv_ref[pl.ds(at + tokens, span), :]
+        k0, k1 = span_ref[2 * source], span_ref[2 * source + 1]
+        first_row = pl.multiple_of(chunk * 2 * tokens, 2 * tokens)
         k_rows = pl.ds(pl.multiple_of(chunk * 2 * depth, depth), depth)
         v_rows = pl.ds(pl.multiple_of(chunk * 2 * depth + depth, depth), depth)
-        lanes = pl.ds(pl.multiple_of(j * span, span), span)
-        a0, a1 = k_id < q0, k_id < q1
-
-        def run(base, rows):
-            terms, dk, dv = tile(q_ref, do_ref, x_ref, key(), value(), base, rows)
-            for rows_at, term in terms:
-                dq_ref[rows_at, :] += term
-            g_ref[k_rows, lanes] = dk.astype(g_ref.dtype)
-            g_ref[v_rows, lanes] = dv.astype(g_ref.dtype)
-
-        @pl.when(a0 & a1)
+        every = jnp.maximum(k0, k1) < jnp.minimum(q0, q1)
+
+        @pl.when(every)
         def _():
-            run(0, 2 * half)
-
-        @pl.when(a0 != a1)
+            run(0, 2 * half, first_row, tokens, k_rows, v_rows, pl.ds(0, tokens))
+
+        def one_span(j, carry):
+            k_id = jnp.where(j == 0, k0, k1)
+            at = pl.multiple_of(first_row + j * span, span)
+            lanes = pl.ds(pl.multiple_of(j * span, span), span)
+            a0, a1 = k_id < q0, k_id < q1
+
+            @pl.when(a0 & a1)
+            def _():
+                run(0, 2 * half, at, span, k_rows, v_rows, lanes)
+
+            @pl.when(a0 != a1)
+            def _():
+                run(jnp.where(a1, half, 0), half, at, span, k_rows, v_rows, lanes)
+
+            @pl.when(~(a0 | a1))
+            def _():
+                g_ref[k_rows, lanes] = jnp.zeros((depth, span), g_ref.dtype)
+                g_ref[v_rows, lanes] = jnp.zeros((depth, span), g_ref.dtype)
+
+            return carry
+
+        @pl.when(~every)
         def _():
-            run(jnp.where(a1, half, 0), half)
-
-        @pl.when(~(a0 | a1))
-        def _():
-            g_ref[k_rows, lanes] = jnp.zeros((depth, span), g_ref.dtype)
-            g_ref[v_rows, lanes] = jnp.zeros((depth, span), g_ref.dtype)
+            lax.fori_loop(0, 2, one_span, 0)
 
         return carry
 
-    lax.fori_loop(0, 2 * len(distances), step, 0)
+    if len(distances) == 1:
+        block(0, 0)
+    else:
+        lax.fori_loop(0, len(distances), block, 0)
 
 
 def far(distances, spans, q, do, x, kv, dq, dtype, name):
@@ -169,65 +219,88 @@
     )(*args)
 
 
-def own_kernel(span_ref, q_ref, do_ref, x_ref, kv_ref, dqin_ref, dq_ref, g_ref, acc):
+def own_low_kernel(span_ref, q_ref, do_ref, x_ref, kv_ref, _, dq_ref, g_ref):
     me = lax.axis_index("ctx")
     depth = q_ref.shape[1]
     tokens = kv_ref.shape[0] // 2
-    span = tokens // 2
-    half = q_ref.shape[0] // 2
+    span, half = tokens // 2, q_ref.shape[0] // 2
     heads = half // span
-    later_first = span_ref[2 * me] > span_ref[2 * me + 1]
-
-    def causal(base, rows, span):
-        token = (base + lax.broadcasted_iota(jnp.int32, (rows, span), 0)) // heads
-        return lax.broadcasted_iota(jnp.int32, (rows, span), 1) <= token
-
-    def load(j):
-        at = pl.multiple_of(j * span, span)
-        return kv_ref[pl.ds(at, span), :], kv_ref[pl.ds(at + tokens, span), :]
-
-    def step(j, carry):
-        key, value = load(j)
-        terms, dk, dv = tile(q_ref, do_ref, x_ref, key, value, j * half, half, causal)
-        for rows_at, term in terms:
-            acc[rows_at, :] = dqin_ref[rows_at, :] + term
-        lanes = pl.ds(pl.multiple_of(j * span, span), span)
-        g_ref[0:depth, lanes] = dk
-        g_ref[depth : 2 * depth, lanes] = dv
-        return carry
-
-    lax.fori_loop(0, 2, step, 0)
-    j = jnp.where(later_first, 1, 0)
-    key, value = load(j)
-    terms, dk, dv = tile(q_ref, do_ref, x_ref, key, value, (1 - j) * half, half)
+    low = jnp.where(span_ref[2 * me] > span_ref[2 * me + 1], 1, 0)
+
+    def causal(base, rows, keys):
+        token = (base + lax.broadcasted_iota(jnp.int32, (rows, keys), 0)) // heads
+        return lax.broadcasted_iota(jnp.int32, (rows, keys), 1) <= token
+
+    at = pl.multiple_of(low * span, span)
+    key, value = kv_ref[pl.ds(at, span), :], kv_ref[pl.ds(at + tokens, span), :]
+    terms, dk, dv = tile(q_ref, do_ref, x_ref, key, value, low * half, half, causal)
     for rows_at, term in terms:
-        acc[rows_at, :] += term
-    lanes = pl.ds(pl.multiple_of(j * span, span), span)
-    g_ref[0:depth, lanes] += dk
-    g_ref[depth : 2 * depth, lanes] += dv
-    dq_ref[...] = (acc[...] * float(depth**-0.5)).astype(dq_ref.dtype)
-
-
-def own(spans, q, do, x, kv, dq):
+        dq_ref[rows_at, :] += term
+    g_ref[0:depth, :] = dk
+    g_ref[depth : 2 * depth, :] = dv
+
+
+def own_high_kernel(span_ref, q_ref, do_ref, x_ref, kv_ref, g_low_ref, _, dq_ref, g_ref):
+    me = lax.axis_index("ctx")
+    depth = q_ref.shape[1]
+    tokens = kv_ref.shape[0] // 2
+    span, half = tokens // 2, q_ref.shape[0] // 2
+    heads = half // span
+    low = jnp.where(span_ref[2 * me] > span_ref[2 * me + 1], 1, 0)
+
+    def causal(base, rows, keys):
+        token = (base + lax.broadcasted_iota(jnp.int32, (rows, keys), 0)) // heads
+        slot = lax.broadcasted_iota(jnp.int32, (rows, keys), 1)
+        return (slot - (1 - low) * span <= token) & ((slot >= span) | (low == 1)) | (
+            (slot // span) == low
+        )
+
+    terms, dk, dv = tile(
+        q_ref, do_ref, x_ref, kv_ref[0:tokens, :], kv_ref[tokens : 2 * tokens, :],
+        (1 - low) * half, half, causal,
+    )
+    for rows_at, term in terms:
+        dq_ref[rows_at, :] += term
+    g_ref[0:depth, :] = dk
+    g_ref[depth : 2 * depth, :] = dv
+    lanes = pl.ds(pl.multiple_of(low * span, span), span)
+    g_ref[:, lanes] += g_low_ref[...]
+
+
+def own(kernel, spans, q, do, x, kv, extra, dq, keys, name):
     rows, depth = q.shape
-    tokens = kv.shape[0] // 2
-    return pl.pallas_call(
-        own_kernel,
+    args = [spans, q, do, x, kv] + extra + [dq]
+    return pl.pallas_call(
+        kernel,
         out_shape=[
-            jax.ShapeDtypeStruct((rows, depth), BF16),
-            jax.ShapeDtypeStruct((2 * depth, tokens), F32),
+            jax.ShapeDtypeStruct((rows, depth), F32),
+            jax.ShapeDtypeStruct((2 * depth, keys), F32),
         ],
-        in_specs=[SMEM] + [VMEM] * 5,
+        in_specs=[SMEM] + [VMEM] * (len(args) - 1),
         out_specs=[VMEM, VMEM],
-        scratch_shapes=[pltpu.VMEM((rows, depth), F32)],
+        input_output_aliases={len(args) - 1: 0},
         compiler_params=pltpu.CompilerParams(vmem_limit_bytes=24 * 2**20),
         cost_estimate=pl.CostEstimate(
-            flops=10 * rows * tokens * depth,
-            bytes_accessed=2**20,
-            transcendentals=rows * tokens,
+            flops=5 * rows * keys * depth, bytes_accessed=2**20, transcendentals=rows * keys // 2
         ),
-        name="own",
-    )(spans, q, do, x, kv, dq)
+        name=name,
+    )(*args)
+
+
+def finish_kernel(dq_ref, o_ref):
+    o_ref[...] = (dq_ref[...] * float(dq_ref.shape[1] ** -0.5)).astype(BF16)
+
+
+def finish(dq):
+    return pl.pallas_call(
+        finish_kernel,
+        out_shape=jax.ShapeDtypeStruct(dq.shape, BF16),
+        in_specs=[VMEM],
+        out_specs=VMEM,
+        compiler_params=pltpu.CompilerParams(vmem_limit_bytes=8 * 2**20),
+        cost_estimate=pl.CostEstimate(flops=dq.size, bytes_accessed=6 * dq.size, transcendentals=0),
+        name="finish",
+    )(dq)
 
 
 def add_kernel(a_ref, b_ref, o_ref):
@@ -339,7 +412,7 @@
     over_one = ring(count, lambda d: d + 1 if d % 2 else d - 1)
     mates = [(d, d ^ 1) for d in range(count)]
 
-    kv = jnp.concatenate([keys, values], axis=0)
+    kv, q, do, out = load(keys, values, q, do, out)
     kv_a = lax.ppermute(kv, both, over_two)
     kv_b = lax.ppermute(kv, both, over_one)
     x = prep(do, out, lse)
@@ -350,12 +423,15 @@
     dq, g_b = far((-1,), span_order, q, do, x, kv_b, dq, F32, "far_b")
     dq, g_cd = far((1, 2), span_order, q, do, x, kv_cd, dq, BF16, "far_cd")
     got_cd = lax.ppermute(g_cd, "ctx", mates)
+    span = tokens // 2
+    dq, g_low = own(own_low_kernel, span_order, q, do, x, kv, [], dq, span, "own_low")
     got_b = lax.ppermute(add(g_b, got_cd), both, over_one)
-    dq, g_own = own(span_order, q, do, x, kv, dq)
+    dq, g_own = own(own_high_kernel, span_order, q, do, x, kv, [g_low], dq, tokens, "own_high")
     keep, send = merge(g_own, got_a, got_b, got_cd)
     got = lax.ppermute(send, "head", [(0, 1), (1, 0)])
+    grad_q = finish(dq)
     grad_k, grad_v = last(keep, got)
-    return dq.reshape(tokens, heads, depth), grad_k, grad_v
+    return grad_q.reshape(tokens, heads, depth), grad_k, grad_v
 
 
 def solution(mesh):

time: 68.7 us -> 71.6 us (1.042)
  the two profiles are of different devices: /device:TPU:1 before, /device:TPU:0 now
where the time goes in v3:
time: 71.6 us; the launch traced here: 71.1 us
  starting transfers between devices  31.8 us (44%)
  waiting for transfers between devices  20.2 us (28%)
  Pallas kernels  13.4 us (19%)
  local copies, waits for them, and re-layouts  4.93 us (7%)
  between operations  0.81 us (1%)
    ppermute x1, starting transfers between devices, local(): kv_b = lax.ppermute(kv, both, over_one)  10.7 us
    ppermute x1, starting transfers between devices, local(): got_a = lax.ppermute(g_a, both, back_two)  9.31 us
    ppermute x1, waiting for transfers between devices, local(): got_b = lax.ppermute(add(g_b, got_cd), both, over_one)  8.91 us
    ppermute x1, waiting for transfers between devices, local(): got = lax.ppermute(send, 'head', [(0, 1), (1, 0)])  7.64 us
    pallas_call x3, Pallas kernels, far(): pl.pallas_call(functools.partial(far_kernel, distances, dq is None), out_...  6.13 us
    unnamed x14, local copies, waits for them, and re-layouts  4.93 us
    pallas_call x2, Pallas kernels, own(): pl.pallas_call(kernel, out_shape=[jax.ShapeDtypeStruct((rows, depth), F32...  4.01 us
    ppermute x1, starting transfers between devices, local(): got_cd = lax.ppermute(g_cd, 'ctx', mates)  3.85 us
  transfers between devices with their start and end apart: 7, of which 4 were waited for; matrix products, arithmetic and copies ran while one was open for 0% of the time, Pallas kernels for 12%

profile of v3, /device:TPU:0, one launch (start us, length us, event | category | flops | bytes accessed | tf_op | source)
XLA Modules:
  0.0 71.1 jit_solution(315520575385854994)
XLA Ops:
  0.6 0.0 copy-start
  0.6 1.0 %copy-done = bf16[512,4,128]{2,1,0:T(4,128)(2,1)S(1)} copy-done((bf16[512,4,128]{2,1,0:T(4,128)(2,1)S(1)}, bf16[512,4,128]{2,1,0:T(4,128)(2,1)}, u32[]{:S(2)}) %copy-start) | copy-done | bytes 524312
  1.7 0.0 copy-start.1
  1.7 1.0 %copy-done.1 = bf16[512,4,128]{2,1,0:T(4,128)(2,1)S(1)} copy-done((bf16[512,4,128]{2,1,0:T(4,128)(2,1)S(1)}, bf16[512,4,128]{2,1,0:T(4,128)(2,1)}, u32[]{:S(2)}) %copy-start.1) | copy-done | bytes 524312
  2.7 0.0 copy-start.2
  2.7 1.0 %copy-done.2 = bf16[512,4,128]{2,1,0:T(4,128)(2,1)S(1)} copy-done((bf16[512,4,128]{2,1,0:T(4,128)(2,1)S(1)}, bf16[512,4,128]{2,1,0:T(4,128)(2,1)}, u32[]{:S(2)}) %copy-start.2) | copy-done | bytes 524312
  3.8 0.0 copy-start.3
  3.8 0.9 %copy-done.3 = bf16[512,128]{1,0:T(8,128)(2,1)S(1)} copy-done((bf16[512,128]{1,0:T(8,128)(2,1)S(1)}, bf16[512,128]{1,0:T(8,128)(2,1)}, u32[]{:S(2)}) %copy-start.3) | copy-done | bytes 131096
  4.7 0.0 copy-start.4
  4.7 0.9 %copy-done.4 = bf16[512,128]{1,0:T(8,128)(2,1)S(1)} copy-done((bf16[512,128]{1,0:T(8,128)(2,1)S(1)}, bf16[512,128]{1,0:T(8,128)(2,1)}, u32[]{:S(2)}) %copy-start.4) | copy-done | bytes 131096
  5.6 0.0 copy-start.5
  5.6 0.5 load.1
  6.0 1.9 %collective-permute-start.1 = (bf16[1024,128]{1,0:T(8,128)(2,1)S(1)}, bf16[1024,128]{1,0:T(8,128)(2,1)S(1)}, u32[]{:S(2)}, u32[]{:S(2)}) collective-permute-start(bf16[1024,128]{1,0:T(8,128)(2,1)S(1)} %get-tuple-element.24.a_ref.kv_ref), channel_id=1, source_target_pairs={{0,4},{1,5},{2,511},{3,510},{4,8},{5,9},{6,2},{7,3},{8,12},{9,13},... | collective-permute-start | bytes 786440 | tf_op jit(solution)/shard_map/ppermute | solution.py:416
  8.0 10.7 %collective-permute-start = (bf16[1024,128]{1,0:T(8,128)(2,1)S(1)}, bf16[1024,128]{1,0:T(8,128)(2,1)S(1)}, u32[]{:S(2)}, u32[]{:S(2)}) collective-permute-start(bf16[1024,128]{1,0:T(8,128)(2,1)S(1)} %get-tuple-element.24.a_ref.kv_ref), channel_id=1, source_target_pairs={{0,511},{1,510},{2,4},{3,5},{4,2},{5,3},{6,8},{7,9},{8,6},{9,7},{1... | collective-permute-start | bytes 786440 | tf_op jit(solution)/shard_map/ppermute | solution.py:417
  18.6 0.0 copy-done.5
  18.6 0.0 copy-start.6
  18.7 0.9 %prep.1.x_ref = bf16[2048,128]{1,0:T(8,128)(2,1)S(1)} custom-call(bf16[2048,128]{1,0:T(8,128)(2,1)S(1)} %get-tuple-element.22.grad_ref.do_ref, bf16[2048,128]{1,0:T(8,128)(2,1)S(1)} %get-tuple-element.23.out_ref, f32[4,512]{1,0:T(4,128)S(1)} %copy-done.5), custom_call_target="tpu_custom_call" | custom-call | flops 2097152 | bytes 1572864 | tf_op jit(solution)/shard_map/prep/pallas_call | solution.py:86
  19.6 2.6 %collective-permute-done.1.kv_ref = bf16[1024,128]{1,0:T(8,128)(2,1)S(1)} collective-permute-done((bf16[1024,128]{1,0:T(8,128)(2,1)S(1)}, bf16[1024,128]{1,0:T(8,128)(2,1)S(1)}, u32[]{:S(2)}, u32[]{:S(2)}) %collective-permute-start.1) | collective-permute-done | bytes 262176 | tf_op jit(solution)/shard_map/ppermute | solution.py:416
  22.2 0.0 copy-done.6
  22.2 2.1 %far_a.1 = (f32[2048,128]{1,0:T(8,128)S(1)}, bf16[256,512]{1,0:T(8,128)(2,1)S(1)}) custom-call(s32[512]{0:T(512)S(1)} %copy-done.6, bf16[2048,128]{1,0:T(8,128)(2,1)S(1)} %get-tuple-element.21.q_ref, bf16[2048,128]{1,0:T(8,128)(2,1)S(1)} %get-tuple-element.22.grad_ref.do_ref, bf16[2048,128]{1,0:T(8,128)(2,1)S(1)} %prep.1.x_ref, ...), custom_call_target="tpu_custom_call" | custom-call | flops 1342177280 | bytes 1048576 | tf_op jit(solution)/shard_map/far_a/pallas_call | solution.py:203
  24.3 0.0 collective-permute-done.b_ref.kv_ref
  24.3 1.9 %collective-permute-start.2 = (bf16[2048,128]{1,0:T(8,128)(2,1)S(1)}, bf16[2048,128]{1,0:T(8,128)(2,1)S(1)}, u32[]{:S(2)}, u32[]{:S(2)}) collective-permute-start(bf16[2048,128]{1,0:T(8,128)(2,1)S(1)} %pack.1), channel_id=1, source_target_pairs={{0,2},{2,0},{4,6},{6,4},{8,10},{10,8},{12,14},{14,12},{16,18},{18,... | collective-permute-start | bytes 1572872 | tf_op jit(solution)/shard_map/ppermute | solution.py:421
  26.3 0.9 %far_b.1 = (f32[2048,128]{1,0:T(8,128)S(1)}, f32[256,512]{1,0:T(8,128)S(1)}) custom-call(s32[512]{0:T(512)S(1)} %copy-done.6, bf16[2048,128]{1,0:T(8,128)(2,1)S(1)} %get-tuple-element.21.q_ref, bf16[2048,128]{1,0:T(8,128)(2,1)S(1)} %get-tuple-element.22.grad_ref.do_ref, bf16[2048,128]{1,0:T(8,128)(2,1)S(1)} %prep.1.x_ref, ...), custom_call_target="tpu_custom_call", output_to_operand_aliasing={{0}: (5, {})} | custom-call | flops 1342177280 | bytes 1048576 | tf_op jit(solution)/shard_map/far_b/pallas_call | solution.py:203
  27.1 1.0 %collective-permute-done.2.kv_ref = bf16[2048,128]{1,0:T(8,128)(2,1)S(1)} collective-permute-done((bf16[2048,128]{1,0:T(8,128)(2,1)S(1)}, bf16[2048,128]{1,0:T(8,128)(2,1)S(1)}, u32[]{:S(2)}, u32[]{:S(2)}) %collective-permute-start.2) | collective-permute-done | bytes 524320 | tf_op jit(solution)/shard_map/ppermute | solution.py:421
  28.1 3.2 %far_cd.1 = (f32[2048,128]{1,0:T(8,128)S(1)}, bf16[512,512]{1,0:T(8,128)(2,1)S(1)}) custom-call(s32[512]{0:T(512)S(1)} %copy-done.6, bf16[2048,128]{1,0:T(8,128)(2,1)S(1)} %get-tuple-element.21.q_ref, bf16[2048,128]{1,0:T(8,128)(2,1)S(1)} %get-tuple-element.22.grad_ref.do_ref, bf16[2048,128]{1,0:T(8,128)(2,1)S(1)} %prep.1.x_ref, ...), custom_call_target="tpu_custom_call", output_to_operand_aliasing={{0}: (5, {})} | custom-call | flops 2684354560 | bytes 2097152 | tf_op jit(solution)/shard_map/far_cd/pallas_call | solution.py:203
  31.4 3.8 %collective-permute-start.4 = (bf16[512,512]{1,0:T(8,128)(2,1)S(1)}, bf16[512,512]{1,0:T(8,128)(2,1)S(1)}, u32[]{:S(2)}, u32[]{:S(2)}) collective-permute-start(bf16[512,512]{1,0:T(8,128)(2,1)S(1)} %get-tuple-element.34), channel_id=1, source_target_pairs={{0,2},{2,0},{4,6},{6,4},{8,10},{10,8},{12,14},{14,12},{16,18},{18,... | collective-permute-start | bytes 1572872 | tf_op jit(solution)/shard_map/ppermute | solution.py:425
  35.2 9.3 %collective-permute-start.3 = (bf16[256,512]{1,0:T(8,128)(2,1)S(1)}, bf16[256,512]{1,0:T(8,128)(2,1)S(1)}, u32[]{:S(2)}, u32[]{:S(2)}) collective-permute-start(bf16[256,512]{1,0:T(8,128)(2,1)S(1)} %get-tuple-element.25._), channel_id=1, source_target_pairs={{4,0},{5,1},{511,2},{510,3},{8,4},{9,5},{2,6},{3,7},{12,8},{13,9},... | collective-permute-start | bytes 786440 | tf_op jit(solution)/shard_map/ppermute | solution.py:422
  44.5 0.0 collective-permute-done.4.b_ref.c_ref
  44.6 1.9 %collective-permute-start.5 = (bf16[256,512]{1,0:T(8,128)(2,1)S(1)}, bf16[256,512]{1,0:T(8,128)(2,1)S(1)}, u32[]{:S(2)}, u32[]{:S(2)}) collective-permute-start(bf16[256,512]{1,0:T(8,128)(2,1)S(1)} %add.1), channel_id=1, source_target_pairs={{0,511},{1,510},{2,4},{3,5},{4,2},{5,3},{6,8},{7,9},{8,6},{9,7},{1... | collective-permute-start | bytes 786440 | tf_op jit(solution)/shard_map/ppermute | solution.py:428
  46.5 1.5 %own_low.1 = (f32[2048,128]{1,0:T(8,128)S(1)}, f32[256,256]{1,0:T(8,128)S(1)}) custom-call(s32[512]{0:T(512)S(1)} %copy-done.6, bf16[2048,128]{1,0:T(8,128)(2,1)S(1)} %get-tuple-element.21.q_ref, bf16[2048,128]{1,0:T(8,128)(2,1)S(1)} %get-tuple-element.22.grad_ref.do_ref, bf16[2048,128]{1,0:T(8,128)(2,1)S(1)} %prep.1.x_ref, ...), custom_call_target="tpu_custom_call", output_to_operand_aliasing={{0}: (5, {})} | custom-call | flops 335544320 | bytes 1048576 | tf_op jit(solution)/shard_map/own_low/pallas_call | solution.py:273
  48.0 2.5 %own_high.1 = (f32[2048,128]{1,0:T(8,128)S(1)}, f32[256,512]{1,0:T(8,128)S(1)}) custom-call(s32[512]{0:T(512)S(1)} %copy-done.6, bf16[2048,128]{1,0:T(8,128)(2,1)S(1)} %get-tuple-element.21.q_ref, bf16[2048,128]{1,0:T(8,128)(2,1)S(1)} %get-tuple-element.22.grad_ref.do_ref, bf16[2048,128]{1,0:T(8,128)(2,1)S(1)} %prep.1.x_ref, ...), custom_call_target="tpu_custom_call", output_to_operand_aliasing={{0}: (6, {})} | custom-call | flops 671088640 | bytes 1048576 | tf_op jit(solution)/shard_map/own_high/pallas_call | solution.py:273
  50.5 0.0 collective-permute-done.3.a_ref
  50.6 8.9 %collective-permute-done.5.b_ref = bf16[256,512]{1,0:T(8,128)(2,1)S(1)} collective-permute-done((bf16[256,512]{1,0:T(8,128)(2,1)S(1)}, bf16[256,512]{1,0:T(8,128)(2,1)S(1)}, u32[]{:S(2)}, u32[]{:S(2)}) %collective-permute-start.5) | collective-permute-done | bytes 262176 | tf_op jit(solution)/shard_map/ppermute | solution.py:428
  59.5 0.1 merge.1
  59.6 2.2 %collective-permute-start.6 = (bf16[256,256]{1,0:T(8,128)(2,1)S(1)}, bf16[256,256]{1,0:T(8,128)(2,1)S(1)}, u32[]{:S(2)}, u32[]{:S(2)}) collective-permute-start(bf16[256,256]{1,0:T(8,128)(2,1)S(1)} %get-tuple-element.36), channel_id=1, source_target_pairs={{0,1},{1,0},{2,3},{3,2},{4,5},{5,4},{6,7},{7,6},{8,9},{9,8},{10,11... | collective-permute-start | bytes 393224 | tf_op jit(solution)/shard_map/ppermute | solution.py:431
  61.8 0.9 %finish.1 = bf16[2048,128]{1,0:T(8,128)(2,1)} custom-call(f32[2048,128]{1,0:T(8,128)S(1)} %get-tuple-element.31.dq_ref), custom_call_target="tpu_custom_call" | custom-call | flops 262144 | bytes 1572864 | tf_op jit(solution)/shard_map/finish/pallas_call | solution.py:295
  62.7 7.6 %collective-permute-done.6.got_ref = bf16[256,256]{1,0:T(8,128)(2,1)S(1)} collective-permute-done((bf16[256,256]{1,0:T(8,128)(2,1)S(1)}, bf16[256,256]{1,0:T(8,128)(2,1)S(1)}, u32[]{:S(2)}, u32[]{:S(2)}) %collective-permute-start.6) | collective-permute-done | bytes 131104 | tf_op jit(solution)/shard_map/ppermute | solution.py:431
  70.4 0.8 %last.1 = (bf16[256,128]{1,0:T(8,128)(2,1)}, bf16[256,128]{1,0:T(8,128)(2,1)}) custom-call(f32[256,256]{1,0:T(8,128)S(1)} %get-tuple-element.35.keep_ref, bf16[256,256]{1,0:T(8,128)(2,1)S(1)} %collective-permute-done.6.got_ref), custom_call_target="tpu_custom_call" | custom-call | tf_op jit(solution)/shard_map/last/pallas_call | solution.py:365
  (2 shorter events, 0.1 us)
Async XLA Ops:
  0.6 1.0 %copy-start = (bf16[512,4,128]{2,1,0:T(4,128)(2,1)S(1)}, bf16[512,4,128]{2,1,0:T(4,128)(2,1)}, u32[]{:S(2)}) copy-start(bf16[512,4,128]{2,1,0:T(4,128)(2,1)} %param.7) | copy-start | bytes 1572868
  1.7 1.0 %copy-start.1 = (bf16[512,4,128]{2,1,0:T(4,128)(2,1)S(1)}, bf16[512,4,128]{2,1,0:T(4,128)(2,1)}, u32[]{:S(2)}) copy-start(bf16[512,4,128]{2,1,0:T(4,128)(2,1)} %param.11) | copy-start | bytes 1572868
  2.7 1.0 %copy-start.2 = (bf16[512,4,128]{2,1,0:T(4,128)(2,1)S(1)}, bf16[512,4,128]{2,1,0:T(4,128)(2,1)}, u32[]{:S(2)}) copy-start(bf16[512,4,128]{2,1,0:T(4,128)(2,1)} %param.10) | copy-start | bytes 1572868
  3.8 0.9 %copy-start.3 = (bf16[512,128]{1,0:T(8,128)(2,1)S(1)}, bf16[512,128]{1,0:T(8,128)(2,1)}, u32[]{:S(2)}) copy-start(bf16[512,128]{1,0:T(8,128)(2,1)} %k_ref.1) | copy-start | bytes 393220
  4.7 0.9 %copy-start.4 = (bf16[512,128]{1,0:T(8,128)(2,1)S(1)}, bf16[512,128]{1,0:T(8,128)(2,1)}, u32[]{:S(2)}) copy-start(bf16[512,128]{1,0:T(8,128)(2,1)} %v_ref.1) | copy-start | bytes 393220
  5.6 13.1 %copy-start.5 = (f32[4,512]{1,0:T(4,128)S(1)}, f32[4,512]{1,0:T(4,128)}, u32[]{:S(2)}) copy-start(f32[4,512]{1,0:T(4,128)} %lse_ref.1) | copy-start | bytes 24580
  6.0 16.1 %collective-permute-start.1 = (bf16[1024,128]{1,0:T(8,128)(2,1)S(1)}, bf16[1024,128]{1,0:T(8,128)(2,1)S(1)}, u32[]{:S(2)}, u32[]{:S(2)}) collective-permute-start(bf16[1024,128]{1,0:T(8,128)(2,1)S(1)} %get-tuple-element.24.a_ref.kv_ref), channel_id=1, source_target_pairs={{0,4},{1,5},{2,511},{3,510},{4,8},{5,9},{6,2},{7,3},{8,12},{9,13},... | collective-permute-start | bytes 786440 | tf_op jit(solution)/shard_map/ppermute | solution.py:416
  8.0 16.3 %collective-permute-start = (bf16[1024,128]{1,0:T(8,128)(2,1)S(1)}, bf16[1024,128]{1,0:T(8,128)(2,1)S(1)}, u32[]{:S(2)}, u32[]{:S(2)}) collective-permute-start(bf16[1024,128]{1,0:T(8,128)(2,1)S(1)} %get-tuple-element.24.a_ref.kv_ref), channel_id=1, source_target_pairs={{0,511},{1,510},{2,4},{3,5},{4,2},{5,3},{6,8},{7,9},{8,6},{9,7},{1... | collective-permute-start | bytes 786440 | tf_op jit(solution)/shard_map/ppermute | solution.py:417
  18.6 3.6 %copy-start.6 = (s32[512]{0:T(512)S(1)}, s32[512]{0:T(512)}, u32[]{:S(2)}) copy-start(s32[512]{0:T(512)} %span_ref.9) | copy-start | bytes 6148
  24.3 3.8 %collective-permute-start.2 = (bf16[2048,128]{1,0:T(8,128)(2,1)S(1)}, bf16[2048,128]{1,0:T(8,128)(2,1)S(1)}, u32[]{:S(2)}, u32[]{:S(2)}) collective-permute-start(bf16[2048,128]{1,0:T(8,128)(2,1)S(1)} %pack.1), channel_id=1, source_target_pairs={{0,2},{2,0},{4,6},{6,4},{8,10},{10,8},{12,14},{14,12},{16,18},{18,... | collective-permute-start | bytes 1572872 | tf_op jit(solution)/shard_map/ppermute | solution.py:421
  31.4 13.2 %collective-permute-start.4 = (bf16[512,512]{1,0:T(8,128)(2,1)S(1)}, bf16[512,512]{1,0:T(8,128)(2,1)S(1)}, u32[]{:S(2)}, u32[]{:S(2)}) collective-permute-start(bf16[512,512]{1,0:T(8,128)(2,1)S(1)} %get-tuple-element.34), channel_id=1, source_target_pairs={{0,2},{2,0},{4,6},{6,4},{8,10},{10,8},{12,14},{14,12},{16,18},{18,... | collective-permute-start | bytes 1572872 | tf_op jit(solution)/shard_map/ppermute | solution.py:425
  35.2 15.3 %collective-permute-start.3 = (bf16[256,512]{1,0:T(8,128)(2,1)S(1)}, bf16[256,512]{1,0:T(8,128)(2,1)S(1)}, u32[]{:S(2)}, u32[]{:S(2)}) collective-permute-start(bf16[256,512]{1,0:T(8,128)(2,1)S(1)} %get-tuple-element.25._), channel_id=1, source_target_pairs={{4,0},{5,1},{511,2},{510,3},{8,4},{9,5},{2,6},{3,7},{12,8},{13,9},... | collective-permute-start | bytes 786440 | tf_op jit(solution)/shard_map/ppermute | solution.py:422
  44.6 14.9 %collective-permute-start.5 = (bf16[256,512]{1,0:T(8,128)(2,1)S(1)}, bf16[256,512]{1,0:T(8,128)(2,1)S(1)}, u32[]{:S(2)}, u32[]{:S(2)}) collective-permute-start(bf16[256,512]{1,0:T(8,128)(2,1)S(1)} %add.1), channel_id=1, source_target_pairs={{0,511},{1,510},{2,4},{3,5},{4,2},{5,3},{6,8},{7,9},{8,6},{9,7},{1... | collective-permute-start | bytes 786440 | tf_op jit(solution)/shard_map/ppermute | solution.py:428
  59.6 10.8 %collective-permute-start.6 = (bf16[256,256]{1,0:T(8,128)(2,1)S(1)}, bf16[256,256]{1,0:T(8,128)(2,1)S(1)}, u32[]{:S(2)}, u32[]{:S(2)}) collective-permute-start(bf16[256,256]{1,0:T(8,128)(2,1)S(1)} %get-tuple-element.36), channel_id=1, source_target_pairs={{0,1},{1,0},{2,3},{3,2},{4,5},{5,4},{6,7},{7,6},{8,9},{9,8},{10,11... | collective-permute-start | bytes 393224 | tf_op jit(solution)/shard_map/ppermute | solution.py:431

commit v4 on v3

--- a/solution.py
+++ b/solution.py
@@ -47,6 +47,7 @@
 def load(keys, values, q, do, out):
     rows, depth = keys.shape
     wide = jax.ShapeDtypeStruct(q.shape, q.dtype)
+    args = [pltpu.with_memory_space_constraint(a, pltpu.HBM) for a in (keys, values, q, do, out)]
     return pl.pallas_call(
         load_kernel,
         out_shape=[jax.ShapeDtypeStruct((2 * rows, depth), keys.dtype)] + [wide] * 3,
@@ -55,7 +56,7 @@
         scratch_shapes=[pltpu.SemaphoreType.DMA((5,))],
         compiler_params=pltpu.CompilerParams(vmem_limit_bytes=8 * 2**20),
         name="load",
-    )(keys, values, q, do, out)
+    )(*args)
 
 
 def prep_kernel(grad_ref, out_ref, lse_ref, extra_ref, wide):
@@ -126,97 +127,80 @@
     return terms, dk, dv
 
 
-def far_kernel(distances, first, span_ref, q_ref, do_ref, x_ref, kv_ref, *refs):
-    if first:
-        dq_ref, g_ref = refs
-        dq_ref[...] = jnp.zeros_like(dq_ref)
-    else:
-        _, dq_ref, g_ref = refs
+def far_kernel(distance, index, first, span_ref, q_ref, do_ref, x_ref, kv_ref, *refs):
+    dq_ref, g_ref = refs if first else refs[-2:]
     count = lax.axis_size("ctx")
     me = lax.axis_index("ctx")
-    sign = 1 - 2 * (me % 2)
     depth = q_ref.shape[1]
-    tokens = kv_ref.shape[0] // (2 * len(distances))
+    tokens = g_ref.shape[1]
     span = tokens // 2
     half = q_ref.shape[0] // 2
+    first_row = 2 * tokens * index
+    source = (me + (1 - 2 * (me % 2)) * distance + count) % count
     q0, q1 = span_ref[2 * me], span_ref[2 * me + 1]
-
-    def run(base, rows, at, keys, k_rows, v_rows, lanes):
+    k0, k1 = span_ref[2 * source], span_ref[2 * source + 1]
+    every = jnp.maximum(k0, k1) < jnp.minimum(q0, q1)
+
+    def run(base, rows, at, keys, lanes, store=False):
         key, value = kv_ref[pl.ds(at, keys), :], kv_ref[pl.ds(at + tokens, keys), :]
         terms, dk, dv = tile(q_ref, do_ref, x_ref, key, value, base, rows)
         for rows_at, term in terms:
-            dq_ref[rows_at, :] += term
-        g_ref[k_rows, lanes] = dk.astype(g_ref.dtype)
-        g_ref[v_rows, lanes] = dv.astype(g_ref.dtype)
-
-    def block(chunk, carry):
-        distance = distances[0] if len(distances) == 1 else jnp.where(chunk == 0, *distances)
-        source = (me + sign * distance + count) % count
-        k0, k1 = span_ref[2 * source], span_ref[2 * source + 1]
-        first_row = pl.multiple_of(chunk * 2 * tokens, 2 * tokens)
-        k_rows = pl.ds(pl.multiple_of(chunk * 2 * depth, depth), depth)
-        v_rows = pl.ds(pl.multiple_of(chunk * 2 * depth + depth, depth), depth)
-        every = jnp.maximum(k0, k1) < jnp.minimum(q0, q1)
-
-        @pl.when(every)
+            dq_ref[rows_at, :] = term if store else dq_ref[rows_at, :] + term
+        g_ref[0:depth, lanes] = dk.astype(g_ref.dtype)
+        g_ref[depth : 2 * depth, lanes] = dv.astype(g_ref.dtype)
+
+    @pl.when(every)
+    def _():
+        run(0, 2 * half, first_row, tokens, pl.ds(0, tokens), store=first)
+
+    def one_span(j, carry):
+        k_id = jnp.where(j == 0, k0, k1)
+        at = pl.multiple_of(first_row + j * span, span)
+        lanes = pl.ds(pl.multiple_of(j * span, span), span)
+        a0, a1 = k_id < q0, k_id < q1
+
+        @pl.when(a0 & a1)
         def _():
-            run(0, 2 * half, first_row, tokens, k_rows, v_rows, pl.ds(0, tokens))
-
-        def one_span(j, carry):
-            k_id = jnp.where(j == 0, k0, k1)
-            at = pl.multiple_of(first_row + j * span, span)
-            lanes = pl.ds(pl.multiple_of(j * span, span), span)
-            a0, a1 = k_id < q0, k_id < q1
-
-            @pl.when(a0 & a1)
-            def _():
-                run(0, 2 * half, at, span, k_rows, v_rows, lanes)
-
-            @pl.when(a0 != a1)
-            def _():
-                run(jnp.where(a1, half, 0), half, at, span, k_rows, v_rows, lanes)
-
-            @pl.when(~(a0 | a1))
-            def _():
-                g_ref[k_rows, lanes] = jnp.zeros((depth, span), g_ref.dtype)
-                g_ref[v_rows, lanes] = jnp.zeros((depth, span), g_ref.dtype)
-
-            return carry
-
-        @pl.when(~every)
+            run(0, 2 * half, at, span, lanes)
+
+        @pl.when(a0 != a1)
         def _():
-            lax.fori_loop(0, 2, one_span, 0)
+            run(jnp.where(a1, half, 0), half, at, span, lanes)
+
+        @pl.when(~(a0 | a1))
+        def _():
+            g_ref[:, lanes] = jnp.zeros((2 * depth, span), g_ref.dtype)
 
         return carry
 
-    if len(distances) == 1:
-        block(0, 0)
-    else:
-        lax.fori_loop(0, len(distances), block, 0)
-
-
-def far(distances, spans, q, do, x, kv, dq, dtype, name):
+    @pl.when(~every)
+    def _():
+        if first:
+            dq_ref[...] = jnp.zeros_like(dq_ref)
+        lax.fori_loop(0, 2, one_span, 0)
+
+
+def far(distance, index, tokens, spans, q, do, x, kv, dq, dtype, name, after=None, weight=10):
     rows, depth = q.shape
-    chunks = len(distances)
-    tokens = kv.shape[0] // (2 * chunks)
     args = [spans, q, do, x, kv] + ([] if dq is None else [dq])
-    return pl.pallas_call(
-        functools.partial(far_kernel, distances, dq is None),
+    order = [] if after is None else [after]
+    return pl.pallas_call(
+        functools.partial(far_kernel, distance, index, dq is None),
         out_shape=[
             jax.ShapeDtypeStruct((rows, depth), F32),
-            jax.ShapeDtypeStruct((chunks * 2 * depth, tokens), dtype),
+            jax.ShapeDtypeStruct((2 * depth, tokens), dtype),
         ],
-        in_specs=[SMEM] + [VMEM] * (len(args) - 1),
+        in_specs=[SMEM] + [VMEM] * (len(args) - 1) + [pl.BlockSpec(memory_space=pl.ANY)] * len(order),
         out_specs=[VMEM, VMEM],
         input_output_aliases={} if dq is None else {5: 0},
         compiler_params=pltpu.CompilerParams(vmem_limit_bytes=24 * 2**20),
         cost_estimate=pl.CostEstimate(
-            flops=chunks * 10 * rows * tokens * depth,
-            bytes_accessed=chunks * 2**20,
-            transcendentals=chunks * rows * tokens,
+            flops=weight * rows * tokens * depth,
+            bytes_accessed=2**16,
+            transcendentals=weight * rows * tokens // 10,
         ),
         name=name,
-    )(*args)
+    )(*args, *order)
 
 
 def own_low_kernel(span_ref, q_ref, do_ref, x_ref, kv_ref, _, dq_ref, g_ref):
@@ -228,8 +212,8 @@
     low = jnp.where(span_ref[2 * me] > span_ref[2 * me + 1], 1, 0)
 
     def causal(base, rows, keys):
-        token = (base + lax.broadcasted_iota(jnp.int32, (rows, keys), 0)) // heads
-        return lax.broadcasted_iota(jnp.int32, (rows, keys), 1) <= token
+        row = lax.broadcasted_iota(jnp.int32, (rows, keys), 0)
+        return heads * lax.broadcasted_iota(jnp.int32, (rows, keys), 1) - row <= base
 
     at = pl.multiple_of(low * span, span)
     key, value = kv_ref[pl.ds(at, span), :], kv_ref[pl.ds(at + tokens, span), :]
@@ -249,11 +233,10 @@
     low = jnp.where(span_ref[2 * me] > span_ref[2 * me + 1], 1, 0)
 
     def causal(base, rows, keys):
-        token = (base + lax.broadcasted_iota(jnp.int32, (rows, keys), 0)) // heads
-        slot = lax.broadcasted_iota(jnp.int32, (rows, keys), 1)
-        return (slot - (1 - low) * span <= token) & ((slot >= span) | (low == 1)) | (
-            (slot // span) == low
-        )
+        row = lax.broadcasted_iota(jnp.int32, (rows, keys), 0)
+        slot = lax.broadcasted_iota(jnp.int32, (1, keys), 1)
+        own = (slot >= span) == (low == 0)
+        return jnp.where(own, heads * (slot & (span - 1)), -1) - row <= base
 
     terms, dk, dv = tile(
         q_ref, do_ref, x_ref, kv_ref[0:tokens, :], kv_ref[tokens : 2 * tokens, :],
@@ -267,7 +250,7 @@
     g_ref[:, lanes] += g_low_ref[...]
 
 
-def own(kernel, spans, q, do, x, kv, extra, dq, keys, name):
+def own(kernel, spans, q, do, x, kv, extra, dq, keys, name, weight):
     rows, depth = q.shape
     args = [spans, q, do, x, kv] + extra + [dq]
     return pl.pallas_call(
@@ -281,7 +264,7 @@
         input_output_aliases={len(args) - 1: 0},
         compiler_params=pltpu.CompilerParams(vmem_limit_bytes=24 * 2**20),
         cost_estimate=pl.CostEstimate(
-            flops=5 * rows * keys * depth, bytes_accessed=2**20, transcendentals=rows * keys // 2
+            flops=weight * rows * keys * depth, bytes_accessed=2**16, transcendentals=weight * rows * keys // 10
         ),
         name=name,
     )(*args)
@@ -303,20 +286,22 @@
     )(dq)
 
 
-def add_kernel(a_ref, b_ref, o_ref):
-    rows = o_ref.shape[0]
-    o_ref[...] = (a_ref[...] + b_ref[pl.ds(rows, rows), :].astype(F32)).astype(BF16)
-
-
-def add(a, b):
+def add_kernel(a_ref, b_ref, _, __, o_ref):
+    rows = a_ref.shape[0]
+    o_ref[0:rows, :] = (a_ref[...] + b_ref[...].astype(F32)).astype(BF16)
+    o_ref[rows:, :] = jnp.zeros((o_ref.shape[0] - rows, o_ref.shape[1]), BF16)
+
+
+def add(a, b, after, after_too):
+    rows, tokens = a.shape
     return pl.pallas_call(
         add_kernel,
-        out_shape=jax.ShapeDtypeStruct(a.shape, BF16),
-        in_specs=[VMEM, VMEM],
+        out_shape=jax.ShapeDtypeStruct((rows + 16, tokens), BF16),
+        in_specs=[VMEM, VMEM] + [pl.BlockSpec(memory_space=pl.ANY)] * 2,
         out_specs=VMEM,
         compiler_params=pltpu.CompilerParams(vmem_limit_bytes=8 * 2**20),
         name="add",
-    )(a, b)
+    )(a, b, after, after_too)
 
 
 def merge_kernel(own_ref, a_ref, b_ref, c_ref, keep_ref, send_ref):
@@ -329,8 +314,8 @@
         return (
             own_ref[:, lanes]
             + a_ref[:, lanes].astype(F32)
-            + b_ref[:, lanes].astype(F32)
-            + c_ref[0:rows, lanes].astype(F32)
+            + b_ref[0:rows, lanes].astype(F32)
+            + c_ref[:, lanes].astype(F32)
         )
 
     send_ref[...] = part(1 - head).astype(BF16)
@@ -417,17 +402,20 @@
     kv_b = lax.ppermute(kv, both, over_one)
     x = prep(do, out, lse)
 
-    dq, g_a = far((-2,), span_order, q, do, x, kv_a, None, BF16, "far_a")
+    args = (tokens, span_order, q, do, x)
+    dq, g_a = far(-2, 0, *args, kv_a, None, BF16, "far_a")
     kv_cd = lax.ppermute(pack(kv, kv_b, g_a), "ctx", mates)
     got_a = lax.ppermute(g_a, both, back_two)
-    dq, g_b = far((-1,), span_order, q, do, x, kv_b, dq, F32, "far_b")
-    dq, g_cd = far((1, 2), span_order, q, do, x, kv_cd, dq, BF16, "far_cd")
-    got_cd = lax.ppermute(g_cd, "ctx", mates)
-    span = tokens // 2
-    dq, g_low = own(own_low_kernel, span_order, q, do, x, kv, [], dq, span, "own_low")
-    got_b = lax.ppermute(add(g_b, got_cd), both, over_one)
-    dq, g_own = own(own_high_kernel, span_order, q, do, x, kv, [g_low], dq, tokens, "own_high")
-    keep, send = merge(g_own, got_a, got_b, got_cd)
+    dq, g_b = far(-1, 0, *args, kv_b, dq, F32, "far_b")
+    dq, g_d = far(2, 1, *args, kv_cd, dq, BF16, "far_d")
+    got_d = lax.ppermute(g_d, "ctx", mates)
+    dq, g_low = own(own_low_kernel, span_order, q, do, x, kv, [], dq, tokens // 2, "own_low", 5)
+    g_bd = add(g_b, got_d, g_low, got_a)
+    got_b = lax.ppermute(g_bd, both, over_one)
+    dq, g_c = far(1, 0, *args, kv_cd, dq, BF16, "far_c", g_bd, 1)
+    got_c = lax.ppermute(g_c, "ctx", mates)
+    dq, g_own = own(own_high_kernel, span_order, q, do, x, kv, [g_low], dq, tokens, "own_high", 1)
+    keep, send = merge(g_own, got_a, got_b, got_c)
     got = lax.ppermute(send, "head", [(0, 1), (1, 0)])
     grad_q = finish(dq)
     grad_k, grad_v = last(keep, got)

time: 71.6 us -> 67.8 us (0.947)
  the two profiles are of different devices: /device:TPU:0 before, /device:TPU:1 now
where the time goes in v4:
time: 67.8 us; the launch traced here: 67.4 us
  starting transfers between devices  42.2 us (62%)
  Pallas kernels  13.6 us (20%)
  waiting for transfers between devices  10.8 us (16%)
  between operations  0.83 us (1%)
    ppermute x1, starting transfers between devices, local(): kv_a = lax.ppermute(kv, both, over_two)  16.6 us
    ppermute x1, starting transfers between devices, local(): got_d = lax.ppermute(g_d, 'ctx', mates)  7.79 us
    ppermute x1, waiting for transfers between devices, local(): got = lax.ppermute(send, 'head', [(0, 1), (1, 0)])  6.68 us
    ppermute x1, starting transfers between devices, local(): got_c = lax.ppermute(g_c, 'ctx', mates)  5.76 us
    pallas_call x4, Pallas kernels, far(): pl.pallas_call(functools.partial(far_kernel, distance, index, dq is None)...  5.67 us
    ppermute x1, waiting for transfers between devices, local(): kv_b = lax.ppermute(kv, both, over_one)  3.67 us
    pallas_call x2, Pallas kernels, own(): pl.pallas_call(kernel, out_shape=[jax.ShapeDtypeStruct((rows, depth), F32...  3.59 us
    ppermute x1, starting transfers between devices, local(): got = lax.ppermute(send, 'head', [(0, 1), (1, 0)])  3.51 us
  transfers between devices with their start and end apart: 8, of which 3 were waited for; matrix products, arithmetic and copies ran while one was open for 0% of the time, Pallas kernels for 16%

profile of v4, /device:TPU:1, one launch (start us, length us, event | category | flops | bytes accessed | tf_op | source)
XLA Modules:
  0.0 67.4 jit_solution(10763752144254116557)
XLA Ops:
  0.6 0.0 copy-start.1
  0.6 1.5 %load.1 = (bf16[1024,128]{1,0:T(8,128)(2,1)S(1)}, bf16[2048,128]{1,0:T(8,128)(2,1)S(1)}, bf16[2048,128]{1,0:T(8,128)(2,1)S(1)}, bf16[2048,128]{1,0:T(8,128)(2,1)S(1)}) custom-call(bf16[512,128]{1,0:T(8,128)(2,1)} %k_ref.1, bf16[512,128]{1,0:T(8,128)(2,1)} %v_ref.1, bf16[2048,128]{1,0:T(8,128)(2,1)} %bitcast.4, bf16[2048,128]{1,0:T(8,128)(2,1)} %bitcast.5, ...), custom_call_target="tpu_custom_call" | custom-call | tf_op jit(solution)/shard_map/load/pallas_call | solution.py:51
  2.2 16.6 %collective-permute-start.1 = (bf16[1024,128]{1,0:T(8,128)(2,1)S(1)}, bf16[1024,128]{1,0:T(8,128)(2,1)S(1)}, u32[]{:S(2)}, u32[]{:S(2)}) collective-permute-start(bf16[1024,128]{1,0:T(8,128)(2,1)S(1)} %get-tuple-element.26.a_ref.kv_ref), channel_id=1, source_target_pairs={{0,4},{1,5},{2,511},{3,510},{4,8},{5,9},{6,2},{7,3},{8,12},{9,13},... | collective-permute-start | bytes 786440 | tf_op jit(solution)/shard_map/ppermute | solution.py:401
  18.8 1.9 %collective-permute-start = (bf16[1024,128]{1,0:T(8,128)(2,1)S(1)}, bf16[1024,128]{1,0:T(8,128)(2,1)S(1)}, u32[]{:S(2)}, u32[]{:S(2)}) collective-permute-start(bf16[1024,128]{1,0:T(8,128)(2,1)S(1)} %get-tuple-element.26.a_ref.kv_ref), channel_id=1, source_target_pairs={{0,511},{1,510},{2,4},{3,5},{4,2},{5,3},{6,8},{7,9},{8,6},{9,7},{1... | collective-permute-start | bytes 786440 | tf_op jit(solution)/shard_map/ppermute | solution.py:402
  20.7 0.0 copy-done.1
  20.7 0.0 copy-start
  20.7 0.9 %prep.1.x_ref = bf16[2048,128]{1,0:T(8,128)(2,1)S(1)} custom-call(bf16[2048,128]{1,0:T(8,128)(2,1)S(1)} %get-tuple-element.24.grad_ref.do_ref, bf16[2048,128]{1,0:T(8,128)(2,1)S(1)} %get-tuple-element.25.out_ref, f32[4,512]{1,0:T(4,128)S(1)} %copy-done.1), custom_call_target="tpu_custom_call" | custom-call | flops 2097152 | bytes 1572864 | tf_op jit(solution)/shard_map/prep/pallas_call | solution.py:87
  21.7 0.4 collective-permute-done.1.kv_ref
  22.1 0.0 copy-done
  22.1 0.7 %far_a.1 = (f32[2048,128]{1,0:T(8,128)S(1)}, bf16[256,512]{1,0:T(8,128)(2,1)S(1)}) custom-call(s32[512]{0:T(512)S(1)} %copy-done, bf16[2048,128]{1,0:T(8,128)(2,1)S(1)} %get-tuple-element.23.q_ref, bf16[2048,128]{1,0:T(8,128)(2,1)S(1)} %get-tuple-element.24.grad_ref.do_ref, bf16[2048,128]{1,0:T(8,128)(2,1)S(1)} %prep.1.x_ref, ...), custom_call_target="tpu_custom_call" | custom-call | flops 1342177280 | bytes 65536 | tf_op jit(solution)/shard_map/far_a/pallas_call | solution.py:187
  22.8 3.7 %collective-permute-done.b_ref.kv_ref = bf16[1024,128]{1,0:T(8,128)(2,1)S(1)} collective-permute-done((bf16[1024,128]{1,0:T(8,128)(2,1)S(1)}, bf16[1024,128]{1,0:T(8,128)(2,1)S(1)}, u32[]{:S(2)}, u32[]{:S(2)}) %collective-permute-start) | collective-permute-done | bytes 262176 | tf_op jit(solution)/shard_map/ppermute | solution.py:402
  26.5 2.8 %collective-permute-start.2 = (bf16[2048,128]{1,0:T(8,128)(2,1)S(1)}, bf16[2048,128]{1,0:T(8,128)(2,1)S(1)}, u32[]{:S(2)}, u32[]{:S(2)}) collective-permute-start(bf16[2048,128]{1,0:T(8,128)(2,1)S(1)} %pack.1), channel_id=1, source_target_pairs={{0,2},{2,0},{4,6},{6,4},{8,10},{10,8},{12,14},{14,12},{16,18},{18,... | collective-permute-start | bytes 1572872 | tf_op jit(solution)/shard_map/ppermute | solution.py:407
  29.3 1.9 %collective-permute-start.4 = (bf16[256,512]{1,0:T(8,128)(2,1)S(1)}, bf16[256,512]{1,0:T(8,128)(2,1)S(1)}, u32[]{:S(2)}, u32[]{:S(2)}) collective-permute-start(bf16[256,512]{1,0:T(8,128)(2,1)S(1)} %get-tuple-element.27._), channel_id=1, source_target_pairs={{4,0},{5,1},{511,2},{510,3},{8,4},{9,5},{2,6},{3,7},{12,8},{13,9},... | collective-permute-start | bytes 786440 | tf_op jit(solution)/shard_map/ppermute | solution.py:408
  31.2 0.7 %far_b.1 = (f32[2048,128]{1,0:T(8,128)S(1)}, f32[256,512]{1,0:T(8,128)S(1)}) custom-call(s32[512]{0:T(512)S(1)} %copy-done, bf16[2048,128]{1,0:T(8,128)(2,1)S(1)} %get-tuple-element.23.q_ref, bf16[2048,128]{1,0:T(8,128)(2,1)S(1)} %get-tuple-element.24.grad_ref.do_ref, bf16[2048,128]{1,0:T(8,128)(2,1)S(1)} %prep.1.x_ref, ...), custom_call_target="tpu_custom_call", output_to_operand_aliasing={{0}: (5, {})} | custom-call | flops 1342177280 | bytes 65536 | tf_op jit(solution)/shard_map/far_b/pallas_call | solution.py:187
  31.9 0.0 collective-permute-done.2.kv_ref
  31.9 2.2 %far_d.1 = (f32[2048,128]{1,0:T(8,128)S(1)}, bf16[256,512]{1,0:T(8,128)(2,1)S(1)}) custom-call(s32[512]{0:T(512)S(1)} %copy-done, bf16[2048,128]{1,0:T(8,128)(2,1)S(1)} %get-tuple-element.23.q_ref, bf16[2048,128]{1,0:T(8,128)(2,1)S(1)} %get-tuple-element.24.grad_ref.do_ref, bf16[2048,128]{1,0:T(8,128)(2,1)S(1)} %prep.1.x_ref, ...), custom_call_target="tpu_custom_call", output_to_operand_aliasing={{0}: (5, {})} | custom-call | flops 1342177280 | bytes 65536 | tf_op jit(solution)/shard_map/far_d/pallas_call | solution.py:187
  34.2 7.8 %collective-permute-start.3 = (bf16[256,512]{1,0:T(8,128)(2,1)S(1)}, bf16[256,512]{1,0:T(8,128)(2,1)S(1)}, u32[]{:S(2)}, u32[]{:S(2)}) collective-permute-start(bf16[256,512]{1,0:T(8,128)(2,1)S(1)} %get-tuple-element.34), channel_id=1, source_target_pairs={{0,2},{2,0},{4,6},{6,4},{8,10},{10,8},{12,14},{14,12},{16,18},{18,... | collective-permute-start | bytes 786440 | tf_op jit(solution)/shard_map/ppermute | solution.py:411
  42.0 1.4 %own_low.1 = (f32[2048,128]{1,0:T(8,128)S(1)}, f32[256,256]{1,0:T(8,128)S(1)}) custom-call(s32[512]{0:T(512)S(1)} %copy-done, bf16[2048,128]{1,0:T(8,128)(2,1)S(1)} %get-tuple-element.23.q_ref, bf16[2048,128]{1,0:T(8,128)(2,1)S(1)} %get-tuple-element.24.grad_ref.do_ref, bf16[2048,128]{1,0:T(8,128)(2,1)S(1)} %prep.1.x_ref, ...), custom_call_target="tpu_custom_call", output_to_operand_aliasing={{0}: (5, {})} | custom-call | flops 335544320 | bytes 65536 | tf_op jit(solution)/shard_map/own_low/pallas_call | solution.py:256
  43.3 0.0 collective-permute-done.4.__.a_ref
  43.3 0.0 collective-permute-done.3.b_ref
  43.3 0.1 add.1.refs_1_
  43.4 1.9 %collective-permute-start.5 = (bf16[272,512]{1,0:T(8,128)(2,1)S(1)}, bf16[272,512]{1,0:T(8,128)(2,1)S(1)}, u32[]{:S(2)}, u32[]{:S(2)}) collective-permute-start(bf16[272,512]{1,0:T(8,128)(2,1)S(1)} %add.1.refs_1_), channel_id=1, source_target_pairs={{0,511},{1,510},{2,4},{3,5},{4,2},{5,3},{6,8},{7,9},{8,6},{9,7},{1... | collective-permute-start | bytes 835592 | tf_op jit(solution)/shard_map/ppermute | solution.py:414
  45.3 2.0 %far_c.1 = (f32[2048,128]{1,0:T(8,128)S(1)}, bf16[256,512]{1,0:T(8,128)(2,1)S(1)}) custom-call(s32[512]{0:T(512)S(1)} %copy-done, bf16[2048,128]{1,0:T(8,128)(2,1)S(1)} %get-tuple-element.23.q_ref, bf16[2048,128]{1,0:T(8,128)(2,1)S(1)} %get-tuple-element.24.grad_ref.do_ref, bf16[2048,128]{1,0:T(8,128)(2,1)S(1)} %prep.1.x_ref, ...), custom_call_target="tpu_custom_call", output_to_operand_aliasing={{0}: (5, {})} | custom-call | flops 134217728 | bytes 65536 | tf_op jit(solution)/shard_map/far_c/pallas_call | solution.py:187
  47.4 5.8 %collective-permute-start.6 = (bf16[256,512]{1,0:T(8,128)(2,1)S(1)}, bf16[256,512]{1,0:T(8,128)(2,1)S(1)}, u32[]{:S(2)}, u32[]{:S(2)}) collective-permute-start(bf16[256,512]{1,0:T(8,128)(2,1)S(1)} %get-tuple-element.38), channel_id=1, source_target_pairs={{0,2},{2,0},{4,6},{6,4},{8,10},{10,8},{12,14},{14,12},{16,18},{18,... | collective-permute-start | bytes 786440 | tf_op jit(solution)/shard_map/ppermute | solution.py:416
  53.2 2.2 %own_high.1 = (f32[2048,128]{1,0:T(8,128)S(1)}, f32[256,512]{1,0:T(8,128)S(1)}) custom-call(s32[512]{0:T(512)S(1)} %copy-done, bf16[2048,128]{1,0:T(8,128)(2,1)S(1)} %get-tuple-element.23.q_ref, bf16[2048,128]{1,0:T(8,128)(2,1)S(1)} %get-tuple-element.24.grad_ref.do_ref, bf16[2048,128]{1,0:T(8,128)(2,1)S(1)} %prep.1.x_ref, ...), custom_call_target="tpu_custom_call", output_to_operand_aliasing={{0}: (6, {})} | custom-call | flops 134217728 | bytes 65536 | tf_op jit(solution)/shard_map/own_high/pallas_call | solution.py:256
  55.4 0.0 collective-permute-done.6.c_ref
  55.4 0.0 collective-permute-done.5.b_ref
  55.4 0.1 merge.1
  55.6 3.5 %collective-permute-start.7 = (bf16[256,256]{1,0:T(8,128)(2,1)S(1)}, bf16[256,256]{1,0:T(8,128)(2,1)S(1)}, u32[]{:S(2)}, u32[]{:S(2)}) collective-permute-start(bf16[256,256]{1,0:T(8,128)(2,1)S(1)} %get-tuple-element.40), channel_id=1, source_target_pairs={{0,1},{1,0},{2,3},{3,2},{4,5},{5,4},{6,7},{7,6},{8,9},{9,8},{10,11... | collective-permute-start | bytes 393224 | tf_op jit(solution)/shard_map/ppermute | solution.py:419
  59.1 0.9 %finish.1 = bf16[2048,128]{1,0:T(8,128)(2,1)} custom-call(f32[2048,128]{1,0:T(8,128)S(1)} %get-tuple-element.36.dq_ref), custom_call_target="tpu_custom_call" | custom-call | flops 262144 | bytes 1572864 | tf_op jit(solution)/shard_map/finish/pallas_call | solution.py:278
  60.0 6.7 %collective-permute-done.7.got_ref = bf16[256,256]{1,0:T(8,128)(2,1)S(1)} collective-permute-done((bf16[256,256]{1,0:T(8,128)(2,1)S(1)}, bf16[256,256]{1,0:T(8,128)(2,1)S(1)}, u32[]{:S(2)}, u32[]{:S(2)}) %collective-permute-start.7) | collective-permute-done | bytes 131104 | tf_op jit(solution)/shard_map/ppermute | solution.py:419
  66.6 0.8 %last.1 = (bf16[256,128]{1,0:T(8,128)(2,1)}, bf16[256,128]{1,0:T(8,128)(2,1)}) custom-call(f32[256,256]{1,0:T(8,128)S(1)} %get-tuple-element.39.keep_ref, bf16[256,256]{1,0:T(8,128)(2,1)S(1)} %collective-permute-done.7.got_ref), custom_call_target="tpu_custom_call" | custom-call | tf_op jit(solution)/shard_map/last/pallas_call | solution.py:350
  (1 shorter events, 0.0 us)
Async XLA Ops:
  0.6 20.1 %copy-start.1 = (f32[4,512]{1,0:T(4,128)S(1)}, f32[4,512]{1,0:T(4,128)}, u32[]{:S(2)}) copy-start(f32[4,512]{1,0:T(4,128)} %lse_ref.1) | copy-start | bytes 24580
  2.2 19.9 %collective-permute-start.1 = (bf16[1024,128]{1,0:T(8,128)(2,1)S(1)}, bf16[1024,128]{1,0:T(8,128)(2,1)S(1)}, u32[]{:S(2)}, u32[]{:S(2)}) collective-permute-start(bf16[1024,128]{1,0:T(8,128)(2,1)S(1)} %get-tuple-element.26.a_ref.kv_ref), channel_id=1, source_target_pairs={{0,4},{1,5},{2,511},{3,510},{4,8},{5,9},{6,2},{7,3},{8,12},{9,13},... | collective-permute-start | bytes 786440 | tf_op jit(solution)/shard_map/ppermute | solution.py:401
  18.8 7.7 %collective-permute-start = (bf16[1024,128]{1,0:T(8,128)(2,1)S(1)}, bf16[1024,128]{1,0:T(8,128)(2,1)S(1)}, u32[]{:S(2)}, u32[]{:S(2)}) collective-permute-start(bf16[1024,128]{1,0:T(8,128)(2,1)S(1)} %get-tuple-element.26.a_ref.kv_ref), channel_id=1, source_target_pairs={{0,511},{1,510},{2,4},{3,5},{4,2},{5,3},{6,8},{7,9},{8,6},{9,7},{1... | collective-permute-start | bytes 786440 | tf_op jit(solution)/shard_map/ppermute | solution.py:402
  20.7 1.4 %copy-start = (s32[512]{0:T(512)S(1)}, s32[512]{0:T(512)}, u32[]{:S(2)}) copy-start(s32[512]{0:T(512)} %span_ref.11) | copy-start | bytes 6148
  26.5 5.4 %collective-permute-start.2 = (bf16[2048,128]{1,0:T(8,128)(2,1)S(1)}, bf16[2048,128]{1,0:T(8,128)(2,1)S(1)}, u32[]{:S(2)}, u32[]{:S(2)}) collective-permute-start(bf16[2048,128]{1,0:T(8,128)(2,1)S(1)} %pack.1), channel_id=1, source_target_pairs={{0,2},{2,0},{4,6},{6,4},{8,10},{10,8},{12,14},{14,12},{16,18},{18,... | collective-permute-start | bytes 1572872 | tf_op jit(solution)/shard_map/ppermute | solution.py:407
  29.3 14.0 %collective-permute-start.4 = (bf16[256,512]{1,0:T(8,128)(2,1)S(1)}, bf16[256,512]{1,0:T(8,128)(2,1)S(1)}, u32[]{:S(2)}, u32[]{:S(2)}) collective-permute-start(bf16[256,512]{1,0:T(8,128)(2,1)S(1)} %get-tuple-element.27._), channel_id=1, source_target_pairs={{4,0},{5,1},{511,2},{510,3},{8,4},{9,5},{2,6},{3,7},{12,8},{13,9},... | collective-permute-start | bytes 786440 | tf_op jit(solution)/shard_map/ppermute | solution.py:408
  34.2 9.2 %collective-permute-start.3 = (bf16[256,512]{1,0:T(8,128)(2,1)S(1)}, bf16[256,512]{1,0:T(8,128)(2,1)S(1)}, u32[]{:S(2)}, u32[]{:S(2)}) collective-permute-start(bf16[256,512]{1,0:T(8,128)(2,1)S(1)} %get-tuple-element.34), channel_id=1, source_target_pairs={{0,2},{2,0},{4,6},{6,4},{8,10},{10,8},{12,14},{14,12},{16,18},{18,... | collective-permute-start | bytes 786440 | tf_op jit(solution)/shard_map/ppermute | solution.py:411
  43.4 12.0 %collective-permute-start.5 = (bf16[272,512]{1,0:T(8,128)(2,1)S(1)}, bf16[272,512]{1,0:T(8,128)(2,1)S(1)}, u32[]{:S(2)}, u32[]{:S(2)}) collective-permute-start(bf16[272,512]{1,0:T(8,128)(2,1)S(1)} %add.1.refs_1_), channel_id=1, source_target_pairs={{0,511},{1,510},{2,4},{3,5},{4,2},{5,3},{6,8},{7,9},{8,6},{9,7},{1... | collective-permute-start | bytes 835592 | tf_op jit(solution)/shard_map/ppermute | solution.py:414
  47.4 8.0 %collective-permute-start.6 = (bf16[256,512]{1,0:T(8,128)(2,1)S(1)}, bf16[256,512]{1,0:T(8,128)(2,1)S(1)}, u32[]{:S(2)}, u32[]{:S(2)}) collective-permute-start(bf16[256,512]{1,0:T(8,128)(2,1)S(1)} %get-tuple-element.38), channel_id=1, source_target_pairs={{0,2},{2,0},{4,6},{6,4},{8,10},{10,8},{12,14},{14,12},{16,18},{18,... | collective-permute-start | bytes 786440 | tf_op jit(solution)/shard_map/ppermute | solution.py:416
  55.6 11.1 %collective-permute-start.7 = (bf16[256,256]{1,0:T(8,128)(2,1)S(1)}, bf16[256,256]{1,0:T(8,128)(2,1)S(1)}, u32[]{:S(2)}, u32[]{:S(2)}) collective-permute-start(bf16[256,256]{1,0:T(8,128)(2,1)S(1)} %get-tuple-element.40), channel_id=1, source_target_pairs={{0,1},{1,0},{2,3},{3,2},{4,5},{5,4},{6,7},{7,6},{8,9},{9,8},{10,11... | collective-permute-start | bytes 393224 | tf_op jit(solution)/shard_map/ppermute | solution.py:419

commit v5 on v3

--- a/solution.py
+++ b/solution.py
@@ -11,6 +11,7 @@
 BF16 = jnp.bfloat16
 LOG2E = 1.4426950408889634
 SUB = 512
+DISTANCES = (-2, -1, 1, 2)
 VMEM = pl.BlockSpec(memory_space=pltpu.VMEM)
 SMEM = pl.BlockSpec(memory_space=pltpu.SMEM)
 
@@ -47,6 +48,7 @@
 def load(keys, values, q, do, out):
     rows, depth = keys.shape
     wide = jax.ShapeDtypeStruct(q.shape, q.dtype)
+    args = [pltpu.with_memory_space_constraint(a, pltpu.HBM) for a in (keys, values, q, do, out)]
     return pl.pallas_call(
         load_kernel,
         out_shape=[jax.ShapeDtypeStruct((2 * rows, depth), keys.dtype)] + [wide] * 3,
@@ -55,10 +57,24 @@
         scratch_shapes=[pltpu.SemaphoreType.DMA((5,))],
         compiler_params=pltpu.CompilerParams(vmem_limit_bytes=8 * 2**20),
         name="load",
-    )(keys, values, q, do, out)
-
-
-def prep_kernel(grad_ref, out_ref, lse_ref, extra_ref, wide):
+    )(*args)
+
+
+def prep_kernel(span_ref, grad_ref, out_ref, lse_ref, extra_ref, code_ref, wide):
+    count = lax.axis_size("ctx")
+    me = lax.axis_index("ctx")
+    sign = 1 - 2 * (me % 2)
+    q0, q1 = span_ref[2 * me], span_ref[2 * me + 1]
+    row = lax.broadcasted_iota(jnp.int32, code_ref.shape, 0)
+    codes = jnp.where(row == len(DISTANCES), jnp.where(q0 > q1, 1.0, 0.0), 0.0)
+    for r, distance in enumerate(DISTANCES):
+        source = (me + sign * distance + count) % count
+        k0, k1 = span_ref[2 * source], span_ref[2 * source + 1]
+        code = 0.0
+        for bit, allowed in enumerate((k0 < q0, k0 < q1, k1 < q0, k1 < q1)):
+            code = code + jnp.where(allowed, float(2**bit), 0.0)
+        codes = jnp.where(row == r, code, codes)
+    code_ref[...] = codes
     heads, tokens = lse_ref.shape
     depth = grad_ref.shape[1]
     lse = lse_ref[...] * float(depth**0.5)
@@ -81,18 +97,25 @@
     extra_ref[...] = jnp.where(lane < 6, -term, 0.0).astype(BF16)
 
 
-def prep(grad_rows, out_rows, lse):
+def read_code(code_ref, row):
+    return jnp.max(code_ref[pl.ds(row, 1), :]).astype(jnp.int32)
+
+
+def prep(spans, grad_rows, out_rows, lse):
     rows, depth = grad_rows.shape
     return pl.pallas_call(
         prep_kernel,
-        out_shape=jax.ShapeDtypeStruct((rows, 128), BF16),
-        in_specs=[VMEM] * 3,
-        out_specs=VMEM,
+        out_shape=[
+            jax.ShapeDtypeStruct((rows, 128), BF16),
+            jax.ShapeDtypeStruct((8, 128), F32),
+        ],
+        in_specs=[SMEM] + [VMEM] * 3,
+        out_specs=[VMEM] * 2,
         scratch_shapes=[pltpu.VMEM((rows, 128), F32)],
         compiler_params=pltpu.CompilerParams(vmem_limit_bytes=16 * 2**20),
         cost_estimate=pl.CostEstimate(flops=rows * 1024, bytes_accessed=rows * 768, transcendentals=0),
         name="prep",
-    )(grad_rows, out_rows, lse)
+    )(spans, grad_rows, out_rows, lse)
 
 
 def tile(q_ref, do_ref, x_ref, key, value, q_base, rows, mask=None):
@@ -126,47 +149,37 @@
     return terms, dk, dv
 
 
-def far_kernel(distances, first, span_ref, q_ref, do_ref, x_ref, kv_ref, *refs):
-    if first:
-        dq_ref, g_ref = refs
-        dq_ref[...] = jnp.zeros_like(dq_ref)
-    else:
-        _, dq_ref, g_ref = refs
-    count = lax.axis_size("ctx")
-    me = lax.axis_index("ctx")
-    sign = 1 - 2 * (me % 2)
+def far_kernel(first_code, chunks, first, code_ref, q_ref, do_ref, x_ref, kv_ref, *refs):
+    dq_ref, g_ref = refs if first else refs[1:]
     depth = q_ref.shape[1]
-    tokens = kv_ref.shape[0] // (2 * len(distances))
+    tokens = kv_ref.shape[0] // (2 * chunks)
     span = tokens // 2
     half = q_ref.shape[0] // 2
-    q0, q1 = span_ref[2 * me], span_ref[2 * me + 1]
-
-    def run(base, rows, at, keys, k_rows, v_rows, lanes):
+
+    def run(base, rows, at, keys, k_rows, v_rows, lanes, store=False):
         key, value = kv_ref[pl.ds(at, keys), :], kv_ref[pl.ds(at + tokens, keys), :]
         terms, dk, dv = tile(q_ref, do_ref, x_ref, key, value, base, rows)
         for rows_at, term in terms:
-            dq_ref[rows_at, :] += term
+            dq_ref[rows_at, :] = term if store else dq_ref[rows_at, :] + term
         g_ref[k_rows, lanes] = dk.astype(g_ref.dtype)
         g_ref[v_rows, lanes] = dv.astype(g_ref.dtype)
 
     def block(chunk, carry):
-        distance = distances[0] if len(distances) == 1 else jnp.where(chunk == 0, *distances)
-        source = (me + sign * distance + count) % count
-        k0, k1 = span_ref[2 * source], span_ref[2 * source + 1]
+        code = read_code(code_ref, first_code + chunk)
         first_row = pl.multiple_of(chunk * 2 * tokens, 2 * tokens)
         k_rows = pl.ds(pl.multiple_of(chunk * 2 * depth, depth), depth)
         v_rows = pl.ds(pl.multiple_of(chunk * 2 * depth + depth, depth), depth)
-        every = jnp.maximum(k0, k1) < jnp.minimum(q0, q1)
+        every = code == 15
 
         @pl.when(every)
         def _():
-            run(0, 2 * half, first_row, tokens, k_rows, v_rows, pl.ds(0, tokens))
+            run(0, 2 * half, first_row, tokens, k_rows, v_rows, pl.ds(0, tokens), store=first)
 
         def one_span(j, carry):
-            k_id = jnp.where(j == 0, k0, k1)
+            bits = jnp.where(j == 0, code, code // 4)
             at = pl.multiple_of(first_row + j * span, span)
             lanes = pl.ds(pl.multiple_of(j * span, span), span)
-            a0, a1 = k_id < q0, k_id < q1
+            a0, a1 = bits % 2 == 1, (bits // 2) % 2 == 1
 
             @pl.when(a0 & a1)
             def _():
@@ -185,28 +198,29 @@
 
         @pl.when(~every)
         def _():
+            if first:
+                dq_ref[...] = jnp.zeros_like(dq_ref)
             lax.fori_loop(0, 2, one_span, 0)
 
         return carry
 
-    if len(distances) == 1:
+    if chunks == 1:
         block(0, 0)
     else:
-        lax.fori_loop(0, len(distances), block, 0)
-
-
-def far(distances, spans, q, do, x, kv, dq, dtype, name):
+        lax.fori_loop(0, chunks, block, 0)
+
+
+def far(first_code, chunks, codes, q, do, x, kv, dq, dtype, name):
     rows, depth = q.shape
-    chunks = len(distances)
     tokens = kv.shape[0] // (2 * chunks)
-    args = [spans, q, do, x, kv] + ([] if dq is None else [dq])
-    return pl.pallas_call(
-        functools.partial(far_kernel, distances, dq is None),
+    args = [codes, q, do, x, kv] + ([] if dq is None else [dq])
+    return pl.pallas_call(
+        functools.partial(far_kernel, first_code, chunks, dq is None),
         out_shape=[
             jax.ShapeDtypeStruct((rows, depth), F32),
             jax.ShapeDtypeStruct((chunks * 2 * depth, tokens), dtype),
         ],
-        in_specs=[SMEM] + [VMEM] * (len(args) - 1),
+        in_specs=[VMEM] * len(args),
         out_specs=[VMEM, VMEM],
         input_output_aliases={} if dq is None else {5: 0},
         compiler_params=pltpu.CompilerParams(vmem_limit_bytes=24 * 2**20),
@@ -219,17 +233,16 @@
     )(*args)
 
 
-def own_low_kernel(span_ref, q_ref, do_ref, x_ref, kv_ref, _, dq_ref, g_ref):
-    me = lax.axis_index("ctx")
+def own_low_kernel(code_ref, q_ref, do_ref, x_ref, kv_ref, _, dq_ref, g_ref):
     depth = q_ref.shape[1]
     tokens = kv_ref.shape[0] // 2
     span, half = tokens // 2, q_ref.shape[0] // 2
     heads = half // span
-    low = jnp.where(span_ref[2 * me] > span_ref[2 * me + 1], 1, 0)
+    low = read_code(code_ref, len(DISTANCES))
 
     def causal(base, rows, keys):
-        token = (base + lax.broadcasted_iota(jnp.int32, (rows, keys), 0)) // heads
-        return lax.broadcasted_iota(jnp.int32, (rows, keys), 1) <= token
+        row = lax.broadcasted_iota(jnp.int32, (rows, keys), 0)
+        return heads * lax.broadcasted_iota(jnp.int32, (rows, keys), 1) - row <= base
 
     at = pl.multiple_of(low * span, span)
     key, value = kv_ref[pl.ds(at, span), :], kv_ref[pl.ds(at + tokens, span), :]
@@ -240,20 +253,18 @@
     g_ref[depth : 2 * depth, :] = dv
 
 
-def own_high_kernel(span_ref, q_ref, do_ref, x_ref, kv_ref, g_low_ref, _, dq_ref, g_ref):
-    me = lax.axis_index("ctx")
+def own_high_kernel(code_ref, q_ref, do_ref, x_ref, kv_ref, g_low_ref, _, dq_ref, g_ref):
     depth = q_ref.shape[1]
     tokens = kv_ref.shape[0] // 2
     span, half = tokens // 2, q_ref.shape[0] // 2
     heads = half // span
-    low = jnp.where(span_ref[2 * me] > span_ref[2 * me + 1], 1, 0)
+    low = read_code(code_ref, len(DISTANCES))
 
     def causal(base, rows, keys):
-        token = (base + lax.broadcasted_iota(jnp.int32, (rows, keys), 0)) // heads
-        slot = lax.broadcasted_iota(jnp.int32, (rows, keys), 1)
-        return (slot - (1 - low) * span <= token) & ((slot >= span) | (low == 1)) | (
-            (slot // span) == low
-        )
+        row = lax.broadcasted_iota(jnp.int32, (rows, keys), 0)
+        slot = lax.broadcasted_iota(jnp.int32, (1, keys), 1)
+        own = (slot >= span) == (low == 0)
+        return jnp.where(own, heads * (slot & (span - 1)), -1) - row <= base
 
     terms, dk, dv = tile(
         q_ref, do_ref, x_ref, kv_ref[0:tokens, :], kv_ref[tokens : 2 * tokens, :],
@@ -267,16 +278,16 @@
     g_ref[:, lanes] += g_low_ref[...]
 
 
-def own(kernel, spans, q, do, x, kv, extra, dq, keys, name):
+def own(kernel, codes, q, do, x, kv, extra, dq, keys, name):
     rows, depth = q.shape
-    args = [spans, q, do, x, kv] + extra + [dq]
+    args = [codes, q, do, x, kv] + extra + [dq]
     return pl.pallas_call(
         kernel,
         out_shape=[
             jax.ShapeDtypeStruct((rows, depth), F32),
             jax.ShapeDtypeStruct((2 * depth, keys), F32),
         ],
-        in_specs=[SMEM] + [VMEM] * (len(args) - 1),
+        in_specs=[VMEM] * len(args),
         out_specs=[VMEM, VMEM],
         input_output_aliases={len(args) - 1: 0},
         compiler_params=pltpu.CompilerParams(vmem_limit_bytes=24 * 2**20),
@@ -353,7 +364,7 @@
 
 
 def last_kernel(keep_ref, got_ref, dk_ref, dv_ref):
-    total = keep_ref[...] + got_ref[...].astype(F32)
+    total = keep_ref[...] + got_ref[1 - lax.axis_index("head")].astype(F32)
     depth = total.shape[0] // 2
     dk_ref[...] = (total[:depth].T * float(depth**-0.5)).astype(BF16)
     dv_ref[...] = total[depth:].T.astype(BF16)
@@ -415,20 +426,20 @@
     kv, q, do, out = load(keys, values, q, do, out)
     kv_a = lax.ppermute(kv, both, over_two)
     kv_b = lax.ppermute(kv, both, over_one)
-    x = prep(do, out, lse)
-
-    dq, g_a = far((-2,), span_order, q, do, x, kv_a, None, BF16, "far_a")
+    x, codes = prep(span_order, do, out, lse)
+
+    dq, g_a = far(0, 1, codes, q, do, x, kv_a, None, BF16, "far_a")
     kv_cd = lax.ppermute(pack(kv, kv_b, g_a), "ctx", mates)
     got_a = lax.ppermute(g_a, both, back_two)
-    dq, g_b = far((-1,), span_order, q, do, x, kv_b, dq, F32, "far_b")
-    dq, g_cd = far((1, 2), span_order, q, do, x, kv_cd, dq, BF16, "far_cd")
+    dq, g_b = far(1, 1, codes, q, do, x, kv_b, dq, F32, "far_b")
+    dq, g_cd = far(2, 2, codes, q, do, x, kv_cd, dq, BF16, "far_cd")
     got_cd = lax.ppermute(g_cd, "ctx", mates)
     span = tokens // 2
-    dq, g_low = own(own_low_kernel, span_order, q, do, x, kv, [], dq, span, "own_low")
+    dq, g_low = own(own_low_kernel, codes, q, do, x, kv, [], dq, span, "own_low")
     got_b = lax.ppermute(add(g_b, got_cd), both, over_one)
-    dq, g_own = own(own_high_kernel, span_order, q, do, x, kv, [g_low], dq, tokens, "own_high")
+    dq, g_own = own(own_high_kernel, codes, q, do, x, kv, [g_low], dq, tokens, "own_high")
     keep, send = merge(g_own, got_a, got_b, got_cd)
-    got = lax.ppermute(send, "head", [(0, 1), (1, 0)])
+    got = lax.all_gather(send, "head")
     grad_q = finish(dq)
     grad_k, grad_v = last(keep, got)
     return grad_q.reshape(tokens, heads, depth), grad_k, grad_v

time: 71.6 us -> 65 us (0.908)
  waiting for transfers between devices: 20.2 us -> 9.67 us
  blocking collectives: 0 us -> 9.55 us
  local copies, waits for them, and re-layouts: 4.93 us -> 0.01 us
  starting transfers between devices: 31.8 us -> 27.5 us
  Pallas kernels: 13.4 us -> 17.2 us
    all_gather x0 -> x1, blocking collectives: none -> 9.55 us  [local(): got = lax.all_gather(send, 'head')]
    ppermute x1 -> x0, waiting for transfers between devices: 7.64 us -> none  [local(): got = lax.ppermute(send, 'head', [(0, 1), (1, 0)])]
    unnamed x14 -> x4, local copies, waits for them, and re-layouts: 4.93 us -> 0.01 us
    pallas_call x4, Pallas kernels: 7.04 us -> 11.2 us  [the longest x3 9.74 us: far(): pl.pallas_call(functools.partial(far_kernel, first_code, chunks, dq is No...]
    ppermute x1 -> x0, starting transfers between devices: 2.25 us -> none  [local(): got = lax.ppermute(send, 'head', [(0, 1), (1, 0)])]
    ppermute x1, starting transfers between devices: 9.31 us -> 7.33 us  [local(): got_a = lax.ppermute(g_a, both, back_two)]
    ppermute x1, starting transfers between devices: 3.85 us -> 1.92 us  [local(): got_cd = lax.ppermute(g_cd, 'ctx', mates)]
    ppermute x1, starting transfers between devices: 1.92 us -> 3.76 us  [local(): got_b = lax.ppermute(add(g_b, got_cd), both, over_one)]
  transfers between devices with their start and end apart: 7 -> 6, of which waited for: 4 -> 3; matrix products, arithmetic and copies ran while one was open for 0% -> 0% of each run, Pallas kernels for 12% -> 15%
where the time goes in v5:
time: 65 us; the launch traced here: 64.7 us
  starting transfers between devices  27.5 us (42%)
  Pallas kernels  17.2 us (26%)
  waiting for transfers between devices  9.67 us (15%)
  blocking collectives  9.55 us (15%)
  between operations  0.8 us (1%)
    ppermute x1, starting transfers between devices, local(): kv_b = lax.ppermute(kv, both, over_one)  10.7 us
    pallas_call x3, Pallas kernels, far(): pl.pallas_call(functools.partial(far_kernel, first_code, chunks, dq is No...  9.74 us
    all_gather x1, blocking collectives, local(): got = lax.all_gather(send, 'head')  9.55 us
    ppermute x1, waiting for transfers between devices, local(): got_b = lax.ppermute(add(g_b, got_cd), both, over_one)  7.53 us
    ppermute x1, starting transfers between devices, local(): got_a = lax.ppermute(g_a, both, back_two)  7.33 us
    ppermute x1, starting transfers between devices, local(): got_b = lax.ppermute(add(g_b, got_cd), both, over_one)  3.76 us
    pallas_call x2, Pallas kernels, own(): pl.pallas_call(kernel, out_shape=[jax.ShapeDtypeStruct((rows, depth), F32...  2.57 us
    ppermute x1, waiting for transfers between devices, local(): kv_a = lax.ppermute(kv, both, over_two)  2.06 us
  transfers between devices with their start and end apart: 6, of which 3 were waited for; matrix products, arithmetic and copies ran while one was open for 0% of the time, Pallas kernels for 15%

profile of v5, /device:TPU:0, one launch (start us, length us, event | category | flops | bytes accessed | tf_op | source)
XLA Modules:
  0.0 64.7 jit_solution(18426764630362499252)
XLA Ops:
  0.6 0.0 copy-start
  0.6 1.5 %load.1 = (bf16[1024,128]{1,0:T(8,128)(2,1)S(1)}, bf16[2048,128]{1,0:T(8,128)(2,1)S(1)}, bf16[2048,128]{1,0:T(8,128)(2,1)S(1)}, bf16[2048,128]{1,0:T(8,128)(2,1)S(1)}) custom-call(bf16[512,128]{1,0:T(8,128)(2,1)} %k_ref.1, bf16[512,128]{1,0:T(8,128)(2,1)} %v_ref.1, bf16[2048,128]{1,0:T(8,128)(2,1)} %bitcast.6, bf16[2048,128]{1,0:T(8,128)(2,1)} %bitcast.7, ...), custom_call_target="tpu_custom_call" | custom-call | tf_op jit(solution)/shard_map/load/pallas_call | solution.py:52
  2.2 0.0 copy-start.1
  2.2 1.9 %collective-permute-start.1 = (bf16[1024,128]{1,0:T(8,128)(2,1)S(1)}, bf16[1024,128]{1,0:T(8,128)(2,1)S(1)}, u32[]{:S(2)}, u32[]{:S(2)}) collective-permute-start(bf16[1024,128]{1,0:T(8,128)(2,1)S(1)} %get-tuple-element.28.a_ref.kv_ref), channel_id=1, source_target_pairs={{0,4},{1,5},{2,511},{3,510},{4,8},{5,9},{6,2},{7,3},{8,12},{9,13},... | collective-permute-start | bytes 786440 | tf_op jit(solution)/shard_map/ppermute | solution.py:427
  4.1 10.7 %collective-permute-start = (bf16[1024,128]{1,0:T(8,128)(2,1)S(1)}, bf16[1024,128]{1,0:T(8,128)(2,1)S(1)}, u32[]{:S(2)}, u32[]{:S(2)}) collective-permute-start(bf16[1024,128]{1,0:T(8,128)(2,1)S(1)} %get-tuple-element.28.a_ref.kv_ref), channel_id=1, source_target_pairs={{0,511},{1,510},{2,4},{3,5},{4,2},{5,3},{6,8},{7,9},{8,6},{9,7},{1... | collective-permute-start | bytes 786440 | tf_op jit(solution)/shard_map/ppermute | solution.py:428
  14.8 0.0 copy-done
  14.8 0.0 copy-done.1
  14.8 1.5 %prep.1 = (bf16[2048,128]{1,0:T(8,128)(2,1)S(1)}, f32[8,128]{1,0:T(8,128)S(1)}) custom-call(s32[512]{0:T(512)S(1)} %copy-done.1, bf16[2048,128]{1,0:T(8,128)(2,1)S(1)} %get-tuple-element.23.grad_ref.do_ref, bf16[2048,128]{1,0:T(8,128)(2,1)S(1)} %get-tuple-element.24.out_ref, f32[4,512]{1,0:T(4,128)S(1)} %copy-done), custom_call_target="tpu_custom_call" | custom-call | flops 2097152 | bytes 1572864 | tf_op jit(solution)/shard_map/prep/pallas_call | solution.py:106
  16.3 2.1 %collective-permute-done.1.kv_ref = bf16[1024,128]{1,0:T(8,128)(2,1)S(1)} collective-permute-done((bf16[1024,128]{1,0:T(8,128)(2,1)S(1)}, bf16[1024,128]{1,0:T(8,128)(2,1)S(1)}, u32[]{:S(2)}, u32[]{:S(2)}) %collective-permute-start.1) | collective-permute-done | bytes 262176 | tf_op jit(solution)/shard_map/ppermute | solution.py:427
  18.4 2.6 %far_a.1 = (f32[2048,128]{1,0:T(8,128)S(1)}, bf16[256,512]{1,0:T(8,128)(2,1)S(1)}) custom-call(f32[8,128]{1,0:T(8,128)S(1)} %get-tuple-element.25.code_ref, bf16[2048,128]{1,0:T(8,128)(2,1)S(1)} %get-tuple-element.26.q_ref, bf16[2048,128]{1,0:T(8,128)(2,1)S(1)} %get-tuple-element.23.grad_ref.do_ref, bf16[2048,128]{1,0:T(8,128)(2,1)S(1)} %get-tuple-element.27.x_ref, ...), custom_call_target="tpu_custom_call" | custom-call | flops 1342177280 | bytes 1048576 | tf_op jit(solution)/shard_map/far_a/pallas_call | solution.py:217
  21.0 0.0 collective-permute-done.b_ref.kv_ref
  21.0 1.9 %collective-permute-start.2 = (bf16[2048,128]{1,0:T(8,128)(2,1)S(1)}, bf16[2048,128]{1,0:T(8,128)(2,1)S(1)}, u32[]{:S(2)}, u32[]{:S(2)}) collective-permute-start(bf16[2048,128]{1,0:T(8,128)(2,1)S(1)} %pack.1), channel_id=1, source_target_pairs={{0,2},{2,0},{4,6},{6,4},{8,10},{10,8},{12,14},{14,12},{16,18},{18,... | collective-permute-start | bytes 1572872 | tf_op jit(solution)/shard_map/ppermute | solution.py:432
  23.0 1.8 %far_b.1 = (f32[2048,128]{1,0:T(8,128)S(1)}, f32[256,512]{1,0:T(8,128)S(1)}) custom-call(f32[8,128]{1,0:T(8,128)S(1)} %get-tuple-element.25.code_ref, bf16[2048,128]{1,0:T(8,128)(2,1)S(1)} %get-tuple-element.26.q_ref, bf16[2048,128]{1,0:T(8,128)(2,1)S(1)} %get-tuple-element.23.grad_ref.do_ref, ...), custom_call_target="tpu_custom_call", output_to_operand_aliasing={{0}: (5, {})} | custom-call | flops 1342177280 | bytes 1048576 | tf_op jit(solution)/shard_map/far_b/pallas_call | solution.py:217
  24.8 0.1 collective-permute-done.2.kv_ref
  24.8 5.3 %far_cd.1 = (f32[2048,128]{1,0:T(8,128)S(1)}, bf16[512,512]{1,0:T(8,128)(2,1)S(1)}) custom-call(f32[8,128]{1,0:T(8,128)S(1)} %get-tuple-element.25.code_ref, bf16[2048,128]{1,0:T(8,128)(2,1)S(1)} %get-tuple-element.26.q_ref, bf16[2048,128]{1,0:T(8,128)(2,1)S(1)} %get-tuple-element.23.grad_ref.do_ref, ...), custom_call_target="tpu_custom_call", output_to_operand_aliasing={{0}: (5, {})} | custom-call | flops 2684354560 | bytes 2097152 | tf_op jit(solution)/shard_map/far_cd/pallas_call | solution.py:217
  30.2 1.9 %collective-permute-start.4 = (bf16[512,512]{1,0:T(8,128)(2,1)S(1)}, bf16[512,512]{1,0:T(8,128)(2,1)S(1)}, u32[]{:S(2)}, u32[]{:S(2)}) collective-permute-start(bf16[512,512]{1,0:T(8,128)(2,1)S(1)} %get-tuple-element.38), channel_id=1, source_target_pairs={{0,2},{2,0},{4,6},{6,4},{8,10},{10,8},{12,14},{14,12},{16,18},{18,... | collective-permute-start | bytes 1572872 | tf_op jit(solution)/shard_map/ppermute | solution.py:436
  32.1 7.3 %collective-permute-start.3 = (bf16[256,512]{1,0:T(8,128)(2,1)S(1)}, bf16[256,512]{1,0:T(8,128)(2,1)S(1)}, u32[]{:S(2)}, u32[]{:S(2)}) collective-permute-start(bf16[256,512]{1,0:T(8,128)(2,1)S(1)} %get-tuple-element.29._), channel_id=1, source_target_pairs={{4,0},{5,1},{511,2},{510,3},{8,4},{9,5},{2,6},{3,7},{12,8},{13,9},... | collective-permute-start | bytes 786440 | tf_op jit(solution)/shard_map/ppermute | solution.py:433
  39.4 0.0 collective-permute-done.4.b_ref.c_ref
  39.5 0.1 add.1
  39.5 3.8 %collective-permute-start.5 = (bf16[256,512]{1,0:T(8,128)(2,1)S(1)}, bf16[256,512]{1,0:T(8,128)(2,1)S(1)}, u32[]{:S(2)}, u32[]{:S(2)}) collective-permute-start(bf16[256,512]{1,0:T(8,128)(2,1)S(1)} %add.1), channel_id=1, source_target_pairs={{0,511},{1,510},{2,4},{3,5},{4,2},{5,3},{6,8},{7,9},{8,6},{9,7},{1... | collective-permute-start | bytes 786440 | tf_op jit(solution)/shard_map/ppermute | solution.py:439
  43.3 0.9 %own_low.1 = (f32[2048,128]{1,0:T(8,128)S(1)}, f32[256,256]{1,0:T(8,128)S(1)}) custom-call(f32[8,128]{1,0:T(8,128)S(1)} %get-tuple-element.25.code_ref, bf16[2048,128]{1,0:T(8,128)(2,1)S(1)} %get-tuple-element.26.q_ref, bf16[2048,128]{1,0:T(8,128)(2,1)S(1)} %get-tuple-element.23.grad_ref.do_ref, ...), custom_call_target="tpu_custom_call", output_to_operand_aliasing={{0}: (5, {})} | custom-call | flops 335544320 | bytes 1048576 | tf_op jit(solution)/shard_map/own_low/pallas_call | solution.py:284
  44.2 1.6 %own_high.1 = (f32[2048,128]{1,0:T(8,128)S(1)}, f32[256,512]{1,0:T(8,128)S(1)}) custom-call(f32[8,128]{1,0:T(8,128)S(1)} %get-tuple-element.25.code_ref, bf16[2048,128]{1,0:T(8,128)(2,1)S(1)} %get-tuple-element.26.q_ref, bf16[2048,128]{1,0:T(8,128)(2,1)S(1)} %get-tuple-element.23.grad_ref.do_ref, ...), custom_call_target="tpu_custom_call", output_to_operand_aliasing={{0}: (6, {})} | custom-call | flops 671088640 | bytes 1048576 | tf_op jit(solution)/shard_map/own_high/pallas_call | solution.py:284
  45.9 0.9 %finish.1 = bf16[2048,128]{1,0:T(8,128)(2,1)} custom-call(f32[2048,128]{1,0:T(8,128)S(1)} %get-tuple-element.35.dq_ref), custom_call_target="tpu_custom_call" | custom-call | flops 262144 | bytes 1572864 | tf_op jit(solution)/shard_map/finish/pallas_call | solution.py:306
  46.8 0.0 collective-permute-done.3.a_ref
  46.8 7.5 %collective-permute-done.5.b_ref = bf16[256,512]{1,0:T(8,128)(2,1)S(1)} collective-permute-done((bf16[256,512]{1,0:T(8,128)(2,1)S(1)}, bf16[256,512]{1,0:T(8,128)(2,1)S(1)}, u32[]{:S(2)}, u32[]{:S(2)}) %collective-permute-start.5) | collective-permute-done | bytes 262176 | tf_op jit(solution)/shard_map/ppermute | solution.py:439
  54.3 0.1 merge.1
  54.4 9.6 %all-gather = bf16[512,256]{1,0:T(8,128)(2,1)S(1)} all-gather(bf16[256,256]{1,0:T(8,128)(2,1)S(1)} %get-tuple-element.40), channel_id=2, replica_groups=mesh['ctx'=256,'head'=2] {'head'}, dimensions={0}, use_global_device_ids=true | all-gather | bytes 393216 | tf_op jit(solution)/shard_map/all_gather | solution.py:442
  64.0 0.8 %last.1 = (bf16[256,128]{1,0:T(8,128)(2,1)}, bf16[256,128]{1,0:T(8,128)(2,1)}) custom-call(f32[256,256]{1,0:T(8,128)S(1)} %get-tuple-element.39.keep_ref, bf16[2,256,256]{2,1,0:T(8,128)(2,1)S(1)} %bitcast.5), custom_call_target="tpu_custom_call" | custom-call | tf_op jit(solution)/shard_map/last/pallas_call | solution.py:376
  (1 shorter events, 0.0 us)
Async XLA Ops:
  0.6 14.2 %copy-start = (f32[4,512]{1,0:T(4,128)S(1)}, f32[4,512]{1,0:T(4,128)}, u32[]{:S(2)}) copy-start(f32[4,512]{1,0:T(4,128)} %lse_ref.1) | copy-start | bytes 24580
  2.2 12.6 %copy-start.1 = (s32[512]{0:T(512)S(1)}, s32[512]{0:T(512)}, u32[]{:S(2)}) copy-start(s32[512]{0:T(512)} %span_ref.1) | copy-start | bytes 6148
  2.2 16.1 %collective-permute-start.1 = (bf16[1024,128]{1,0:T(8,128)(2,1)S(1)}, bf16[1024,128]{1,0:T(8,128)(2,1)S(1)}, u32[]{:S(2)}, u32[]{:S(2)}) collective-permute-start(bf16[1024,128]{1,0:T(8,128)(2,1)S(1)} %get-tuple-element.28.a_ref.kv_ref), channel_id=1, source_target_pairs={{0,4},{1,5},{2,511},{3,510},{4,8},{5,9},{6,2},{7,3},{8,12},{9,13},... | collective-permute-start | bytes 786440 | tf_op jit(solution)/shard_map/ppermute | solution.py:427
  4.1 16.8 %collective-permute-start = (bf16[1024,128]{1,0:T(8,128)(2,1)S(1)}, bf16[1024,128]{1,0:T(8,128)(2,1)S(1)}, u32[]{:S(2)}, u32[]{:S(2)}) collective-permute-start(bf16[1024,128]{1,0:T(8,128)(2,1)S(1)} %get-tuple-element.28.a_ref.kv_ref), channel_id=1, source_target_pairs={{0,511},{1,510},{2,4},{3,5},{4,2},{5,3},{6,8},{7,9},{8,6},{9,7},{1... | collective-permute-start | bytes 786440 | tf_op jit(solution)/shard_map/ppermute | solution.py:428
  21.0 3.8 %collective-permute-start.2 = (bf16[2048,128]{1,0:T(8,128)(2,1)S(1)}, bf16[2048,128]{1,0:T(8,128)(2,1)S(1)}, u32[]{:S(2)}, u32[]{:S(2)}) collective-permute-start(bf16[2048,128]{1,0:T(8,128)(2,1)S(1)} %pack.1), channel_id=1, source_target_pairs={{0,2},{2,0},{4,6},{6,4},{8,10},{10,8},{12,14},{14,12},{16,18},{18,... | collective-permute-start | bytes 1572872 | tf_op jit(solution)/shard_map/ppermute | solution.py:432
  30.2 9.3 %collective-permute-start.4 = (bf16[512,512]{1,0:T(8,128)(2,1)S(1)}, bf16[512,512]{1,0:T(8,128)(2,1)S(1)}, u32[]{:S(2)}, u32[]{:S(2)}) collective-permute-start(bf16[512,512]{1,0:T(8,128)(2,1)S(1)} %get-tuple-element.38), channel_id=1, source_target_pairs={{0,2},{2,0},{4,6},{6,4},{8,10},{10,8},{12,14},{14,12},{16,18},{18,... | collective-permute-start | bytes 1572872 | tf_op jit(solution)/shard_map/ppermute | solution.py:436
  32.1 14.7 %collective-permute-start.3 = (bf16[256,512]{1,0:T(8,128)(2,1)S(1)}, bf16[256,512]{1,0:T(8,128)(2,1)S(1)}, u32[]{:S(2)}, u32[]{:S(2)}) collective-permute-start(bf16[256,512]{1,0:T(8,128)(2,1)S(1)} %get-tuple-element.29._), channel_id=1, source_target_pairs={{4,0},{5,1},{511,2},{510,3},{8,4},{9,5},{2,6},{3,7},{12,8},{13,9},... | collective-permute-start | bytes 786440 | tf_op jit(solution)/shard_map/ppermute | solution.py:433
  39.5 14.8 %collective-permute-start.5 = (bf16[256,512]{1,0:T(8,128)(2,1)S(1)}, bf16[256,512]{1,0:T(8,128)(2,1)S(1)}, u32[]{:S(2)}, u32[]{:S(2)}) collective-permute-start(bf16[256,512]{1,0:T(8,128)(2,1)S(1)} %add.1), channel_id=1, source_target_pairs={{0,511},{1,510},{2,4},{3,5},{4,2},{5,3},{6,8},{7,9},{8,6},{9,7},{1... | collective-permute-start | bytes 786440 | tf_op jit(solution)/shard_map/ppermute | solution.py:439

commit v6 on v4

v6 whole, which is shorter than its diff:
```python
import functools

import jax
import jax.numpy as jnp
from jax import lax
from jax.experimental import pallas as pl
from jax.experimental.pallas import tpu as pltpu
from jax.sharding import PartitionSpec as P

F32 = jnp.float32
BF16 = jnp.bfloat16
LOG2E = 1.4426950408889634
SUB = 512
LOW = 4
VMEM = pl.BlockSpec(memory_space=pltpu.VMEM)
SMEM = pl.BlockSpec(memory_space=pltpu.SMEM)


def dot(a, b, ca, cb):
    return lax.dot_general(a, b, (((ca,), (cb,)), ((), ())), preferred_element_type=F32)


def lane_ones(rows, low, high):
    lane = lax.broadcasted_iota(jnp.int32, (rows, 128), 1)
    return jnp.where((lane >= low) & (lane < high), 1.0, 0.0).astype(BF16)


def load_kernel(k_ref, v_ref, q_ref, do_ref, out_ref, kv_to, rows_to, out_to, sems):
    tokens, rows = k_ref.shape[0], q_ref.shape[0]
    copies = [
        pltpu.make_async_copy(source, target, sems.at[i])
        for i, (source, target) in enumerate(
            [
                (k_ref, kv_to.at[pl.ds(0, tokens)]),
                (v_ref, kv_to.at[pl.ds(tokens, tokens)]),
                (do_ref, rows_to.at[pl.ds(rows, rows)]),
                (out_ref, out_to),
                (q_ref, rows_to.at[pl.ds(0, rows)]),
            ]
        )
    ]
    for copy in copies:
        copy.start()
    for copy in copies:
        copy.wait()


def load(keys, values, q, do, out):
    tokens, depth = keys.shape
    rows = q.shape[0]
    args = [pltpu.with_memory_space_constraint(a, pltpu.HBM) for a in (keys, values, q, do, out)]
    return pl.pallas_call(
        load_kernel,
        out_shape=[
            jax.ShapeDtypeStruct((2 * tokens, depth), BF16),
            jax.ShapeDtypeStruct((3 * rows, depth), BF16),
            jax.ShapeDtypeStruct((rows, depth), BF16),
        ],
        in_specs=[pl.BlockSpec(memory_space=pltpu.HBM)] * 5,
        out_specs=[VMEM] * 3,
        scratch_shapes=[pltpu.SemaphoreType.DMA((5,))],
        compiler_params=pltpu.CompilerParams(vmem_limit_bytes=8 * 2**20),
        name="load",
    )(*args)


def prep_kernel(span_ref, rows_in_ref, out_ref, lse_ref, rows_ref, code_ref, wide):
    count = lax.axis_size("ctx")
    me = lax.axis_index("ctx")
    sign = 1 - 2 * (me % 2)
    mate, near, far = me + sign, (me - sign + count) % count, (me - 2 * sign + count) % count
    row = lax.broadcasted_iota(jnp.int32, code_ref.shape, 0)
    later = span_ref[2 * me] > span_ref[2 * me + 1]
    codes = jnp.where(row == LOW, jnp.where(later, 1.0, 0.0), 0.0)
    for r, (query, source) in enumerate(((me, far), (me, near), (mate, near), (mate, me))):
        q0, q1 = span_ref[2 * query], span_ref[2 * query + 1]
        k0, k1 = span_ref[2 * source], span_ref[2 * source + 1]
        code = 0.0
        for bit, allowed in enumerate((k0 < q0, k0 < q1, k1 < q0, k1 < q1)):
            code = code + jnp.where(allowed, float(2**bit), 0.0)
        codes = jnp.where(row == r, code, codes)
    code_ref[...] = codes
    rows = out_ref.shape[0]
    heads, tokens = lse_ref.shape
    depth = out_ref.shape[1]
    lse = lse_ref[...] * float(depth**0.5)
    turned = jnp.concatenate([lse, jnp.zeros((128 - heads, tokens), F32)], axis=0).T
    for g in range(heads):
        wide[pl.ds(g, tokens, stride=heads), :] = jnp.broadcast_to(
            turned[:, g : g + 1], (tokens, 128)
        )
    delta = jnp.sum(
        rows_in_ref[rows : 2 * rows, :].astype(F32) * out_ref[...].astype(F32), axis=1, keepdims=True
    )
    lane = lax.broadcasted_iota(jnp.int32, wide.shape, 1)
    rest = jnp.where(lane < 3, wide[...], delta)
    high = rest.astype(BF16).astype(F32)
    rest = rest - high
    mid = rest.astype(BF16).astype(F32)
    low = rest - mid
    place = jnp.where(lane < 3, lane, lane - 3)
    term = jnp.where(place == 0, high, jnp.where(place == 1, mid, low))
    rows_ref[2 * rows : 3 * rows, :] = jnp.where(lane < 6, -term, 0.0).astype(BF16)


def read_code(code_ref, row):
    return jnp.max(code_ref[pl.ds(row, 1), :]).astype(jnp.int32)


def prep(spans, q_rows, out_rows, lse):
    rows = out_rows.shape[0]
    return pl.pallas_call(
        prep_kernel,
        out_shape=[
            jax.ShapeDtypeStruct(q_rows.shape, BF16),
            jax.ShapeDtypeStruct((8, 128), F32),
        ],
        in_specs=[SMEM] + [VMEM] * 3,
        out_specs=[VMEM] * 2,
        input_output_aliases={1: 0},
        scratch_shapes=[pltpu.VMEM((rows, 128), F32)],
        compiler_params=pltpu.CompilerParams(vmem_limit_bytes=16 * 2**20),
        cost_estimate=pl.CostEstimate(flops=rows * 1024, bytes_accessed=rows * 768, transcendentals=0),
        name="prep",
    )(spans, q_rows, out_rows, lse)


def tile(rows_ref, key, value, q_base, rows, mask=None):
    span, depth = key.shape
    count = rows_ref.shape[0] // 3
    exponent = float(depth**-0.5 * LOG2E)
    key_x = jnp.concatenate([key, lane_ones(span, 0, 3)], axis=1)
    value_x = jnp.concatenate([value, lane_ones(span, 3, 6)], axis=1)

    def front(i):
        first = pl.multiple_of(q_base + i * SUB, SUB)
        at = pl.ds(first, SUB)
        q, do, x = (rows_ref[pl.ds(first + part * count, SUB), :] for part in range(3))
        p = jnp.exp2(dot(jnp.concatenate([q, x], axis=1), key_x, 1, 1) * exponent)
        if mask is not None:
            p = jnp.where(mask(i * SUB, SUB, span), p, 0.0)
        dp = dot(jnp.concatenate([do, x], axis=1), value_x, 1, 1)
        return at, q, do, p.astype(BF16), (p * dp).astype(BF16)

    dk, dv = None, None
    pieces = rows // SUB
    later = front(0)
    terms = []
    for i in range(pieces):
        at, q, do, p, ds = later
        if i + 1 < pieces:
            later = front(i + 1)
        yield_dq = dot(ds, key, 1, 0)
        terms.append((at, yield_dq))
        part_v, part_k = dot(do, p, 0, 0), dot(q, ds, 0, 0)
        dv = part_v if dv is None else dv + part_v
        dk = part_k if dk is None else dk + part_k
    return terms, dk, dv


def far_kernel(row, has_dq, has_g, has_low, code_ref, rows_ref, kv_ref, *refs):
    refs = list(refs)
    dq_in = refs.pop(0) if has_dq else None
    g_in = refs.pop(0) if has_g else None
    low_ref = refs.pop() if has_low else None
    dq_ref, g_ref = refs[-2:]
    depth = kv_ref.shape[1]
    tokens = kv_ref.shape[0] // 2
    span = tokens // 2
    half = rows_ref.shape[0] // 6
    code = read_code(code_ref, row)
    every = code == 15

    def put(rows, lanes, value):
        if has_g:
            value = value + g_in[rows, lanes]
        g_ref[rows, lanes] = value.astype(g_ref.dtype)

    def run(base, count, at, keys, lanes, store=False):
        key, value = kv_ref[pl.ds(at, keys), :], kv_ref[pl.ds(at + tokens, keys), :]
        terms, dk, dv = tile(rows_ref, key, value, base, count)
        for rows_at, term in terms:
            dq_ref[rows_at, :] = term if store else dq_ref[rows_at, :] + term
        put(pl.ds(0, depth), lanes, dk)
        put(pl.ds(depth, depth), lanes, dv)

    @pl.when(every)
    def _():
        run(0, 2 * half, 0, tokens, pl.ds(0, tokens), store=not has_dq)

    def one_span(j, carry):
        bits = jnp.where(j == 0, code, code // 4)
        at = pl.multiple_of(j * span, span)
        lanes = pl.ds(at, span)
        a0, a1 = bits % 2 == 1, (bits // 2) % 2 == 1

        @pl.when(a0 & a1)
        def _():
            run(0, 2 * half, at, span, lanes)

        @pl.when(a0 != a1)
        def _():
            run(jnp.where(a1, half, 0), half, at, span, lanes)

        @pl.when(~(a0 | a1))
        def _():
            put(pl.ds(0, 2 * depth), lanes, jnp.zeros((2 * depth, span), F32))

        return carry

    @pl.when(~every)
    def _():
        if not has_dq:
            dq_ref[...] = jnp.zeros_like(dq_ref)
        lax.fori_loop(0, 2, one_span, 0)

    if has_low:
        low_ref[...] = dq_ref[...].astype(BF16)


def far(row, codes, q_rows, kv, name, dq=None, g=None, dtype=F32, low=False, weight=10):
    rows, depth = q_rows.shape[0] // 3, q_rows.shape[1]
    tokens = kv.shape[0] // 2
    args = [codes, q_rows, kv] + [a for a in (dq, g) if a is not None]
    wide = jax.ShapeDtypeStruct((rows, depth), F32)
    return pl.pallas_call(
        functools.partial(far_kernel, row, dq is not None, g is not None, low),
        out_shape=[wide, jax.ShapeDtypeStruct((2 * depth, tokens), dtype)]
        + ([jax.ShapeDtypeStruct((rows, depth), BF16)] if low else []),
        in_specs=[VMEM] * len(args),
        out_specs=[VMEM] * (3 if low else 2),
        input_output_aliases={} if dq is None else {3: 0},
        compiler_params=pltpu.CompilerParams(vmem_limit_bytes=24 * 2**20),
        cost_estimate=pl.CostEstimate(
            flops=weight * rows * tokens * depth,
            bytes_accessed=2**16,
            transcendentals=weight * rows * tokens // 10,
        ),
        name=name,
    )(*args)


def own_low_kernel(code_ref, rows_ref, kv_ref, _, dq_ref, g_ref):
    depth = kv_ref.shape[1]
    tokens = kv_ref.shape[0] // 2
    span, half = tokens // 2, rows_ref.shape[0] // 6
    heads = half // span
    low = read_code(code_ref, LOW)

    def causal(base, rows, keys):
        row = lax.broadcasted_iota(jnp.int32, (rows, keys), 0)
        return heads * lax.broadcasted_iota(jnp.int32, (rows, keys), 1) - row <= base

    at = pl.multiple_of(low * span, span)
    key, value = kv_ref[pl.ds(at, span), :], kv_ref[pl.ds(at + tokens, span), :]
    terms, dk, dv = tile(rows_ref, key, value, low * half, half, causal)
    for rows_at, term in terms:
        dq_ref[rows_at, :] += term
    g_ref[0:depth, :] = dk
    g_ref[depth : 2 * depth, :] = dv


def own_high_kernel(code_ref, rows_ref, kv_ref, g_low_ref, _, dq_ref, g_ref):
    depth = kv_ref.shape[1]
    tokens = kv_ref.shape[0] // 2
    span, half = tokens // 2, rows_ref.shape[0] // 6
    heads = half // span
    low = read_code(code_ref, LOW)

    def causal(base, rows, keys):
        row = lax.broadcasted_iota(jnp.int32, (rows, keys), 0)
        slot = lax.broadcasted_iota(jnp.int32, (1, keys), 1)
        own = (slot >= span) == (low == 0)
        return jnp.where(own, heads * (slot & (span - 1)), -1) - row <= base

    terms, dk, dv = tile(
        rows_ref, kv_ref[0:tokens, :], kv_ref[tokens : 2 * tokens, :],
        (1 - low) * half, half, causal,
    )
    for rows_at, term in terms:
        dq_ref[rows_at, :] += term
    g_ref[0:depth, :] = dk
    g_ref[depth : 2 * depth, :] = dv
    lanes = pl.ds(pl.multiple_of(low * span, span), span)
    g_ref[:, lanes] += g_low_ref[...]


def own(kernel, codes, q_rows, kv, extra, dq, keys, name):
    rows, depth = dq.shape
    args = [codes, q_rows, kv] + extra + [dq]
    return pl.pallas_call(
        kernel,
        out_shape=[
            jax.ShapeDtypeStruct((rows, depth), F32),
            jax.ShapeDtypeStruct((2 * depth, keys), F32),
        ],
        in_specs=[VMEM] * len(args),
        out_specs=[VMEM, VMEM],
        input_output_aliases={len(args) - 1: 0},
        compiler_params=pltpu.CompilerParams(vmem_limit_bytes=24 * 2**20),
        cost_estimate=pl.CostEstimate(
            flops=rows * keys * depth // 10, bytes_accessed=2**16, transcendentals=rows * keys // 100
        ),
        name=name,
    )(*args)


def finish_kernel(dq_ref, mate_ref, o_ref):
    total = dq_ref[...] + mate_ref[...].astype(F32)
    o_ref[...] = (total * float(dq_ref.shape[1] ** -0.5)).astype(BF16)


def finish(dq, mate):
    return pl.pallas_call(
        finish_kernel,
        out_shape=jax.ShapeDtypeStruct(dq.shape, BF16),
        in_specs=[VMEM, VMEM],
        out_specs=VMEM,
        compiler_params=pltpu.CompilerParams(vmem_limit_bytes=8 * 2**20),
        cost_estimate=pl.CostEstimate(flops=dq.size, bytes_accessed=6 * dq.size, transcendentals=0),
        name="finish",
    )(dq, mate)


def merge_kernel(own_ref, a_ref, b_ref, c_ref, _, keep_ref, send_ref):
    rows, tokens = own_ref.shape
    half = tokens // 2
    head = lax.axis_index("head")

    def part(index):
        lanes = pl.ds(pl.multiple_of(index * half, half), half)
        return (
            own_ref[:, lanes]
            + a_ref[:, lanes].astype(F32)
            + b_ref[:, lanes].astype(F32)
            + c_ref[:, lanes]
        )

    send_ref[...] = part(1 - head).astype(BF16)
    keep_ref[...] = part(head)


def merge(g, a, b, c, after):
    rows, tokens = g.shape
    return pl.pallas_call(
        merge_kernel,
        out_shape=[
            jax.ShapeDtypeStruct((rows, tokens // 2), F32),
            jax.ShapeDtypeStruct((rows, tokens // 2), BF16),
        ],
        in_specs=[VMEM] * 4 + [pl.BlockSpec(memory_space=pl.ANY)],
        out_specs=[VMEM, VMEM],
        compiler_params=pltpu.CompilerParams(vmem_limit_bytes=8 * 2**20),
        name="merge",
    )(g, a, b, c, after)


def last_kernel(keep_ref, got_ref, dk_ref, dv_ref):
    total = keep_ref[...] + got_ref[1 - lax.axis_index("head")].astype(F32)
    depth = total.shape[0] // 2
    dk_ref[...] = (total[:depth].T * float(depth**-0.5)).astype(BF16)
    dv_ref[...] = total[depth:].T.astype(BF16)


def last(keep, got):
    rows, tokens = keep.shape
    shape = jax.ShapeDtypeStruct((tokens, rows // 2), BF16)
    return pl.pallas_call(
        last_kernel,
        out_shape=[shape, shape],
        in_specs=[VMEM, VMEM],
        out_specs=[VMEM, VMEM],
        compiler_params=pltpu.CompilerParams(vmem_limit_bytes=8 * 2**20),
        name="last",
    )(keep, got)


def ring(count, move):
    pairs = []
    for d in range(count):
        target = move(d)
        flip = 0 if 0 <= target < count else 1
        for h in range(2):
            pairs.append((2 * d + h, 2 * (target % count) + (h ^ flip)))
    return pairs


def local(queries, keys, values, outputs, grad_out, lse, span_order):
    tokens, heads, depth = queries.shape
    count = lax.axis_size("ctx")
    both = ("ctx", "head")
    q = queries.reshape(tokens * heads, depth)
    do = grad_out.reshape(tokens * heads, depth)
    out = outputs.reshape(tokens * heads, depth)
    over_two = ring(count, lambda d: d - 2 if d % 2 else d + 2)
    back_two = [(b, a) for a, b in over_two]
    over_one = ring(count, lambda d: d + 1 if d % 2 else d - 1)
    mates = [(d, d ^ 1) for d in range(count)]

    kv, q_rows, out = load(keys, values, q, do, out)
    kv_a = lax.ppermute(kv, both, over_two)
    kv_b = lax.ppermute(kv, both, over_one)
    q_rows, codes = prep(span_order, q_rows, out, lse)
    mate_rows = lax.ppermute(q_rows, "ctx", mates)

    dq, g_a = far(0, codes, q_rows, kv_a, "far_a", dtype=BF16)
    got_a = lax.ppermute(g_a, both, back_two)
    dq, g_b = far(1, codes, q_rows, kv_b, "far_b", dq=dq, weight=1000)
    dq_mate, g_mate = far(3, codes, mate_rows, kv, "own_mate")
    _, g_b, dq_low = far(
        2, codes, mate_rows, kv_b, "far_b_mate", dq=dq_mate, g=g_b, dtype=BF16, low=True
    )
    got_b = lax.ppermute(g_b, both, over_one)
    got_dq = lax.ppermute(dq_low, "ctx", mates)
    dq, g_low = own(own_low_kernel, codes, q_rows, kv, [], dq, tokens // 2, "own_low")
    dq, g_own = own(own_high_kernel, codes, q_rows, kv, [g_low], dq, tokens, "own_high")
    grad_q = finish(dq, got_dq)
    keep, send = merge(g_own, got_a, got_b, g_mate, grad_q)
    got = lax.all_gather(send, "head")
    grad_k, grad_v = last(keep, got)
    return grad_q.reshape(tokens, heads, depth), grad_k, grad_v


def solution(mesh):
    return jax.shard_map(
        local,
        mesh=mesh,
        in_specs=(
            P("ctx", "head", None),
            P("ctx", None),
            P("ctx", None),
            P("ctx", "head", None),
            P("ctx", "head", None),
            P("head", "ctx"),
            P(),
        ),
        out_specs=(P("ctx", "head", None), P(("ctx", "head"), None), P(("ctx", "head"), None)),
        check_vma=False,
    )
```

time: 67.8 us -> 60.6 us (0.89)
  the two profiles are of different devices: /device:TPU:1 before, /device:TPU:0 now
where the time goes in v6:
time: 60.6 us; the launch traced here: 60.2 us
  starting transfers between devices  27.5 us (45%)
  Pallas kernels  16.1 us (27%)
  blocking collectives  10.2 us (17%)
  waiting for transfers between devices  4.63 us (8%)
  local copies, waits for them, and re-layouts  1.05 us (2%)
  between operations  0.8 us (1%)
    ppermute x1, starting transfers between devices, local(): kv_b = lax.ppermute(kv, both, over_one)  10.7 us
    all_gather x1, blocking collectives, local(): got = lax.all_gather(send, 'head')  10.2 us
    pallas_call x4, Pallas kernels, far(): pl.pallas_call(functools.partial(far_kernel, row, dq is not None, g is no...  8.66 us
    ppermute x1, starting transfers between devices, local(): got_b = lax.ppermute(g_b, both, over_one)  5.99 us
    ppermute x1, starting transfers between devices, local(): got_a = lax.ppermute(g_a, both, back_two)  5.11 us
    ppermute x1, waiting for transfers between devices, local(): got_b = lax.ppermute(g_b, both, over_one)  4.5 us
    pallas_call x2, Pallas kernels, own(): pl.pallas_call(kernel, out_shape=[jax.ShapeDtypeStruct((rows, depth), F32...  2.57 us
    ppermute x1, starting transfers between devices, local(): mate_rows = lax.ppermute(q_rows, 'ctx', mates)  1.92 us
  transfers between devices with their start and end apart: 6, of which 2 were waited for; matrix products, arithmetic and copies ran while one was open for 0% of the time, Pallas kernels for 15%

profile of v6, /device:TPU:0, one launch (start us, length us, event | category | flops | bytes accessed | tf_op | source)
XLA Modules:
  0.0 60.2 jit_solution(13081466537028734036)
XLA Ops:
  0.6 0.0 copy-start.2
  0.6 0.0 copy-start.1
  0.7 1.5 %load.1 = (bf16[1024,128]{1,0:T(8,128)(2,1)S(1)}, bf16[6144,128]{1,0:T(8,128)(2,1)S(1)}, bf16[2048,128]{1,0:T(8,128)(2,1)S(1)}) custom-call(bf16[512,128]{1,0:T(8,128)(2,1)} %k_ref.1, bf16[512,128]{1,0:T(8,128)(2,1)} %v_ref.1, bf16[2048,128]{1,0:T(8,128)(2,1)} %bitcast.7, bf16[2048,128]{1,0:T(8,128)(2,1)} %bitcast.8, bf16[2048,128]{1,0:T(8,128)(2,1)} %bitcast.9), custom_call_target="tpu_custom_call" | custom-call | tf_op jit(solution)/shard_map/load/pallas_call | solution.py:52
  2.2 1.9 %collective-permute-start.1 = (bf16[1024,128]{1,0:T(8,128)(2,1)S(1)}, bf16[1024,128]{1,0:T(8,128)(2,1)S(1)}, u32[]{:S(2)}, u32[]{:S(2)}) collective-permute-start(bf16[1024,128]{1,0:T(8,128)(2,1)S(1)} %get-tuple-element.28.kv_ref), channel_id=1, source_target_pairs={{0,4},{1,5},{2,511},{3,510},{4,8},{5,9},{6,2},{7,3},{8,12},{9,13},... | collective-permute-start | bytes 786440 | tf_op jit(solution)/shard_map/ppermute | solution.py:401
  4.1 10.7 %collective-permute-start = (bf16[1024,128]{1,0:T(8,128)(2,1)S(1)}, bf16[1024,128]{1,0:T(8,128)(2,1)S(1)}, u32[]{:S(2)}, u32[]{:S(2)}) collective-permute-start(bf16[1024,128]{1,0:T(8,128)(2,1)S(1)} %get-tuple-element.28.kv_ref), channel_id=1, source_target_pairs={{0,511},{1,510},{2,4},{3,5},{4,2},{5,3},{6,8},{7,9},{8,6},{9,7},{1... | collective-permute-start | bytes 786440 | tf_op jit(solution)/shard_map/ppermute | solution.py:402
  14.8 0.0 copy-done.2
  14.8 0.0 copy-done.1
  14.8 1.5 %prep.1 = (bf16[6144,128]{1,0:T(8,128)(2,1)S(1)}, f32[8,128]{1,0:T(8,128)S(1)}) custom-call(s32[512]{0:T(512)S(1)} %copy-done.2, bf16[6144,128]{1,0:T(8,128)(2,1)S(1)} %get-tuple-element.24.rows_in_ref, bf16[2048,128]{1,0:T(8,128)(2,1)S(1)} %get-tuple-element.25.out_ref, f32[4,512]{1,0:T(4,128)S(1)} %copy-done.1), custom_call_target="tpu_custom_call", output_to_operand_aliasing={{0}: (1, {})} | custom-call | flops 2097152 | bytes 1572864 | tf_op jit(solution)/shard_map/prep/pallas_call | solution.py:112
  16.3 1.9 %collective-permute-start.2 = (bf16[6144,128]{1,0:T(8,128)(2,1)S(1)}, bf16[6144,128]{1,0:T(8,128)(2,1)S(1)}, u32[]{:S(2)}, u32[]{:S(2)}) collective-permute-start(bf16[6144,128]{1,0:T(8,128)(2,1)S(1)} %get-tuple-element.27.rows_ref), channel_id=1, source_target_pairs={{0,2},{2,0},{4,6},{6,4},{8,10},{10,8},{12,14},{14,12},{16,18},{18,... | collective-permute-start | bytes 4718600 | tf_op jit(solution)/shard_map/ppermute | solution.py:404
  18.2 0.1 collective-permute-done.1.kv_ref
  18.4 2.4 %far_a.1 = (f32[2048,128]{1,0:T(8,128)S(1)}, bf16[256,512]{1,0:T(8,128)(2,1)S(1)}) custom-call(f32[8,128]{1,0:T(8,128)S(1)} %get-tuple-element.26.code_ref, bf16[6144,128]{1,0:T(8,128)(2,1)S(1)} %get-tuple-element.27.rows_ref, bf16[1024,128]{1,0:T(8,128)(2,1)S(1)} %collective-permute-done.1.kv_ref), custom_call_target="tpu_custom_call" | custom-call | flops 1342177280 | bytes 65536 | tf_op jit(solution)/shard_map/far_a/pallas_call | solution.py:226
  20.8 0.0 collective-permute-done.kv_ref
  20.8 1.7 %far_b.1 = (f32[2048,128]{1,0:T(8,128)S(1)}, f32[256,512]{1,0:T(8,128)S(1)}) custom-call(f32[8,128]{1,0:T(8,128)S(1)} %get-tuple-element.26.code_ref, bf16[6144,128]{1,0:T(8,128)(2,1)S(1)} %get-tuple-element.27.rows_ref, bf16[1024,128]{1,0:T(8,128)(2,1)S(1)} %collective-permute-done.kv_ref, ...), custom_call_target="tpu_custom_call", output_to_operand_aliasing={{0}: (3, {})} | custom-call | flops 134217728000 | bytes 65536 | tf_op jit(solution)/shard_map/far_b/pallas_call | solution.py:226
  22.5 0.0 collective-permute-done.2.rows_ref
  22.5 1.8 %own_mate.1 = (f32[2048,128]{1,0:T(8,128)S(1)}, f32[256,512]{1,0:T(8,128)S(1)}) custom-call(f32[8,128]{1,0:T(8,128)S(1)} %get-tuple-element.26.code_ref, bf16[6144,128]{1,0:T(8,128)(2,1)S(1)} %collective-permute-done.2.rows_ref, bf16[1024,128]{1,0:T(8,128)(2,1)S(1)} %get-tuple-element.28.kv_ref), custom_call_target="tpu_custom_call" | custom-call | flops 1342177280 | bytes 65536 | tf_op jit(solution)/shard_map/own_mate/pallas_call | solution.py:226
  24.4 2.7 %far_b_mate.1 = (f32[2048,128]{1,0:T(8,128)S(1)}, bf16[256,512]{1,0:T(8,128)(2,1)S(1)}, bf16[2048,128]{1,0:T(8,128)(2,1)S(1)}) custom-call(f32[8,128]{1,0:T(8,128)S(1)} %get-tuple-element.26.code_ref, bf16[6144,128]{1,0:T(8,128)(2,1)S(1)} %collective-permute-done.2.rows_ref, ...), custom_call_target="tpu_custom_call", output_to_operand_aliasing={{0}: (3, {})} | custom-call | flops 1342177280 | bytes 65536 | tf_op jit(solution)/shard_map/far_b_mate/pallas_call | solution.py:226
  27.1 1.9 %collective-permute-start.3 = (bf16[2048,128]{1,0:T(8,128)(2,1)S(1)}, bf16[2048,128]{1,0:T(8,128)(2,1)S(1)}, u32[]{:S(2)}, u32[]{:S(2)}) collective-permute-start(bf16[2048,128]{1,0:T(8,128)(2,1)S(1)} %get-tuple-element.36), channel_id=1, source_target_pairs={{0,2},{2,0},{4,6},{6,4},{8,10},{10,8},{12,14},{14,12},{16,18},{18,... | collective-permute-start | bytes 1572872 | tf_op jit(solution)/shard_map/ppermute | solution.py:414
  29.0 5.1 %collective-permute-start.4 = (bf16[256,512]{1,0:T(8,128)(2,1)S(1)}, bf16[256,512]{1,0:T(8,128)(2,1)S(1)}, u32[]{:S(2)}, u32[]{:S(2)}) collective-permute-start(bf16[256,512]{1,0:T(8,128)(2,1)S(1)} %get-tuple-element.38), channel_id=1, source_target_pairs={{4,0},{5,1},{511,2},{510,3},{8,4},{9,5},{2,6},{3,7},{12,8},{13,9},... | collective-permute-start | bytes 786440 | tf_op jit(solution)/shard_map/ppermute | solution.py:407
  34.1 6.0 %collective-permute-start.5 = (bf16[256,512]{1,0:T(8,128)(2,1)S(1)}, bf16[256,512]{1,0:T(8,128)(2,1)S(1)}, u32[]{:S(2)}, u32[]{:S(2)}) collective-permute-start(bf16[256,512]{1,0:T(8,128)(2,1)S(1)} %get-tuple-element.39), channel_id=1, source_target_pairs={{0,511},{1,510},{2,4},{3,5},{4,2},{5,3},{6,8},{7,9},{8,6},{9,7},{1... | collective-permute-start | bytes 786440 | tf_op jit(solution)/shard_map/ppermute | solution.py:413
  40.1 0.9 %own_low.1 = (f32[2048,128]{1,0:T(8,128)S(1)}, f32[256,256]{1,0:T(8,128)S(1)}) custom-call(f32[8,128]{1,0:T(8,128)S(1)} %get-tuple-element.26.code_ref, bf16[6144,128]{1,0:T(8,128)(2,1)S(1)} %get-tuple-element.27.rows_ref, bf16[1024,128]{1,0:T(8,128)(2,1)S(1)} %get-tuple-element.28.kv_ref, ...), custom_call_target="tpu_custom_call", output_to_operand_aliasing={{0}: (3, {})} | custom-call | flops 6710886 | bytes 65536 | tf_op jit(solution)/shard_map/own_low/pallas_call | solution.py:291
  41.0 1.7 %own_high.1 = (f32[2048,128]{1,0:T(8,128)S(1)}, f32[256,512]{1,0:T(8,128)S(1)}) custom-call(f32[8,128]{1,0:T(8,128)S(1)} %get-tuple-element.26.code_ref, bf16[6144,128]{1,0:T(8,128)(2,1)S(1)} %get-tuple-element.27.rows_ref, bf16[1024,128]{1,0:T(8,128)(2,1)S(1)} %get-tuple-element.28.kv_ref, ...), custom_call_target="tpu_custom_call", output_to_operand_aliasing={{0}: (4, {})} | custom-call | flops 13421772 | bytes 65536 | tf_op jit(solution)/shard_map/own_high/pallas_call | solution.py:291
  42.7 0.0 collective-permute-done.3.mate_ref
  42.7 0.9 %finish.1._ = bf16[2048,128]{1,0:T(8,128)(2,1)} custom-call(f32[2048,128]{1,0:T(8,128)S(1)} %get-tuple-element.33.dq_ref, bf16[2048,128]{1,0:T(8,128)(2,1)S(1)} %collective-permute-done.3.mate_ref), custom_call_target="tpu_custom_call" | custom-call | flops 262144 | bytes 1572864 | tf_op jit(solution)/shard_map/finish/pallas_call | solution.py:314
  43.6 0.0 collective-permute-done.4.a_ref
  43.6 4.5 %collective-permute-done.5.b_ref = bf16[256,512]{1,0:T(8,128)(2,1)S(1)} collective-permute-done((bf16[256,512]{1,0:T(8,128)(2,1)S(1)}, bf16[256,512]{1,0:T(8,128)(2,1)S(1)}, u32[]{:S(2)}, u32[]{:S(2)}) %collective-permute-start.5) | collective-permute-done | bytes 262176 | tf_op jit(solution)/shard_map/ppermute | solution.py:413
  48.1 0.0 copy-start
  48.1 1.0 %copy-done = bf16[2048,128]{1,0:T(8,128)(2,1)S(1)} copy-done((bf16[2048,128]{1,0:T(8,128)(2,1)S(1)}, bf16[2048,128]{1,0:T(8,128)(2,1)}, u32[]{:S(2)}) %copy-start) | copy-done | bytes 524312
  49.2 0.1 merge.1
  49.3 10.2 %all-gather = bf16[512,256]{1,0:T(8,128)(2,1)S(1)} all-gather(bf16[256,256]{1,0:T(8,128)(2,1)S(1)} %get-tuple-element.42), channel_id=2, replica_groups=mesh['ctx'=256,'head'=2] {'head'}, dimensions={0}, use_global_device_ids=true | all-gather | bytes 393216 | tf_op jit(solution)/shard_map/all_gather | solution.py:419
  59.4 0.8 %last.1 = (bf16[256,128]{1,0:T(8,128)(2,1)}, bf16[256,128]{1,0:T(8,128)(2,1)}) custom-call(f32[256,256]{1,0:T(8,128)S(1)} %get-tuple-element.41.keep_ref, bf16[2,256,256]{2,1,0:T(8,128)(2,1)S(1)} %bitcast.6), custom_call_target="tpu_custom_call" | custom-call | tf_op jit(solution)/shard_map/last/pallas_call | solution.py:368
Async XLA Ops:
  0.6 14.2 %copy-start.2 = (s32[512]{0:T(512)S(1)}, s32[512]{0:T(512)}, u32[]{:S(2)}) copy-start(s32[512]{0:T(512)} %span_ref.1) | copy-start | bytes 6148
  0.6 14.2 %copy-start.1 = (f32[4,512]{1,0:T(4,128)S(1)}, f32[4,512]{1,0:T(4,128)}, u32[]{:S(2)}) copy-start(f32[4,512]{1,0:T(4,128)} %lse_ref.1) | copy-start | bytes 24580
  2.2 16.1 %collective-permute-start.1 = (bf16[1024,128]{1,0:T(8,128)(2,1)S(1)}, bf16[1024,128]{1,0:T(8,128)(2,1)S(1)}, u32[]{:S(2)}, u32[]{:S(2)}) collective-permute-start(bf16[1024,128]{1,0:T(8,128)(2,1)S(1)} %get-tuple-element.28.kv_ref), channel_id=1, source_target_pairs={{0,4},{1,5},{2,511},{3,510},{4,8},{5,9},{6,2},{7,3},{8,12},{9,13},... | collective-permute-start | bytes 786440 | tf_op jit(solution)/shard_map/ppermute | solution.py:401
  4.1 16.6 %collective-permute-start = (bf16[1024,128]{1,0:T(8,128)(2,1)S(1)}, bf16[1024,128]{1,0:T(8,128)(2,1)S(1)}, u32[]{:S(2)}, u32[]{:S(2)}) collective-permute-start(bf16[1024,128]{1,0:T(8,128)(2,1)S(1)} %get-tuple-element.28.kv_ref), channel_id=1, source_target_pairs={{0,511},{1,510},{2,4},{3,5},{4,2},{5,3},{6,8},{7,9},{8,6},{9,7},{1... | collective-permute-start | bytes 786440 | tf_op jit(solution)/shard_map/ppermute | solution.py:402
  16.3 6.2 %collective-permute-start.2 = (bf16[6144,128]{1,0:T(8,128)(2,1)S(1)}, bf16[6144,128]{1,0:T(8,128)(2,1)S(1)}, u32[]{:S(2)}, u32[]{:S(2)}) collective-permute-start(bf16[6144,128]{1,0:T(8,128)(2,1)S(1)} %get-tuple-element.27.rows_ref), channel_id=1, source_target_pairs={{0,2},{2,0},{4,6},{6,4},{8,10},{10,8},{12,14},{14,12},{16,18},{18,... | collective-permute-start | bytes 4718600 | tf_op jit(solution)/shard_map/ppermute | solution.py:404
  27.1 15.6 %collective-permute-start.3 = (bf16[2048,128]{1,0:T(8,128)(2,1)S(1)}, bf16[2048,128]{1,0:T(8,128)(2,1)S(1)}, u32[]{:S(2)}, u32[]{:S(2)}) collective-permute-start(bf16[2048,128]{1,0:T(8,128)(2,1)S(1)} %get-tuple-element.36), channel_id=1, source_target_pairs={{0,2},{2,0},{4,6},{6,4},{8,10},{10,8},{12,14},{14,12},{16,18},{18,... | collective-permute-start | bytes 1572872 | tf_op jit(solution)/shard_map/ppermute | solution.py:414
  29.0 14.6 %collective-permute-start.4 = (bf16[256,512]{1,0:T(8,128)(2,1)S(1)}, bf16[256,512]{1,0:T(8,128)(2,1)S(1)}, u32[]{:S(2)}, u32[]{:S(2)}) collective-permute-start(bf16[256,512]{1,0:T(8,128)(2,1)S(1)} %get-tuple-element.38), channel_id=1, source_target_pairs={{4,0},{5,1},{511,2},{510,3},{8,4},{9,5},{2,6},{3,7},{12,8},{13,9},... | collective-permute-start | bytes 786440 | tf_op jit(solution)/shard_map/ppermute | solution.py:407
  34.1 14.0 %collective-permute-start.5 = (bf16[256,512]{1,0:T(8,128)(2,1)S(1)}, bf16[256,512]{1,0:T(8,128)(2,1)S(1)}, u32[]{:S(2)}, u32[]{:S(2)}) collective-permute-start(bf16[256,512]{1,0:T(8,128)(2,1)S(1)} %get-tuple-element.39), channel_id=1, source_target_pairs={{0,511},{1,510},{2,4},{3,5},{4,2},{5,3},{6,8},{7,9},{8,6},{9,7},{1... | collective-permute-start | bytes 786440 | tf_op jit(solution)/shard_map/ppermute | solution.py:413
  48.1 1.0 %copy-start = (bf16[2048,128]{1,0:T(8,128)(2,1)S(1)}, bf16[2048,128]{1,0:T(8,128)(2,1)}, u32[]{:S(2)}) copy-start(bf16[2048,128]{1,0:T(8,128)(2,1)} %finish.1._) | copy-start | bytes 1572868

commit v7 on v6

--- a/solution.py
+++ b/solution.py
@@ -240,7 +240,7 @@
     )(*args)
 
 
-def own_low_kernel(code_ref, rows_ref, kv_ref, _, dq_ref, g_ref):
+def own_low_kernel(code_ref, rows_ref, kv_ref, _, __, dq_ref, g_ref):
     depth = kv_ref.shape[1]
     tokens = kv_ref.shape[0] // 2
     span, half = tokens // 2, rows_ref.shape[0] // 6
@@ -285,7 +285,7 @@
     g_ref[:, lanes] += g_low_ref[...]
 
 
-def own(kernel, codes, q_rows, kv, extra, dq, keys, name):
+def own(kernel, codes, q_rows, kv, extra, dq, keys, name, weight):
     rows, depth = dq.shape
     args = [codes, q_rows, kv] + extra + [dq]
     return pl.pallas_call(
@@ -299,7 +299,7 @@
         input_output_aliases={len(args) - 1: 0},
         compiler_params=pltpu.CompilerParams(vmem_limit_bytes=24 * 2**20),
         cost_estimate=pl.CostEstimate(
-            flops=rows * keys * depth // 10, bytes_accessed=2**16, transcendentals=rows * keys // 100
+            flops=weight * rows * keys * depth // 10, bytes_accessed=2**16, transcendentals=rows * keys // 100
         ),
         name=name,
     )(*args)
@@ -348,11 +348,11 @@
             jax.ShapeDtypeStruct((rows, tokens // 2), F32),
             jax.ShapeDtypeStruct((rows, tokens // 2), BF16),
         ],
-        in_specs=[VMEM] * 4 + [pl.BlockSpec(memory_space=pl.ANY)],
+        in_specs=[VMEM] * 4 + [pl.BlockSpec(memory_space=pltpu.HBM)],
         out_specs=[VMEM, VMEM],
         compiler_params=pltpu.CompilerParams(vmem_limit_bytes=8 * 2**20),
         name="merge",
-    )(g, a, b, c, after)
+    )(g, a, b, c, pltpu.with_memory_space_constraint(after, pltpu.HBM))
 
 
 def last_kernel(keep_ref, got_ref, dk_ref, dv_ref):
@@ -412,8 +412,8 @@
     )
     got_b = lax.ppermute(g_b, both, over_one)
     got_dq = lax.ppermute(dq_low, "ctx", mates)
-    dq, g_low = own(own_low_kernel, codes, q_rows, kv, [], dq, tokens // 2, "own_low")
-    dq, g_own = own(own_high_kernel, codes, q_rows, kv, [g_low], dq, tokens, "own_high")
+    dq, g_low = own(own_low_kernel, codes, q_rows, kv, [got_a], dq, tokens // 2, "own_low", 10000)
+    dq, g_own = own(own_high_kernel, codes, q_rows, kv, [g_low], dq, tokens, "own_high", 1)
     grad_q = finish(dq, got_dq)
     keep, send = merge(g_own, got_a, got_b, g_mate, grad_q)
     got = lax.all_gather(send, "head")

time: 60.6 us -> 59.9 us (0.988)
  the two profiles are of different devices: /device:TPU:0 before, /device:TPU:1 now
where the time goes in v7:
time: 59.9 us; the launch traced here: 59.6 us
  starting transfers between devices  33.6 us (56%)
  Pallas kernels  14.7 us (25%)
  blocking collectives  10.5 us (18%)
  between operations  0.82 us (1%)
    ppermute x1, starting transfers between devices, local(): kv_a = lax.ppermute(kv, both, over_two)  16.6 us
    all_gather x1, blocking collectives, local(): got = lax.all_gather(send, 'head')  10.5 us
    ppermute x1, starting transfers between devices, local(): got_dq = lax.ppermute(dq_low, 'ctx', mates)  7.55 us
    pallas_call x4, Pallas kernels, far(): pl.pallas_call(functools.partial(far_kernel, row, dq is not None, g is no...  7.28 us
    ppermute x1, starting transfers between devices, local(): mate_rows = lax.ppermute(q_rows, 'ctx', mates)  2.84 us
    ppermute x1, starting transfers between devices, local(): got_a = lax.ppermute(g_a, both, back_two)  2.71 us
    pallas_call x2, Pallas kernels, own(): pl.pallas_call(kernel, out_shape=[jax.ShapeDtypeStruct((rows, depth), F32...  2.58 us
    ppermute x1, starting transfers between devices, local(): got_b = lax.ppermute(g_b, both, over_one)  1.95 us
  transfers between devices with their start and end apart: 6, of which 0 were waited for; matrix products, arithmetic and copies ran while one was open for 0% of the time, Pallas kernels for 21%

profile of v7, /device:TPU:1, one launch (start us, length us, event | category | flops | bytes accessed | tf_op | source)
XLA Modules:
  0.0 59.6 jit_solution(3064353809075374723)
XLA Ops:
  0.6 0.0 copy-start.1
  0.6 0.0 copy-start
  0.7 1.5 %load.1 = (bf16[1024,128]{1,0:T(8,128)(2,1)S(1)}, bf16[6144,128]{1,0:T(8,128)(2,1)S(1)}, bf16[2048,128]{1,0:T(8,128)(2,1)S(1)}) custom-call(bf16[512,128]{1,0:T(8,128)(2,1)} %k_ref.1, bf16[512,128]{1,0:T(8,128)(2,1)} %v_ref.1, bf16[2048,128]{1,0:T(8,128)(2,1)} %bitcast.7, bf16[2048,128]{1,0:T(8,128)(2,1)} %bitcast.8, bf16[2048,128]{1,0:T(8,128)(2,1)} %bitcast.9), custom_call_target="tpu_custom_call" | custom-call | tf_op jit(solution)/shard_map/load/pallas_call | solution.py:52
  2.2 16.6 %collective-permute-start = (bf16[1024,128]{1,0:T(8,128)(2,1)S(1)}, bf16[1024,128]{1,0:T(8,128)(2,1)S(1)}, u32[]{:S(2)}, u32[]{:S(2)}) collective-permute-start(bf16[1024,128]{1,0:T(8,128)(2,1)S(1)} %get-tuple-element.28.kv_ref), channel_id=1, source_target_pairs={{0,4},{1,5},{2,511},{3,510},{4,8},{5,9},{6,2},{7,3},{8,12},{9,13},... | collective-permute-start | bytes 786440 | tf_op jit(solution)/shard_map/ppermute | solution.py:401
  18.8 1.9 %collective-permute-start.2 = (bf16[1024,128]{1,0:T(8,128)(2,1)S(1)}, bf16[1024,128]{1,0:T(8,128)(2,1)S(1)}, u32[]{:S(2)}, u32[]{:S(2)}) collective-permute-start(bf16[1024,128]{1,0:T(8,128)(2,1)S(1)} %get-tuple-element.28.kv_ref), channel_id=1, source_target_pairs={{0,511},{1,510},{2,4},{3,5},{4,2},{5,3},{6,8},{7,9},{8,6},{9,7},{1... | collective-permute-start | bytes 786440 | tf_op jit(solution)/shard_map/ppermute | solution.py:402
  20.7 0.0 copy-done.1
  20.8 0.0 copy-done
  20.8 1.5 %prep.1 = (bf16[6144,128]{1,0:T(8,128)(2,1)S(1)}, f32[8,128]{1,0:T(8,128)S(1)}) custom-call(s32[512]{0:T(512)S(1)} %copy-done.1, bf16[6144,128]{1,0:T(8,128)(2,1)S(1)} %get-tuple-element.24.rows_in_ref, bf16[2048,128]{1,0:T(8,128)(2,1)S(1)} %get-tuple-element.25.out_ref, f32[4,512]{1,0:T(4,128)S(1)} %copy-done), custom_call_target="tpu_custom_call", output_to_operand_aliasing={{0}: (1, {})} | custom-call | flops 2097152 | bytes 1572864 | tf_op jit(solution)/shard_map/prep/pallas_call | solution.py:112
  22.2 2.8 %collective-permute-start.3 = (bf16[6144,128]{1,0:T(8,128)(2,1)S(1)}, bf16[6144,128]{1,0:T(8,128)(2,1)S(1)}, u32[]{:S(2)}, u32[]{:S(2)}) collective-permute-start(bf16[6144,128]{1,0:T(8,128)(2,1)S(1)} %get-tuple-element.27.rows_ref), channel_id=1, source_target_pairs={{0,2},{2,0},{4,6},{6,4},{8,10},{10,8},{12,14},{14,12},{16,18},{18,... | collective-permute-start | bytes 4718600 | tf_op jit(solution)/shard_map/ppermute | solution.py:404
  25.1 0.0 collective-permute-done.kv_ref
  25.1 1.8 %far_a.1 = (f32[2048,128]{1,0:T(8,128)S(1)}, bf16[256,512]{1,0:T(8,128)(2,1)S(1)}) custom-call(f32[8,128]{1,0:T(8,128)S(1)} %get-tuple-element.26.code_ref, bf16[6144,128]{1,0:T(8,128)(2,1)S(1)} %get-tuple-element.27.rows_ref, bf16[1024,128]{1,0:T(8,128)(2,1)S(1)} %collective-permute-done.kv_ref), custom_call_target="tpu_custom_call" | custom-call | flops 1342177280 | bytes 65536 | tf_op jit(solution)/shard_map/far_a/pallas_call | solution.py:226
  26.9 2.7 %collective-permute-start.1 = (bf16[256,512]{1,0:T(8,128)(2,1)S(1)}, bf16[256,512]{1,0:T(8,128)(2,1)S(1)}, u32[]{:S(2)}, u32[]{:S(2)}) collective-permute-start(bf16[256,512]{1,0:T(8,128)(2,1)S(1)} %get-tuple-element.29), channel_id=1, source_target_pairs={{4,0},{5,1},{511,2},{510,3},{8,4},{9,5},{2,6},{3,7},{12,8},{13,9},... | collective-permute-start | bytes 786440 | tf_op jit(solution)/shard_map/ppermute | solution.py:407
  29.6 0.0 collective-permute-done.2.kv_ref
  29.6 2.6 %far_b.1 = (f32[2048,128]{1,0:T(8,128)S(1)}, f32[256,512]{1,0:T(8,128)S(1)}) custom-call(f32[8,128]{1,0:T(8,128)S(1)} %get-tuple-element.26.code_ref, bf16[6144,128]{1,0:T(8,128)(2,1)S(1)} %get-tuple-element.27.rows_ref, bf16[1024,128]{1,0:T(8,128)(2,1)S(1)} %collective-permute-done.2.kv_ref, ...), custom_call_target="tpu_custom_call", output_to_operand_aliasing={{0}: (3, {})} | custom-call | flops 134217728000 | bytes 65536 | tf_op jit(solution)/shard_map/far_b/pallas_call | solution.py:226
  32.3 0.0 collective-permute-done.3.rows_ref
  32.3 0.5 own_mate.1
  32.8 2.4 %far_b_mate.1 = (f32[2048,128]{1,0:T(8,128)S(1)}, bf16[256,512]{1,0:T(8,128)(2,1)S(1)}, bf16[2048,128]{1,0:T(8,128)(2,1)S(1)}) custom-call(f32[8,128]{1,0:T(8,128)S(1)} %get-tuple-element.26.code_ref, bf16[6144,128]{1,0:T(8,128)(2,1)S(1)} %collective-permute-done.3.rows_ref, ...), custom_call_target="tpu_custom_call", output_to_operand_aliasing={{0}: (3, {})} | custom-call | flops 1342177280 | bytes 65536 | tf_op jit(solution)/shard_map/far_b_mate/pallas_call | solution.py:226
  35.2 1.9 %collective-permute-start.5 = (bf16[256,512]{1,0:T(8,128)(2,1)S(1)}, bf16[256,512]{1,0:T(8,128)(2,1)S(1)}, u32[]{:S(2)}, u32[]{:S(2)}) collective-permute-start(bf16[256,512]{1,0:T(8,128)(2,1)S(1)} %get-tuple-element.39), channel_id=1, source_target_pairs={{0,511},{1,510},{2,4},{3,5},{4,2},{5,3},{6,8},{7,9},{8,6},{9,7},{1... | collective-permute-start | bytes 786440 | tf_op jit(solution)/shard_map/ppermute | solution.py:413
  37.1 7.6 %collective-permute-start.4 = (bf16[2048,128]{1,0:T(8,128)(2,1)S(1)}, bf16[2048,128]{1,0:T(8,128)(2,1)S(1)}, u32[]{:S(2)}, u32[]{:S(2)}) collective-permute-start(bf16[2048,128]{1,0:T(8,128)(2,1)S(1)} %get-tuple-element.37), channel_id=1, source_target_pairs={{0,2},{2,0},{4,6},{6,4},{8,10},{10,8},{12,14},{14,12},{16,18},{18,... | collective-permute-start | bytes 1572872 | tf_op jit(solution)/shard_map/ppermute | solution.py:414
  44.7 0.0 collective-permute-done.1._.a_ref
  44.7 0.9 %own_low.1 = (f32[2048,128]{1,0:T(8,128)S(1)}, f32[256,256]{1,0:T(8,128)S(1)}) custom-call(f32[8,128]{1,0:T(8,128)S(1)} %get-tuple-element.26.code_ref, bf16[6144,128]{1,0:T(8,128)(2,1)S(1)} %get-tuple-element.27.rows_ref, bf16[1024,128]{1,0:T(8,128)(2,1)S(1)} %get-tuple-element.28.kv_ref, ...), custom_call_target="tpu_custom_call", output_to_operand_aliasing={{0}: (4, {})} | custom-call | flops 67108864000 | bytes 65536 | tf_op jit(solution)/shard_map/own_low/pallas_call | solution.py:291
  45.6 1.7 %own_high.1 = (f32[2048,128]{1,0:T(8,128)S(1)}, f32[256,512]{1,0:T(8,128)S(1)}) custom-call(f32[8,128]{1,0:T(8,128)S(1)} %get-tuple-element.26.code_ref, bf16[6144,128]{1,0:T(8,128)(2,1)S(1)} %get-tuple-element.27.rows_ref, bf16[1024,128]{1,0:T(8,128)(2,1)S(1)} %get-tuple-element.28.kv_ref, ...), custom_call_target="tpu_custom_call", output_to_operand_aliasing={{0}: (4, {})} | custom-call | flops 13421772 | bytes 65536 | tf_op jit(solution)/shard_map/own_high/pallas_call | solution.py:291
  47.3 0.0 collective-permute-done.4.mate_ref
  47.3 0.9 %finish.1._ = bf16[2048,128]{1,0:T(8,128)(2,1)} custom-call(f32[2048,128]{1,0:T(8,128)S(1)} %get-tuple-element.34.dq_ref, bf16[2048,128]{1,0:T(8,128)(2,1)S(1)} %collective-permute-done.4.mate_ref), custom_call_target="tpu_custom_call" | custom-call | flops 262144 | bytes 1572864 | tf_op jit(solution)/shard_map/finish/pallas_call | solution.py:314
  48.2 0.0 collective-permute-done.5.b_ref
  48.2 0.1 merge.1
  48.3 10.5 %all-gather = bf16[512,256]{1,0:T(8,128)(2,1)S(1)} all-gather(bf16[256,256]{1,0:T(8,128)(2,1)S(1)} %get-tuple-element.42), channel_id=2, replica_groups=mesh['ctx'=256,'head'=2] {'head'}, dimensions={0}, use_global_device_ids=true | all-gather | bytes 393216 | tf_op jit(solution)/shard_map/all_gather | solution.py:419
  58.9 0.8 %last.1 = (bf16[256,128]{1,0:T(8,128)(2,1)}, bf16[256,128]{1,0:T(8,128)(2,1)}) custom-call(f32[256,256]{1,0:T(8,128)S(1)} %get-tuple-element.41.keep_ref, bf16[2,256,256]{2,1,0:T(8,128)(2,1)S(1)} %bitcast.5), custom_call_target="tpu_custom_call" | custom-call | tf_op jit(solution)/shard_map/last/pallas_call | solution.py:368
Async XLA Ops:
  0.6 20.1 %copy-start.1 = (s32[512]{0:T(512)S(1)}, s32[512]{0:T(512)}, u32[]{:S(2)}) copy-start(s32[512]{0:T(512)} %span_ref.1) | copy-start | bytes 6148
  0.6 20.1 %copy-start = (f32[4,512]{1,0:T(4,128)S(1)}, f32[4,512]{1,0:T(4,128)}, u32[]{:S(2)}) copy-start(f32[4,512]{1,0:T(4,128)} %lse_ref.1) | copy-start | bytes 24580
  2.2 22.9 %collective-permute-start = (bf16[1024,128]{1,0:T(8,128)(2,1)S(1)}, bf16[1024,128]{1,0:T(8,128)(2,1)S(1)}, u32[]{:S(2)}, u32[]{:S(2)}) collective-permute-start(bf16[1024,128]{1,0:T(8,128)(2,1)S(1)} %get-tuple-element.28.kv_ref), channel_id=1, source_target_pairs={{0,4},{1,5},{2,511},{3,510},{4,8},{5,9},{6,2},{7,3},{8,12},{9,13},... | collective-permute-start | bytes 786440 | tf_op jit(solution)/shard_map/ppermute | solution.py:401
  18.8 10.8 %collective-permute-start.2 = (bf16[1024,128]{1,0:T(8,128)(2,1)S(1)}, bf16[1024,128]{1,0:T(8,128)(2,1)S(1)}, u32[]{:S(2)}, u32[]{:S(2)}) collective-permute-start(bf16[1024,128]{1,0:T(8,128)(2,1)S(1)} %get-tuple-element.28.kv_ref), channel_id=1, source_target_pairs={{0,511},{1,510},{2,4},{3,5},{4,2},{5,3},{6,8},{7,9},{8,6},{9,7},{1... | collective-permute-start | bytes 786440 | tf_op jit(solution)/shard_map/ppermute | solution.py:402
  22.2 10.0 %collective-permute-start.3 = (bf16[6144,128]{1,0:T(8,128)(2,1)S(1)}, bf16[6144,128]{1,0:T(8,128)(2,1)S(1)}, u32[]{:S(2)}, u32[]{:S(2)}) collective-permute-start(bf16[6144,128]{1,0:T(8,128)(2,1)S(1)} %get-tuple-element.27.rows_ref), channel_id=1, source_target_pairs={{0,2},{2,0},{4,6},{6,4},{8,10},{10,8},{12,14},{14,12},{16,18},{18,... | collective-permute-start | bytes 4718600 | tf_op jit(solution)/shard_map/ppermute | solution.py:404
  26.9 17.8 %collective-permute-start.1 = (bf16[256,512]{1,0:T(8,128)(2,1)S(1)}, bf16[256,512]{1,0:T(8,128)(2,1)S(1)}, u32[]{:S(2)}, u32[]{:S(2)}) collective-permute-start(bf16[256,512]{1,0:T(8,128)(2,1)S(1)} %get-tuple-element.29), channel_id=1, source_target_pairs={{4,0},{5,1},{511,2},{510,3},{8,4},{9,5},{2,6},{3,7},{12,8},{13,9},... | collective-permute-start | bytes 786440 | tf_op jit(solution)/shard_map/ppermute | solution.py:407
  35.2 13.1 %collective-permute-start.5 = (bf16[256,512]{1,0:T(8,128)(2,1)S(1)}, bf16[256,512]{1,0:T(8,128)(2,1)S(1)}, u32[]{:S(2)}, u32[]{:S(2)}) collective-permute-start(bf16[256,512]{1,0:T(8,128)(2,1)S(1)} %get-tuple-element.39), channel_id=1, source_target_pairs={{0,511},{1,510},{2,4},{3,5},{4,2},{5,3},{6,8},{7,9},{8,6},{9,7},{1... | collective-permute-start | bytes 786440 | tf_op jit(solution)/shard_map/ppermute | solution.py:413
  37.1 10.2 %collective-permute-start.4 = (bf16[2048,128]{1,0:T(8,128)(2,1)S(1)}, bf16[2048,128]{1,0:T(8,128)(2,1)S(1)}, u32[]{:S(2)}, u32[]{:S(2)}) collective-permute-start(bf16[2048,128]{1,0:T(8,128)(2,1)S(1)} %get-tuple-element.37), channel_id=1, source_target_pairs={{0,2},{2,0},{4,6},{6,4},{8,10},{10,8},{12,14},{14,12},{16,18},{18,... | collective-permute-start | bytes 1572872 | tf_op jit(solution)/shard_map/ppermute | solution.py:414

commit v8 on v7

--- a/solution.py
+++ b/solution.py
@@ -25,12 +25,15 @@
     return jnp.where((lane >= low) & (lane < high), 1.0, 0.0).astype(BF16)
 
 
-def load_kernel(k_ref, v_ref, q_ref, do_ref, out_ref, kv_to, rows_to, out_to, sems):
+def load_kernel(
+    span_from, k_ref, v_ref, q_ref, do_ref, out_ref, kv_to, rows_to, out_to, code_ref, span_ref, sems
+):
     tokens, rows = k_ref.shape[0], q_ref.shape[0]
     copies = [
         pltpu.make_async_copy(source, target, sems.at[i])
         for i, (source, target) in enumerate(
             [
+                (span_from, span_ref),
                 (k_ref, kv_to.at[pl.ds(0, tokens)]),
                 (v_ref, kv_to.at[pl.ds(tokens, tokens)]),
                 (do_ref, rows_to.at[pl.ds(rows, rows)]),
@@ -41,30 +44,7 @@
     ]
     for copy in copies:
         copy.start()
-    for copy in copies:
-        copy.wait()
-
-
-def load(keys, values, q, do, out):
-    tokens, depth = keys.shape
-    rows = q.shape[0]
-    args = [pltpu.with_memory_space_constraint(a, pltpu.HBM) for a in (keys, values, q, do, out)]
-    return pl.pallas_call(
-        load_kernel,
-        out_shape=[
-            jax.ShapeDtypeStruct((2 * tokens, depth), BF16),
-            jax.ShapeDtypeStruct((3 * rows, depth), BF16),
-            jax.ShapeDtypeStruct((rows, depth), BF16),
-        ],
-        in_specs=[pl.BlockSpec(memory_space=pltpu.HBM)] * 5,
-        out_specs=[VMEM] * 3,
-        scratch_shapes=[pltpu.SemaphoreType.DMA((5,))],
-        compiler_params=pltpu.CompilerParams(vmem_limit_bytes=8 * 2**20),
-        name="load",
-    )(*args)
-
-
-def prep_kernel(span_ref, rows_in_ref, out_ref, lse_ref, rows_ref, code_ref, wide):
+    copies[0].wait()
     count = lax.axis_size("ctx")
     me = lax.axis_index("ctx")
     sign = 1 - 2 * (me % 2)
@@ -80,6 +60,31 @@
             code = code + jnp.where(allowed, float(2**bit), 0.0)
         codes = jnp.where(row == r, code, codes)
     code_ref[...] = codes
+    for copy in copies[1:]:
+        copy.wait()
+
+
+def load(spans, keys, values, q, do, out):
+    tokens, depth = keys.shape
+    rows = q.shape[0]
+    args = [pltpu.with_memory_space_constraint(a, pltpu.HBM) for a in (spans, keys, values, q, do, out)]
+    return pl.pallas_call(
+        load_kernel,
+        out_shape=[
+            jax.ShapeDtypeStruct((2 * tokens, depth), BF16),
+            jax.ShapeDtypeStruct((3 * rows, depth), BF16),
+            jax.ShapeDtypeStruct((rows, depth), BF16),
+            jax.ShapeDtypeStruct((8, 128), F32),
+        ],
+        in_specs=[pl.BlockSpec(memory_space=pltpu.HBM)] * 6,
+        out_specs=[VMEM] * 4,
+        scratch_shapes=[pltpu.SMEM(spans.shape, jnp.int32), pltpu.SemaphoreType.DMA((6,))],
+        compiler_params=pltpu.CompilerParams(vmem_limit_bytes=8 * 2**20),
+        name="load",
+    )(*args)
+
+
+def prep_kernel(rows_in_ref, out_ref, lse_ref, rows_ref, wide):
     rows = out_ref.shape[0]
     heads, tokens = lse_ref.shape
     depth = out_ref.shape[1]
@@ -107,22 +112,19 @@
     return jnp.max(code_ref[pl.ds(row, 1), :]).astype(jnp.int32)
 
 
-def prep(spans, q_rows, out_rows, lse):
+def prep(q_rows, out_rows, lse):
     rows = out_rows.shape[0]
     return pl.pallas_call(
         prep_kernel,
-        out_shape=[
-            jax.ShapeDtypeStruct(q_rows.shape, BF16),
-            jax.ShapeDtypeStruct((8, 128), F32),
-        ],
-        in_specs=[SMEM] + [VMEM] * 3,
-        out_specs=[VMEM] * 2,
-        input_output_aliases={1: 0},
+        out_shape=jax.ShapeDtypeStruct(q_rows.shape, BF16),
+        in_specs=[VMEM] * 3,
+        out_specs=VMEM,
+        input_output_aliases={0: 0},
         scratch_shapes=[pltpu.VMEM((rows, 128), F32)],
         compiler_params=pltpu.CompilerParams(vmem_limit_bytes=16 * 2**20),
         cost_estimate=pl.CostEstimate(flops=rows * 1024, bytes_accessed=rows * 768, transcendentals=0),
         name="prep",
-    )(spans, q_rows, out_rows, lse)
+    )(q_rows, out_rows, lse)
 
 
 def tile(rows_ref, key, value, q_base, rows, mask=None):
@@ -397,10 +399,10 @@
     over_one = ring(count, lambda d: d + 1 if d % 2 else d - 1)
     mates = [(d, d ^ 1) for d in range(count)]
 
-    kv, q_rows, out = load(keys, values, q, do, out)
+    kv, q_rows, out, codes = load(span_order, keys, values, q, do, out)
     kv_a = lax.ppermute(kv, both, over_two)
     kv_b = lax.ppermute(kv, both, over_one)
-    q_rows, codes = prep(span_order, q_rows, out, lse)
+    q_rows = prep(q_rows, out, lse)
     mate_rows = lax.ppermute(q_rows, "ctx", mates)
 
     dq, g_a = far(0, codes, q_rows, kv_a, "far_a", dtype=BF16)
@@ -412,7 +414,7 @@
     )
     got_b = lax.ppermute(g_b, both, over_one)
     got_dq = lax.ppermute(dq_low, "ctx", mates)
-    dq, g_low = own(own_low_kernel, codes, q_rows, kv, [got_a], dq, tokens // 2, "own_low", 10000)
+    dq, g_low = own(own_low_kernel, codes, q_rows, kv, [got_a], dq, tokens // 2, "own_low", 600)
     dq, g_own = own(own_high_kernel, codes, q_rows, kv, [g_low], dq, tokens, "own_high", 1)
     grad_q = finish(dq, got_dq)
     keep, send = merge(g_own, got_a, got_b, g_mate, grad_q)

time: 59.9 us -> 59.8 us (level)
  the two profiles are of different devices: /device:TPU:1 before, /device:TPU:0 now
where the time goes in v8:
time: 59.8 us; the launch traced here: 59.6 us
  starting transfers between devices  23.4 us (39%)
  Pallas kernels  15.8 us (26%)
  waiting for transfers between devices  10.1 us (17%)
  blocking collectives  9.55 us (16%)
  between operations  0.79 us (1%)
    ppermute x1, starting transfers between devices, local(): kv_b = lax.ppermute(kv, both, over_one)  10.7 us
    all_gather x1, blocking collectives, local(): got = lax.all_gather(send, 'head')  9.55 us
    ppermute x1, waiting for transfers between devices, local(): got_b = lax.ppermute(g_b, both, over_one)  9.37 us
    pallas_call x4, Pallas kernels, far(): pl.pallas_call(functools.partial(far_kernel, row, dq is not None, g is no...  8.96 us
    ppermute x1, starting transfers between devices, local(): got_a = lax.ppermute(g_a, both, back_two)  4.2 us
    ppermute x1, starting transfers between devices, local(): got_b = lax.ppermute(g_b, both, over_one)  2.76 us
    pallas_call x2, Pallas kernels, own(): pl.pallas_call(kernel, out_shape=[jax.ShapeDtypeStruct((rows, depth), F32...  2.58 us
    ppermute x1, starting transfers between devices, local(): kv_a = lax.ppermute(kv, both, over_two)  1.92 us
  transfers between devices with their start and end apart: 6, of which 2 were waited for; matrix products, arithmetic and copies ran while one was open for 0% of the time, Pallas kernels for 22%

profile of v8, /device:TPU:0, one launch (start us, length us, event | category | flops | bytes accessed | tf_op | source)
XLA Modules:
  0.0 59.6 jit_solution(13852532933201964846)
XLA Ops:
  0.6 0.0 copy-start
  0.6 1.6 %load.1 = (bf16[1024,128]{1,0:T(8,128)(2,1)S(1)}, bf16[6144,128]{1,0:T(8,128)(2,1)S(1)}, bf16[2048,128]{1,0:T(8,128)(2,1)S(1)}, f32[8,128]{1,0:T(8,128)S(1)}) custom-call(s32[512]{0:T(512)} %span_from.1, bf16[512,128]{1,0:T(8,128)(2,1)} %k_ref.1, bf16[512,128]{1,0:T(8,128)(2,1)} %v_ref.1, bf16[2048,128]{1,0:T(8,128)(2,1)} %bitcast.7, ...), custom_call_target="tpu_custom_call" | custom-call | tf_op jit(solution)/shard_map/load/pallas_call | solution.py:71
  2.2 1.9 %collective-permute-start = (bf16[1024,128]{1,0:T(8,128)(2,1)S(1)}, bf16[1024,128]{1,0:T(8,128)(2,1)S(1)}, u32[]{:S(2)}, u32[]{:S(2)}) collective-permute-start(bf16[1024,128]{1,0:T(8,128)(2,1)S(1)} %get-tuple-element.26.kv_ref), channel_id=1, source_target_pairs={{0,4},{1,5},{2,511},{3,510},{4,8},{5,9},{6,2},{7,3},{8,12},{9,13},... | collective-permute-start | bytes 786440 | tf_op jit(solution)/shard_map/ppermute | solution.py:403
  4.1 10.7 %collective-permute-start.2 = (bf16[1024,128]{1,0:T(8,128)(2,1)S(1)}, bf16[1024,128]{1,0:T(8,128)(2,1)S(1)}, u32[]{:S(2)}, u32[]{:S(2)}) collective-permute-start(bf16[1024,128]{1,0:T(8,128)(2,1)S(1)} %get-tuple-element.26.kv_ref), channel_id=1, source_target_pairs={{0,511},{1,510},{2,4},{3,5},{4,2},{5,3},{6,8},{7,9},{8,6},{9,7},{1... | collective-permute-start | bytes 786440 | tf_op jit(solution)/shard_map/ppermute | solution.py:404
  14.8 0.0 copy-done
  14.8 0.9 %prep.1.rows_ref = bf16[6144,128]{1,0:T(8,128)(2,1)S(1)} custom-call(bf16[6144,128]{1,0:T(8,128)(2,1)S(1)} %get-tuple-element.24.rows_in_ref, bf16[2048,128]{1,0:T(8,128)(2,1)S(1)} %get-tuple-element.25.out_ref, f32[4,512]{1,0:T(4,128)S(1)} %copy-done), custom_call_target="tpu_custom_call", output_to_operand_aliasing={{}: (0, {})} | custom-call | flops 2097152 | bytes 1572864 | tf_op jit(solution)/shard_map/prep/pallas_call | solution.py:117
  15.7 1.9 %collective-permute-start.3 = (bf16[6144,128]{1,0:T(8,128)(2,1)S(1)}, bf16[6144,128]{1,0:T(8,128)(2,1)S(1)}, u32[]{:S(2)}, u32[]{:S(2)}) collective-permute-start(bf16[6144,128]{1,0:T(8,128)(2,1)S(1)} %prep.1.rows_ref), channel_id=1, source_target_pairs={{0,2},{2,0},{4,6},{6,4},{8,10},{10,8},{12,14},{14,12},{16,18},{18,... | collective-permute-start | bytes 4718600 | tf_op jit(solution)/shard_map/ppermute | solution.py:406
  17.6 0.7 %collective-permute-done.kv_ref = bf16[1024,128]{1,0:T(8,128)(2,1)S(1)} collective-permute-done((bf16[1024,128]{1,0:T(8,128)(2,1)S(1)}, bf16[1024,128]{1,0:T(8,128)(2,1)S(1)}, u32[]{:S(2)}, u32[]{:S(2)}) %collective-permute-start) | collective-permute-done | bytes 262176 | tf_op jit(solution)/shard_map/ppermute | solution.py:403
  18.4 2.4 %far_a.1 = (f32[2048,128]{1,0:T(8,128)S(1)}, bf16[256,512]{1,0:T(8,128)(2,1)S(1)}) custom-call(f32[8,128]{1,0:T(8,128)S(1)} %get-tuple-element.23.code_ref, bf16[6144,128]{1,0:T(8,128)(2,1)S(1)} %prep.1.rows_ref, bf16[1024,128]{1,0:T(8,128)(2,1)S(1)} %collective-permute-done.kv_ref), custom_call_target="tpu_custom_call" | custom-call | flops 1342177280 | bytes 65536 | tf_op jit(solution)/shard_map/far_a/pallas_call | solution.py:228
  20.8 4.2 %collective-permute-start.1 = (bf16[256,512]{1,0:T(8,128)(2,1)S(1)}, bf16[256,512]{1,0:T(8,128)(2,1)S(1)}, u32[]{:S(2)}, u32[]{:S(2)}) collective-permute-start(bf16[256,512]{1,0:T(8,128)(2,1)S(1)} %get-tuple-element.27), channel_id=1, source_target_pairs={{4,0},{5,1},{511,2},{510,3},{8,4},{9,5},{2,6},{3,7},{12,8},{13,9},... | collective-permute-start | bytes 786440 | tf_op jit(solution)/shard_map/ppermute | solution.py:409
  25.0 0.0 collective-permute-done.2.kv_ref
  25.0 2.6 %far_b.1 = (f32[2048,128]{1,0:T(8,128)S(1)}, f32[256,512]{1,0:T(8,128)S(1)}) custom-call(f32[8,128]{1,0:T(8,128)S(1)} %get-tuple-element.23.code_ref, bf16[6144,128]{1,0:T(8,128)(2,1)S(1)} %prep.1.rows_ref, bf16[1024,128]{1,0:T(8,128)(2,1)S(1)} %collective-permute-done.2.kv_ref, ...), custom_call_target="tpu_custom_call", output_to_operand_aliasing={{0}: (3, {})} | custom-call | flops 134217728000 | bytes 65536 | tf_op jit(solution)/shard_map/far_b/pallas_call | solution.py:228
  27.6 0.0 collective-permute-done.3.rows_ref
  27.6 1.2 %own_mate.1 = (f32[2048,128]{1,0:T(8,128)S(1)}, f32[256,512]{1,0:T(8,128)S(1)}) custom-call(f32[8,128]{1,0:T(8,128)S(1)} %get-tuple-element.23.code_ref, bf16[6144,128]{1,0:T(8,128)(2,1)S(1)} %collective-permute-done.3.rows_ref, bf16[1024,128]{1,0:T(8,128)(2,1)S(1)} %get-tuple-element.26.kv_ref), custom_call_target="tpu_custom_call" | custom-call | flops 1342177280 | bytes 65536 | tf_op jit(solution)/shard_map/own_mate/pallas_call | solution.py:228
  28.9 2.7 %far_b_mate.1 = (f32[2048,128]{1,0:T(8,128)S(1)}, bf16[256,512]{1,0:T(8,128)(2,1)S(1)}, bf16[2048,128]{1,0:T(8,128)(2,1)S(1)}) custom-call(f32[8,128]{1,0:T(8,128)S(1)} %get-tuple-element.23.code_ref, bf16[6144,128]{1,0:T(8,128)(2,1)S(1)} %collective-permute-done.3.rows_ref, ...), custom_call_target="tpu_custom_call", output_to_operand_aliasing={{0}: (3, {})} | custom-call | flops 1342177280 | bytes 65536 | tf_op jit(solution)/shard_map/far_b_mate/pallas_call | solution.py:228
  31.6 1.9 %collective-permute-start.4 = (bf16[2048,128]{1,0:T(8,128)(2,1)S(1)}, bf16[2048,128]{1,0:T(8,128)(2,1)S(1)}, u32[]{:S(2)}, u32[]{:S(2)}) collective-permute-start(bf16[2048,128]{1,0:T(8,128)(2,1)S(1)} %get-tuple-element.35), channel_id=1, source_target_pairs={{0,2},{2,0},{4,6},{6,4},{8,10},{10,8},{12,14},{14,12},{16,18},{18,... | collective-permute-start | bytes 1572872 | tf_op jit(solution)/shard_map/ppermute | solution.py:416
  33.5 2.8 %collective-permute-start.5 = (bf16[256,512]{1,0:T(8,128)(2,1)S(1)}, bf16[256,512]{1,0:T(8,128)(2,1)S(1)}, u32[]{:S(2)}, u32[]{:S(2)}) collective-permute-start(bf16[256,512]{1,0:T(8,128)(2,1)S(1)} %get-tuple-element.37), channel_id=1, source_target_pairs={{0,511},{1,510},{2,4},{3,5},{4,2},{5,3},{6,8},{7,9},{8,6},{9,7},{1... | collective-permute-start | bytes 786440 | tf_op jit(solution)/shard_map/ppermute | solution.py:415
  36.3 0.0 collective-permute-done.1._.a_ref
  36.3 0.9 %own_low.1 = (f32[2048,128]{1,0:T(8,128)S(1)}, f32[256,256]{1,0:T(8,128)S(1)}) custom-call(f32[8,128]{1,0:T(8,128)S(1)} %get-tuple-element.23.code_ref, bf16[6144,128]{1,0:T(8,128)(2,1)S(1)} %prep.1.rows_ref, bf16[1024,128]{1,0:T(8,128)(2,1)S(1)} %get-tuple-element.26.kv_ref, ...), custom_call_target="tpu_custom_call", output_to_operand_aliasing={{0}: (4, {})} | custom-call | flops 4026531840 | bytes 65536 | tf_op jit(solution)/shard_map/own_low/pallas_call | solution.py:293
  37.2 1.7 %own_high.1 = (f32[2048,128]{1,0:T(8,128)S(1)}, f32[256,512]{1,0:T(8,128)S(1)}) custom-call(f32[8,128]{1,0:T(8,128)S(1)} %get-tuple-element.23.code_ref, bf16[6144,128]{1,0:T(8,128)(2,1)S(1)} %prep.1.rows_ref, bf16[1024,128]{1,0:T(8,128)(2,1)S(1)} %get-tuple-element.26.kv_ref, ...), custom_call_target="tpu_custom_call", output_to_operand_aliasing={{0}: (4, {})} | custom-call | flops 13421772 | bytes 65536 | tf_op jit(solution)/shard_map/own_high/pallas_call | solution.py:293
  38.9 0.0 collective-permute-done.4.mate_ref
  38.9 0.9 %finish.1._ = bf16[2048,128]{1,0:T(8,128)(2,1)} custom-call(f32[2048,128]{1,0:T(8,128)S(1)} %get-tuple-element.32.dq_ref, bf16[2048,128]{1,0:T(8,128)(2,1)S(1)} %collective-permute-done.4.mate_ref), custom_call_target="tpu_custom_call" | custom-call | flops 262144 | bytes 1572864 | tf_op jit(solution)/shard_map/finish/pallas_call | solution.py:316
  39.8 9.4 %collective-permute-done.5.b_ref = bf16[256,512]{1,0:T(8,128)(2,1)S(1)} collective-permute-done((bf16[256,512]{1,0:T(8,128)(2,1)S(1)}, bf16[256,512]{1,0:T(8,128)(2,1)S(1)}, u32[]{:S(2)}, u32[]{:S(2)}) %collective-permute-start.5) | collective-permute-done | bytes 262176 | tf_op jit(solution)/shard_map/ppermute | solution.py:415
  49.2 0.1 merge.1
  49.3 9.6 %all-gather = bf16[512,256]{1,0:T(8,128)(2,1)S(1)} all-gather(bf16[256,256]{1,0:T(8,128)(2,1)S(1)} %get-tuple-element.40), channel_id=2, replica_groups=mesh['ctx'=256,'head'=2] {'head'}, dimensions={0}, use_global_device_ids=true | all-gather | bytes 393216 | tf_op jit(solution)/shard_map/all_gather | solution.py:421
  58.8 0.8 %last.1 = (bf16[256,128]{1,0:T(8,128)(2,1)}, bf16[256,128]{1,0:T(8,128)(2,1)}) custom-call(f32[256,256]{1,0:T(8,128)S(1)} %get-tuple-element.39.keep_ref, bf16[2,256,256]{2,1,0:T(8,128)(2,1)S(1)} %bitcast.5), custom_call_target="tpu_custom_call" | custom-call | tf_op jit(solution)/shard_map/last/pallas_call | solution.py:370
Async XLA Ops:
  0.6 14.2 %copy-start = (f32[4,512]{1,0:T(4,128)S(1)}, f32[4,512]{1,0:T(4,128)}, u32[]{:S(2)}) copy-start(f32[4,512]{1,0:T(4,128)} %lse_ref.1) | copy-start | bytes 24580
  2.2 16.1 %collective-permute-start = (bf16[1024,128]{1,0:T(8,128)(2,1)S(1)}, bf16[1024,128]{1,0:T(8,128)(2,1)S(1)}, u32[]{:S(2)}, u32[]{:S(2)}) collective-permute-start(bf16[1024,128]{1,0:T(8,128)(2,1)S(1)} %get-tuple-element.26.kv_ref), channel_id=1, source_target_pairs={{0,4},{1,5},{2,511},{3,510},{4,8},{5,9},{6,2},{7,3},{8,12},{9,13},... | collective-permute-start | bytes 786440 | tf_op jit(solution)/shard_map/ppermute | solution.py:403
  4.1 20.8 %collective-permute-start.2 = (bf16[1024,128]{1,0:T(8,128)(2,1)S(1)}, bf16[1024,128]{1,0:T(8,128)(2,1)S(1)}, u32[]{:S(2)}, u32[]{:S(2)}) collective-permute-start(bf16[1024,128]{1,0:T(8,128)(2,1)S(1)} %get-tuple-element.26.kv_ref), channel_id=1, source_target_pairs={{0,511},{1,510},{2,4},{3,5},{4,2},{5,3},{6,8},{7,9},{8,6},{9,7},{1... | collective-permute-start | bytes 786440 | tf_op jit(solution)/shard_map/ppermute | solution.py:404
  15.7 11.9 %collective-permute-start.3 = (bf16[6144,128]{1,0:T(8,128)(2,1)S(1)}, bf16[6144,128]{1,0:T(8,128)(2,1)S(1)}, u32[]{:S(2)}, u32[]{:S(2)}) collective-permute-start(bf16[6144,128]{1,0:T(8,128)(2,1)S(1)} %prep.1.rows_ref), channel_id=1, source_target_pairs={{0,2},{2,0},{4,6},{6,4},{8,10},{10,8},{12,14},{14,12},{16,18},{18,... | collective-permute-start | bytes 4718600 | tf_op jit(solution)/shard_map/ppermute | solution.py:406
  20.8 15.5 %collective-permute-start.1 = (bf16[256,512]{1,0:T(8,128)(2,1)S(1)}, bf16[256,512]{1,0:T(8,128)(2,1)S(1)}, u32[]{:S(2)}, u32[]{:S(2)}) collective-permute-start(bf16[256,512]{1,0:T(8,128)(2,1)S(1)} %get-tuple-element.27), channel_id=1, source_target_pairs={{4,0},{5,1},{511,2},{510,3},{8,4},{9,5},{2,6},{3,7},{12,8},{13,9},... | collective-permute-start | bytes 786440 | tf_op jit(solution)/shard_map/ppermute | solution.py:409
  31.6 7.3 %collective-permute-start.4 = (bf16[2048,128]{1,0:T(8,128)(2,1)S(1)}, bf16[2048,128]{1,0:T(8,128)(2,1)S(1)}, u32[]{:S(2)}, u32[]{:S(2)}) collective-permute-start(bf16[2048,128]{1,0:T(8,128)(2,1)S(1)} %get-tuple-element.35), channel_id=1, source_target_pairs={{0,2},{2,0},{4,6},{6,4},{8,10},{10,8},{12,14},{14,12},{16,18},{18,... | collective-permute-start | bytes 1572872 | tf_op jit(solution)/shard_map/ppermute | solution.py:416
  33.5 15.7 %collective-permute-start.5 = (bf16[256,512]{1,0:T(8,128)(2,1)S(1)}, bf16[256,512]{1,0:T(8,128)(2,1)S(1)}, u32[]{:S(2)}, u32[]{:S(2)}) collective-permute-start(bf16[256,512]{1,0:T(8,128)(2,1)S(1)} %get-tuple-element.37), channel_id=1, source_target_pairs={{0,511},{1,510},{2,4},{3,5},{4,2},{5,3},{6,8},{7,9},{8,6},{9,7},{1... | collective-permute-start | bytes 786440 | tf_op jit(solution)/shard_map/ppermute | solution.py:415
